TPU v7x, 32 devices: a whole 2x2x4 slice. The times are simulated.
32 devices in a mesh: blk: 8 (over y, x, core), uly: 4 (over z).
Axes of the slice: x: 2, y: 2, z: 4, core: 2. Of those that a mesh axis runs over, the one named last changes fastest.
Arguments:
- hidden_in: bfloat16 [2048, 3072], P(('blk', 'uly')), may hold values from -6 to 6
- cached_out: bfloat16 [2048, 3072], P(('blk', 'uly')), may hold values from -6 to 6
- cache_keys: bfloat16 [2048, 3072], P(('blk', 'uly')), may hold values from -288 to 288
- cache_values: bfloat16 [2048, 3072], P(('blk', 'uly')), may hold values from -36 to 36
- refresh_idx: int32 [512], P(('blk', 'uly')), may hold values from -1 to 63, as said below
- modulation: float32 [6, 3072], replicated, may hold values from -3 to 3
- q_gain: float32 [128], replicated, may hold values from 1.5 to 4
- w_query: bfloat16 [3072, 3072], P(None, 'uly'), may hold values from -0.109375 to 0.109375
- w_out: bfloat16 [3072, 3072], P('uly'), may hold values from -0.109375 to 0.109375
- w_up: bfloat16 [3072, 12288], P(None, 'blk'), may hold values from -0.109375 to 0.109375
- w_down: bfloat16 [12288, 3072], P('blk'), may hold values from -0.0546875 to 0.0546875
Outputs:
- features: bfloat16 [2048, 3072], P(('blk', 'uly'))
Inputs may be any that keep to these rules, and one draw needn't show every extreme that they name: `refresh_idx`: each device's 16 slots name distinct positions among that device's own 64 positions, live slots first and -1 in the rest. Among the devices that share a blk index, one has all 16 slots live and every other at most 8; so such a group has at most 40 live slots, and some group has exactly 40.
All inputs are finite; a program needn't handle non-finite values.
Results may differ from a plain program's by a relative error of at most 0.023.
The roundings to bfloat16 on the way count: a program that leaves them out, or rounds other values in their place, can miss the bound.
Values may be sent and summed in bfloat16 or wider, within the bound.
No kernel may reach another device: no remote copies, remote signals or barrier semaphores. Data moves between devices by JAX's collectives and lax.ppermute only.
A program may use at most 128 MiB of HBM per device.

v0:
```python
import functools
import math

import jax
import jax.numpy as jnp
from jax import lax
from jax.experimental import pallas as pl
from jax.experimental.pallas import tpu as pltpu
from jax.sharding import PartitionSpec as P

DH = 128
OTHER = 8
VMEM_SPEC = pl.BlockSpec(memory_space=pltpu.VMEM)
TOKEN = jax.ShapeDtypeStruct((8, DH), jnp.float32)
ANY_SPEC = pl.BlockSpec(memory_space=pl.ANY)


def double(x, axis, scale, count, on_arrival=()):
    have = {0: x}
    for k in sorted(range(1, count), key=lambda k: (bin(k).count("1"), -k)):
        low = k & -k
        have[k] = trade(have[k ^ low], axis, low * scale)
        if k in on_arrival:
            have[k] = on_arrival[k](have[k])
    return [have[k] for k in range(count)]


def layer_norm(row_block, shift_by, scale_by):
    average = jnp.mean(row_block, axis=-1, keepdims=True)
    centred = row_block - average
    spread = jnp.mean(centred * centred, axis=-1, keepdims=True)
    return centred * lax.rsqrt(spread + 1e-06) * (1.0 + scale_by) + shift_by


def trade(x, axis, flip):
    if flip == 0:
        return x
    return lax.ppermute(x, axis, [(i, i ^ flip) for i in range(lax.axis_size(axis))])


def in_hbm(x):
    return pltpu.with_memory_space_constraint(x, pltpu.HBM)


def hold_kernel(count, *refs):
    source_refs, sems = refs[1 : count + 1], refs[-1]
    *held_refs, token_ref = refs[count + 1 : -1]
    token_ref[...] = jnp.zeros_like(token_ref)
    copies = [
        pltpu.make_async_copy(source_ref, held_ref, sems.at[i])
        for i, (source_ref, held_ref) in enumerate(zip(source_refs, held_refs))
    ]
    for copy in copies:
        copy.start()
    for copy in copies:
        copy.wait()


def hold(after, *weights):
    count = len(weights)
    moved = sum(w.size * w.dtype.itemsize for w in weights)
    return pl.pallas_call(
        functools.partial(hold_kernel, count),
        in_specs=[VMEM_SPEC] + [ANY_SPEC] * count,
        out_specs=[VMEM_SPEC] * (count + 1),
        out_shape=[pltpu.VMEM(w.shape, w.dtype) for w in weights] + [TOKEN],
        scratch_shapes=[pltpu.SemaphoreType.DMA((count,))],
        cost_estimate=pl.CostEstimate(flops=0, bytes_accessed=moved, transcendentals=0),
        compiler_params=pltpu.CompilerParams(vmem_limit_bytes=2 << 20),
        name="hold",
    )(after, *[in_hbm(w) for w in weights])


def my_core(pair):
    return lax.rem(lax.axis_index("blk"), pair)


def enter_kernel(pair, idx_hbm, hidden_hbm, mod_hbm, key_hbm, value_hbm, *refs):
    rows_ref, normed_ref, select_ref, mod_ref, *side_refs = refs[: pair + 4]
    idx_ref, hidden_ref, sems, kv_sem = refs[pair + 4 :]
    copies = [
        pltpu.make_async_copy(source, target, sems.at[i])
        for i, (source, target) in enumerate(
            [(idx_hbm, idx_ref), (hidden_hbm, hidden_ref), (mod_hbm, mod_ref)]
        )
    ]
    for copy in copies:
        copy.start()
    parts, _, both = side_refs[0].shape
    half = both // 2
    uly, core = lax.axis_index("uly"), my_core(pair)
    kv_copies = []
    for side, side_ref in enumerate(side_refs):
        for flip in range(parts):
            start = pl.multiple_of(((uly ^ flip) * pair + (core ^ side)) * half, DH)
            for at, source in enumerate((key_hbm, value_hbm)):
                copy = pltpu.make_async_copy(
                    source.at[:, pl.ds(start, half)],
                    side_ref.at[flip, :, pl.ds(at * half, half)],
                    kv_sem.at[side, flip, at],
                )
                copy.start()
                kv_copies.append(copy)
    for copy in copies:
        copy.wait()
    tokens, width = hidden_ref.shape
    slots = idx_ref.shape[1]
    position = lax.broadcasted_iota(jnp.int32, (tokens, slots), 0)
    select = (position == idx_ref[...]).astype(jnp.float32).astype(jnp.bfloat16)
    select_ref[...] = select
    contract = (((0,), (0,)), ((), ()))
    rows = lax.dot_general(
        select, hidden_ref[...], contract, preferred_element_type=jnp.float32
    )
    live = lax.dot_general(
        select,
        jnp.ones((tokens, DH), jnp.bfloat16),
        contract,
        preferred_element_type=jnp.float32,
    )
    rows_ref[...] = rows
    normed = layer_norm(rows, mod_ref[0:1, :], mod_ref[1:2, :])
    normed_ref[:, :width] = normed.astype(jnp.bfloat16)
    normed_ref[:, width:] = live.astype(jnp.bfloat16)
    for copy in kv_copies:
        copy.wait()


def enter(refresh_idx, hidden_in, modulation, cache_keys, cache_values, parts, pair):
    slots = refresh_idx.shape[0]
    tokens, width = hidden_in.shape
    both = 2 * width // (parts * pair)
    out = pl.pallas_call(
        functools.partial(enter_kernel, pair),
        in_specs=[ANY_SPEC] * 5,
        out_specs=[VMEM_SPEC] * (pair + 4),
        out_shape=[
            pltpu.VMEM((slots, width), jnp.float32),
            pltpu.VMEM((slots, width + DH), jnp.bfloat16),
            pltpu.VMEM((tokens, slots), jnp.bfloat16),
            pltpu.VMEM(modulation.shape, modulation.dtype),
        ]
        + [pltpu.VMEM((parts, tokens, both), cache_keys.dtype)] * pair,
        scratch_shapes=[
            pltpu.VMEM((1, slots), jnp.int32),
            pltpu.VMEM(hidden_in.shape, hidden_in.dtype),
            pltpu.SemaphoreType.DMA((3,)),
            pltpu.SemaphoreType.DMA((pair, parts, 2)),
        ],
        compiler_params=pltpu.CompilerParams(vmem_limit_bytes=8 << 20),
        name="enter",
    )(
        *[
            in_hbm(x)
            for x in (refresh_idx.reshape(1, slots), hidden_in, modulation, cache_keys, cache_values)
        ]
    )
    return *out[:4], out[4:]


def merge_kv_kernel(sides, flips, *refs):
    *refs, token_ref = refs
    token_ref[...] = jnp.zeros_like(token_ref)
    for flip, out_ref in zip(flips, refs[-len(flips) :]):
        for side in range(sides):
            out_ref[side] = refs[side][flip]


def merge_kv(sides, flips, after):
    _, tokens, both = sides[0].shape
    *merged, token = pl.pallas_call(
        functools.partial(merge_kv_kernel, len(sides), flips),
        out_specs=[VMEM_SPEC] * (len(flips) + 1),
        out_shape=[pltpu.VMEM((len(sides), tokens, both), sides[0].dtype) for _ in flips]
        + [TOKEN],
        compiler_params=pltpu.CompilerParams(vmem_limit_bytes=8 << 20),
        name="merge_kv",
    )(*sides, *after)
    return merged, token


def relay_kernel(x_ref, after_ref, out_ref):
    out_ref[...] = x_ref[...]


def relay(x, after):
    return pl.pallas_call(
        relay_kernel,
        out_specs=VMEM_SPEC,
        out_shape=pltpu.VMEM(x.shape, x.dtype),
        compiler_params=pltpu.CompilerParams(vmem_limit_bytes=2 << 20),
        name="relay",
    )(x, after)


def project_kernel(pieces, after_ref, *refs):
    rows_refs, (w_ref, gain_hbm_ref) = refs[:pieces], refs[pieces : pieces + 2]
    *query_refs, spread_ref, token_ref, heads_ref, gain_ref, sem = refs[pieces + 2 :]
    token_ref[...] = jnp.zeros_like(token_ref)
    copy = pltpu.make_async_copy(gain_hbm_ref, gain_ref, sem)
    copy.start()
    core = my_core(len(query_refs))
    width = w_ref.shape[0]
    group, half = query_refs[0].shape
    rows = jnp.concatenate([ref[...] for ref in rows_refs], axis=0)
    everyone = rows.shape[0]
    flags = rows[:, width:]
    shape = (everyone, everyone)
    before = lax.broadcasted_iota(jnp.int32, shape, 1) < lax.broadcasted_iota(jnp.int32, shape, 0)
    before = before.astype(jnp.float32).astype(jnp.bfloat16)
    rank = jnp.dot(before, flags, preferred_element_type=jnp.float32)
    lane = lax.broadcasted_iota(jnp.int32, rank.shape, 1).astype(jnp.float32)
    spread = jnp.where((rank == lane) & (flags.astype(jnp.float32) > 0.0), 1.0, 0.0)
    spread = spread.astype(jnp.bfloat16)
    spread_ref[...] = spread
    live_rows = lax.dot_general(
        spread[:, :group],
        rows[:, :width],
        (((0,), (0,)), ((), ())),
        preferred_element_type=jnp.float32,
    ).astype(jnp.bfloat16)
    projected = jnp.dot(live_rows, w_ref[...], preferred_element_type=jnp.float32)
    copy.wait()
    for start in range(0, projected.shape[1], DH):
        head = projected[:, start : start + DH]
        squares = jnp.mean(head * head, axis=-1, keepdims=True)
        heads_ref[:, start : start + DH] = (
            head * lax.rsqrt(squares + 1e-06) * (gain_ref[...] / math.sqrt(DH))
        )
    for side, query_ref in enumerate(query_refs):
        start = pl.multiple_of((core ^ side) * half, DH)
        query_ref[...] = heads_ref[:, pl.ds(start, half)].astype(jnp.bfloat16)


def project(after, rows, w_query, q_gain, group, pair):
    half = w_query.shape[1] // pair
    everyone = len(rows) * rows[0].shape[0]
    query = jax.ShapeDtypeStruct((group, half), jnp.bfloat16)
    out = pl.pallas_call(
        functools.partial(project_kernel, len(rows)),
        in_specs=[VMEM_SPEC] * (len(rows) + 2) + [ANY_SPEC],
        out_shape=[query] * pair + [jax.ShapeDtypeStruct((everyone, DH), jnp.bfloat16), TOKEN],
        scratch_shapes=[
            pltpu.VMEM((group, w_query.shape[1]), jnp.float32),
            pltpu.VMEM((1, DH), jnp.float32),
            pltpu.SemaphoreType.DMA,
        ],
        compiler_params=pltpu.CompilerParams(vmem_limit_bytes=16 << 20),
        name="project",
    )(after, *rows, w_query, in_hbm(q_gain.reshape(1, DH)))
    return out[:-2], out[-2], out[-1]


def head_scores(queries, kv_refs, head):
    half = queries.shape[1]
    cols = slice(head * DH, (head + 1) * DH)
    vals = slice(half + head * DH, half + (head + 1) * DH)
    sides = kv_refs[0].shape[0]
    keys = [ref[side, :, cols] for ref in kv_refs for side in range(sides)]
    values = [ref[side, :, vals] for ref in kv_refs for side in range(sides)]
    scores = lax.dot_general(
        queries[:, cols],
        jnp.concatenate(keys, axis=0),
        (((1,), (1,)), ((), ())),
        preferred_element_type=jnp.float32,
    )
    return scores, jnp.concatenate(values, axis=0)


def stacked(refs):
    rows = [ref[core].astype(jnp.float32) for ref in refs for core in range(ref.shape[0])]
    return jnp.concatenate(rows, axis=0).astype(jnp.bfloat16)


def attend_first_kernel(pieces, *refs):
    query_refs, (*kv_refs, sum_ref, stat_ref) = refs[:pieces], refs[pieces:]
    cores, group, half = query_refs[0].shape
    rows = cores * group
    for at in range(0, pieces, 4):
        queries = stacked(query_refs[at : at + 4])
        mine = slice(at * rows, at * rows + queries.shape[0])
        lane = lax.broadcasted_iota(jnp.int32, (queries.shape[0], DH), 1)
        stats = jnp.zeros((queries.shape[0], DH), jnp.float32)
        for head in range(half // DH):
            scores, values = head_scores(queries, kv_refs, head)
            maxima = jnp.max(scores, axis=-1, keepdims=True)
            weights = jnp.exp(scores - maxima)
            total = jnp.sum(weights, axis=-1, keepdims=True)
            sum_ref[mine, head * DH : (head + 1) * DH] = jnp.dot(
                weights.astype(jnp.bfloat16), values, preferred_element_type=jnp.float32
            )
            stats = jnp.where(lane == 2 * head, maxima, stats)
            stats = jnp.where(lane == 2 * head + 1, total, stats)
        stat_ref[mine, :] = stats


def attend_first(queries, kv_parts):
    cores, group, half = queries[0].shape
    count = cores * group * len(queries)
    return pl.pallas_call(
        functools.partial(attend_first_kernel, len(queries)),
        out_shape=[
            jax.ShapeDtypeStruct((count, half), jnp.float32),
            jax.ShapeDtypeStruct((count, DH), jnp.float32),
        ],
        cost_estimate=pl.CostEstimate(flops=10**9, bytes_accessed=0, transcendentals=0),
        compiler_params=pltpu.CompilerParams(vmem_limit_bytes=24 << 20),
        name="attend_first",
    )(*queries, *kv_parts)


def attend_last_kernel(pieces, after_ref, sum_ref, stat_ref, *refs):
    *refs, token_ref = refs
    token_ref[...] = jnp.zeros_like(token_ref)
    query_refs, kv_refs, out_refs = refs[:pieces], refs[pieces:-pieces], refs[-pieces:]
    cores, group, half = query_refs[0].shape
    rows = cores * group
    pad = jnp.zeros((DH - rows, DH), jnp.float32)
    for at in range(0, pieces, 4):
        stop = min(at + 4, pieces)
        queries = stacked(query_refs[at:stop])
        mine = slice(at * rows, stop * rows)
        before = stat_ref[mine, :]
        lane = lax.broadcasted_iota(jnp.int32, before.shape, 1)
        stats = jnp.zeros_like(before)
        for head in range(half // DH):
            cols = slice(head * DH, (head + 1) * DH)
            scores, values = head_scores(queries, kv_refs, head)
            earlier = before[:, 2 * head : 2 * head + 1]
            maxima = jnp.maximum(earlier, jnp.max(scores, axis=-1, keepdims=True))
            weights = jnp.exp(scores - maxima)
            factor = jnp.exp(earlier - maxima)
            total = before[:, 2 * head + 1 : 2 * head + 2] * factor
            total = total + jnp.sum(weights, axis=-1, keepdims=True)
            weighted = sum_ref[mine, cols] * factor + jnp.dot(
                weights.astype(jnp.bfloat16), values, preferred_element_type=jnp.float32
            )
            stats = jnp.where(lane == 2 * head, maxima, stats)
            stats = jnp.where(lane == 2 * head + 1, total, stats)
            for j in range(at, stop):
                out_refs[j][:rows, cols] = weighted[(j - at) * rows : (j - at + 1) * rows]
        for j in range(at, stop):
            own = stats[(j - at) * rows : (j - at + 1) * rows]
            out_refs[j][rows:, DH:] = jnp.zeros((8, half - DH), jnp.float32)
            out_refs[j][rows:, :DH] = jnp.concatenate([own, pad], axis=0).T[:8]


def attend_last(after, first, queries, kv_parts):
    cores, group, half = queries[0].shape
    rows = cores * group
    return pl.pallas_call(
        functools.partial(attend_last_kernel, len(queries)),
        out_shape=[jax.ShapeDtypeStruct((rows + 8, half), jnp.float32)] * len(queries) + [TOKEN],
        compiler_params=pltpu.CompilerParams(vmem_limit_bytes=24 << 20),
        name="attend_last",
    )(after, *first, *queries, *kv_parts)


def combine_kernel(pieces, after_ref, *refs):
    part_refs, out_refs = refs[:pieces], refs[pieces:]
    group, half = out_refs[0].shape
    rows = group * len(out_refs)
    stats = []
    for ref in part_refs:
        packed = ref[rows:, :DH]
        packed = jnp.concatenate([packed, jnp.zeros((DH - 8, DH), jnp.float32)], axis=0)
        stats.append(packed.T[:rows])
    for head in range(half // DH):
        cols = slice(head * DH, (head + 1) * DH)
        maxima = [stat[:, 2 * head : 2 * head + 1] for stat in stats]
        top = functools.reduce(jnp.maximum, maxima)
        total = jnp.zeros_like(top)
        attended = jnp.zeros((rows, DH), jnp.float32)
        for ref, stat, maximum in zip(part_refs, stats, maxima):
            factor = jnp.exp(maximum - top)
            total = total + stat[:, 2 * head + 1 : 2 * head + 2] * factor
            attended = attended + ref[:rows, cols] * factor
        attended = attended / total
        for side, out_ref in enumerate(out_refs):
            out_ref[:, cols] = attended[side * group : (side + 1) * group].astype(jnp.bfloat16)


def combine(after, parts, group, pair):
    half = parts[0].shape[1]
    return pl.pallas_call(
        functools.partial(combine_kernel, len(parts)),
        out_shape=[jax.ShapeDtypeStruct((group, half), jnp.bfloat16)] * pair,
        compiler_params=pltpu.CompilerParams(vmem_limit_bytes=16 << 20),
        name="combine",
    )(after, *parts)


def output_kernel(sides, spread_ref, *refs):
    side_refs, w_ref, (*out_refs, token_ref) = refs[:sides], refs[sides], refs[sides + 1 :]
    token_ref[...] = jnp.zeros_like(token_ref)
    group, half = side_refs[0].shape
    slots, width = out_refs[0].shape
    spread = spread_ref[:, :group]
    attended = [
        jnp.dot(spread, ref[...], preferred_element_type=jnp.float32).astype(jnp.bfloat16)
        for ref in side_refs
    ]
    core = my_core(sides)
    starts = [pl.multiple_of((core ^ side) * half, DH) for side in range(sides)]
    step = math.gcd(width, 1024)
    for col in range(0, width, step):
        terms = jnp.zeros((spread.shape[0], step), jnp.float32)
        for start, side in zip(starts, attended):
            terms = terms + jnp.dot(
                side, w_ref[pl.ds(start, half), col : col + step], preferred_element_type=jnp.float32
            )
        for k, out_ref in enumerate(out_refs):
            piece = terms[k * slots : (k + 1) * slots]
            out_ref[:, col : col + step] = piece.astype(out_ref.dtype)


def output(spread, sides, w_out, slots, parts):
    width = w_out.shape[1]
    return pl.pallas_call(
        functools.partial(output_kernel, len(sides)),
        out_shape=[
            jax.ShapeDtypeStruct((slots, width), jnp.bfloat16 if k else jnp.float32)
            for k in range(parts)
        ]
        + [TOKEN],
        compiler_params=pltpu.CompilerParams(vmem_limit_bytes=16 << 20),
        name="output",
    )(spread, *sides, w_out)


def mlp_kernel(pieces, *refs):
    row_refs, (up_ref, down_ref) = refs[:pieces], refs[pieces : pieces + 2]
    *out_refs, act_ref = refs[pieces + 2 :]
    hidden, width = down_ref.shape
    rows = [ref[j] for ref in row_refs for j in range(ref.shape[0])]
    rows = jnp.concatenate(rows, axis=0)
    count = out_refs[0].shape[0]
    step = math.gcd(hidden, 512)
    for col in range(0, hidden, step):
        lifted = jnp.dot(rows, up_ref[:, col : col + step], preferred_element_type=jnp.float32)
        act_ref[:, col : col + step] = jax.nn.gelu(lifted, approximate=True).astype(jnp.bfloat16)
    step = math.gcd(width, 512)
    for col in range(0, width, step):
        down = jnp.dot(
            act_ref[...], down_ref[:, col : col + step], preferred_element_type=jnp.float32
        )
        for side, out_ref in enumerate(out_refs):
            piece = down[side * count : (side + 1) * count]
            out_ref[:, col : col + step] = piece.astype(out_ref.dtype)


def mlp(rows, w_up, w_down, pair):
    count = sum(x.shape[0] * x.shape[1] for x in rows)
    hidden, width = w_down.shape
    return pl.pallas_call(
        functools.partial(mlp_kernel, len(rows)),
        out_shape=[
            jax.ShapeDtypeStruct((count // pair, width), jnp.bfloat16 if side else jnp.float32)
            for side in range(pair)
        ],
        scratch_shapes=[pltpu.VMEM((count, hidden), jnp.bfloat16)],
        compiler_params=pltpu.CompilerParams(vmem_limit_bytes=32 << 20),
        name="mlp",
    )(*rows, w_up, w_down)


def join_kernel(count, *refs):
    part_refs, out_ref = refs[:count], refs[-1]
    for at, ref in enumerate(part_refs):
        out_ref[at] = ref[...]


def join(parts, after=()):
    return pl.pallas_call(
        functools.partial(join_kernel, len(parts)),
        out_shape=jax.ShapeDtypeStruct((len(parts), *parts[0].shape), parts[0].dtype),
        compiler_params=pltpu.CompilerParams(vmem_limit_bytes=8 << 20),
        name="join",
    )(*parts, *after)


def renorm_kernel(hold_ref, rows_ref, mod_ref, *refs):
    *term_refs, after_ref, normed_ref = refs
    branch = term_refs[0][...]
    for ref in term_refs[1:]:
        branch = branch + ref[...].astype(jnp.float32)
    after = rows_ref[...] + mod_ref[2:3, :] * branch
    after_ref[...] = after
    normed_ref[...] = layer_norm(after, mod_ref[3:4, :], mod_ref[4:5, :]).astype(jnp.bfloat16)


def renorm(after, rows_in, modulation, terms):
    return pl.pallas_call(
        renorm_kernel,
        out_shape=[
            jax.ShapeDtypeStruct(rows_in.shape, jnp.float32),
            jax.ShapeDtypeStruct(rows_in.shape, jnp.bfloat16),
        ],
        compiler_params=pltpu.CompilerParams(vmem_limit_bytes=8 << 20),
        name="renorm",
    )(after, rows_in, modulation, *terms)


def fold_kernel(sides, *refs):
    side_refs, out_refs = refs[:sides], refs[sides:]
    slots = out_refs[0].shape[0]
    for j, out_ref in enumerate(out_refs):
        total = side_refs[0][j * slots : (j + 1) * slots]
        for ref in side_refs[1:]:
            total = total + ref[j * slots : (j + 1) * slots].astype(jnp.float32)
        out_ref[...] = total.astype(out_ref.dtype)


def fold(sides, slots):
    count, width = sides[0].shape
    return pl.pallas_call(
        functools.partial(fold_kernel, len(sides)),
        out_shape=[
            jax.ShapeDtypeStruct((slots, width), jnp.bfloat16 if j else jnp.float32)
            for j in range(count // slots)
        ],
        compiler_params=pltpu.CompilerParams(vmem_limit_bytes=8 << 20),
        name="fold",
    )(*sides)


def finish_kernel(select_ref, cached_ref, after_ref, mod_ref, *refs):
    *term_refs, out_ref = refs
    total = term_refs[0][...]
    for ref in term_refs[1:]:
        total = total + ref[...].astype(jnp.float32)
    renewed = (after_ref[...] + mod_ref[5:6, :] * total).astype(jnp.bfloat16)
    select = select_ref[...]
    placed = jnp.dot(select, renewed, preferred_element_type=jnp.float32)
    covered = jnp.sum(select.astype(jnp.float32), axis=1, keepdims=True)
    blended = cached_ref[...].astype(jnp.float32) * (1.0 - covered) + placed
    out_ref[...] = blended.astype(jnp.bfloat16)


def finish(select, cached, after_attn, modulation, terms):
    return pl.pallas_call(
        finish_kernel,
        out_shape=jax.ShapeDtypeStruct(cached.shape, jnp.bfloat16),
        compiler_params=pltpu.CompilerParams(vmem_limit_bytes=8 << 20),
        name="finish",
    )(select, cached, after_attn, modulation, *terms)


def body(
    hidden_in,
    cached_out,
    cache_keys,
    cache_values,
    refresh_idx,
    modulation,
    q_gain,
    w_query,
    w_out,
    w_up,
    w_down,
):
    slots = refresh_idx.shape[0]
    uly_size = lax.axis_size("uly")
    blk_size = lax.axis_size("blk")
    local_heads = w_query.shape[1] // DH
    group = min(slots * uly_size, slots + (uly_size - 1) * OTHER)
    pair = 2 if blk_size % 2 == 0 and local_heads % 2 == 0 else 1
    chips = blk_size // pair

    rows_in, normed, select, modulation, sides = enter(
        refresh_idx, hidden_in, modulation, cache_keys, cache_values, uly_size, pair
    )
    sides = [trade(x, "blk", side) for side, x in enumerate(sides)]
    w_query, token = hold(normed, w_query)
    half_way = uly_size // 2
    cuts = [[half_way, 0], [k for k in reversed(range(uly_size)) if k not in (0, 1, half_way)]]
    first, token = merge_kv(sides, cuts[0], [token])
    group_rows = double(normed, "uly", 1, uly_size, {half_way: lambda x: relay(x, token)})
    second, token = merge_kv(sides, cuts[1], group_rows[1:])
    kv_parts = [trade(x, "uly", k) for k, x in zip(cuts[0] + cuts[1], first + second)]

    queries, spread, token = project(token, group_rows, w_query, q_gain, group, pair)
    last, _ = merge_kv(sides, [1], [token])
    kv_parts.append(trade(last[0], "uly", 1))
    w_out, token = hold(token, w_out)
    queries = join([trade(x, "blk", side) for side, x in enumerate(queries)])
    queries = double(queries, "blk", pair, chips)
    first = attend_first(queries, kv_parts[:2])
    *parts, token = attend_last(token, first, queries, kv_parts[2:])
    w_up, token = hold(token, w_up)
    parts = [trade(x, "blk", j * pair) for j, x in enumerate(parts)]
    attended = combine(token, parts, group, pair)
    attended = [trade(x, "blk", side) for side, x in enumerate(attended)]
    *terms, token = output(spread, attended, w_out, slots, uly_size)
    w_down, cached, token = hold(token, w_down, cached_out)
    terms = [trade(x, "uly", k) for k, x in enumerate(terms)]
    after_attn, norm_mlp = renorm(token, rows_in, modulation, terms)

    rows = [join([trade(norm_mlp, "blk", j * pair) for j in range(chips)])]
    if pair == 2:
        rows.append(trade(rows[0], "blk", 1))
    down = mlp(rows, w_up, w_down, pair)
    down = [trade(x, "blk", side) for side, x in enumerate(down)]
    terms = [trade(x, "blk", j * pair) for j, x in enumerate(fold(down, slots))]
    return finish(select, cached, after_attn, modulation, terms)


def solution(mesh):
    return jax.shard_map(
        body,
        mesh=mesh,
        in_specs=(
            P(("blk", "uly"), None),
            P(("blk", "uly"), None),
            P(("blk", "uly"), None),
            P(("blk", "uly"), None),
            P(("blk", "uly")),
            P(),
            P(),
            P(None, "uly"),
            P("uly", None),
            P(None, "blk"),
            P("blk", None),
        ),
        out_specs=P(("blk", "uly"), None),
        check_vma=False,
    )
```

profile of v0, /device:TPU:0, one launch (start us, length us, event | category | flops | bytes accessed | tf_op | source)
XLA Modules:
  0.0 83.0 jit_solution(9738963198086274767)
XLA Ops:
  0.0 2.0 %enter.1 = (f32[16,3072]{1,0:T(8,128)S(1)}, bf16[16,3200]{1,0:T(8,128)(2,1)S(1)}, bf16[64,16]{1,0:T(8,128)(2,1)S(1)}, f32[6,3072]{1,0:T(8,128)S(1)}, bf16[4,64,7...) custom-call(s32[1,16]{1,0:T(1,128)} %bitcast.2, bf16[64,3072]{1,0:T(8,128)(2,1)} %hidden_hbm.1, f32[6,3072]{1,0:T(8,128)} %mod_hbm.1, ...), custom_call_target="tpu_custom_call" | custom-call | tf_op jit(solution)/shard_map/enter/pallas_call | solution.py:133
  2.6 3.7 %collective-permute-start.2 = (bf16[16,3200]{1,0:T(8,128)(2,1)S(1)}, bf16[16,3200]{1,0:T(8,128)(2,1)S(1)}, u32[]{:S(2)}, u32[]{:S(2)}) collective-permute-start(bf16[16,3200]{1,0:T(8,128)(2,1)S(1)} %get-tuple-element.55.refs_0_), channel_id=1, source_target_pairs={{0,2},{1,3},{2,0},{3,1},{4,6},{5,7},{6,4},{7,5},{8,10},{9,11},{10,... | collective-permute-start | bytes 307208 | tf_op jit(solution)/shard_map/ppermute | solution.py:38
  6.2 1.6 %collective-permute-start.1 = (bf16[16,3200]{1,0:T(8,128)(2,1)S(1)}, bf16[16,3200]{1,0:T(8,128)(2,1)S(1)}, u32[]{:S(2)}, u32[]{:S(2)}) collective-permute-start(bf16[16,3200]{1,0:T(8,128)(2,1)S(1)} %get-tuple-element.55.refs_0_), channel_id=1, source_target_pairs={{0,1},{1,0},{2,3},{3,2},{4,5},{5,4},{6,7},{7,6},{8,9},{9,8},{10,11... | collective-permute-start | bytes 307208 | tf_op jit(solution)/shard_map/ppermute | solution.py:38
  7.8 2.3 %hold.4 = (bf16[3072,768]{1,0:T(8,128)(2,1)S(1)}, f32[8,128]{1,0:T(8,128)S(1)}) custom-call(bf16[16,3200]{1,0:T(8,128)(2,1)S(1)} %get-tuple-element.55.refs_0_, bf16[3072,768]{1,0:T(8,128)(2,1)} %refs_1_.4), custom_call_target="tpu_custom_call" | custom-call | bytes 4718592 | tf_op jit(solution)/shard_map/hold/pallas_call | solution.py:62
  10.2 1.8 %collective-permute-done.2.x_ref = bf16[16,3200]{1,0:T(8,128)(2,1)S(1)} collective-permute-done((bf16[16,3200]{1,0:T(8,128)(2,1)S(1)}, bf16[16,3200]{1,0:T(8,128)(2,1)S(1)}, u32[]{:S(2)}, u32[]{:S(2)}) %collective-permute-start.2) | collective-permute-done | bytes 102432 | tf_op jit(solution)/shard_map/ppermute | solution.py:38
  12.7 3.4 %collective-permute-start.8 = (bf16[2,64,768]{2,1,0:T(8,128)(2,1)S(1)}, bf16[2,64,768]{2,1,0:T(8,128)(2,1)S(1)}, u32[]{:S(2)}, u32[]{:S(2)}) collective-permute-start(bf16[2,64,768]{2,1,0:T(8,128)(2,1)S(1)} %get-tuple-element.65), channel_id=1, source_target_pairs={{0,2},{1,3},{2,0},{3,1},{4,6},{5,7},{6,4},{7,5},{8,10},{9,11},{10,... | collective-permute-start | bytes 589832 | tf_op jit(solution)/shard_map/ppermute | solution.py:38
  19.4 1.6 %collective-permute-start.6 = (bf16[2,40,384]{2,1,0:T(8,128)(2,1)S(1)}, bf16[2,40,384]{2,1,0:T(8,128)(2,1)S(1)}, u32[]{:S(2)}, u32[]{:S(2)}) collective-permute-start(bf16[2,40,384]{2,1,0:T(8,128)(2,1)S(1)} %join.2.refs_0_), channel_id=1, source_target_pairs={{0,16},{4,20},{8,24},{12,28},{16,0},{20,4},{24,8},{28,12},{1,17},{... | collective-permute-start | bytes 184328 | tf_op jit(solution)/shard_map/ppermute | solution.py:38
  22.4 4.0 %collective-permute-start.9 = (bf16[2,64,768]{2,1,0:T(8,128)(2,1)S(1)}, bf16[2,64,768]{2,1,0:T(8,128)(2,1)S(1)}, u32[]{:S(2)}, u32[]{:S(2)}) collective-permute-start(bf16[2,64,768]{2,1,0:T(8,128)(2,1)S(1)} %get-tuple-element.69), channel_id=1, source_target_pairs={{0,3},{1,2},{2,1},{3,0},{4,7},{5,6},{6,5},{7,4},{8,11},{9,10},{10,... | collective-permute-start | bytes 589832 | tf_op jit(solution)/shard_map/ppermute | solution.py:38
  28.4 2.3 %hold.5 = (bf16[768,3072]{1,0:T(8,128)(2,1)S(1)}, f32[8,128]{1,0:T(8,128)S(1)}) custom-call(f32[8,128]{1,0:T(8,128)S(1)} %get-tuple-element.61.refs_0_.refs_2_, bf16[768,3072]{1,0:T(8,128)(2,1)} %refs_1_.5), custom_call_target="tpu_custom_call" | custom-call | bytes 4718592 | tf_op jit(solution)/shard_map/hold/pallas_call | solution.py:62
  32.7 2.9 %collective-permute-done.9.refs_4_ = bf16[2,64,768]{2,1,0:T(8,128)(2,1)S(1)} collective-permute-done((bf16[2,64,768]{2,1,0:T(8,128)(2,1)S(1)}, bf16[2,64,768]{2,1,0:T(8,128)(2,1)S(1)}, u32[]{:S(2)}, u32[]{:S(2)}) %collective-permute-start.9) | collective-permute-done | bytes 196640 | tf_op jit(solution)/shard_map/ppermute | solution.py:38
  35.6 2.3 %attend_last.1 = (f32[88,384]{1,0:T(8,128)S(1)}, f32[88,384]{1,0:T(8,128)S(1)}, f32[88,384]{1,0:T(8,128)S(1)}, f32[88,384]{1,0:T(8,128)S(1)}, f32[8,128]{1,0:T(8,128)S(1)}) custom-call(f32[8,128]{1,0:T(8,128)S(1)} %get-tuple-element.62.after_ref, f32[320,384]{1,0:T(8,128)S(1)} %get-tuple-element.67.sum_ref, f32[320,128]{1,0:T(8,128)S(1)} %get-tuple-element.68.stat_ref, ...), custom_call_target="tpu_custom_call" | custom-call | tf_op jit(solution)/shard_map/attend_last/pallas_call | solution.py:351
  37.9 1.5 %collective-permute-start.11 = (f32[88,384]{1,0:T(8,128)S(1)}, f32[88,384]{1,0:T(8,128)S(1)}, u32[]{:S(2)}, u32[]{:S(2)}) collective-permute-start(f32[88,384]{1,0:T(8,128)S(1)} %get-tuple-element.74), channel_id=1, source_target_pairs={{0,8},{4,12},{8,0},{12,4},{16,24},{20,28},{24,16},{28,20},{1,9},{5... | collective-permute-start | bytes 405512 | tf_op jit(solution)/shard_map/ppermute | solution.py:38
  41.4 3.7 %hold.6 = (bf16[3072,1536]{1,0:T(8,128)(2,1)S(1)}, f32[8,128]{1,0:T(8,128)S(1)}) custom-call(f32[8,128]{1,0:T(8,128)S(1)} %get-tuple-element.71.refs_0_, bf16[3072,1536]{1,0:T(8,128)(2,1)} %refs_1_.6), custom_call_target="tpu_custom_call" | custom-call | bytes 9437184 | tf_op jit(solution)/shard_map/hold/pallas_call | solution.py:62
  45.1 1.8 %collective-permute-done.12.refs_2_ = f32[88,384]{1,0:T(8,128)S(1)} collective-permute-done((f32[88,384]{1,0:T(8,128)S(1)}, f32[88,384]{1,0:T(8,128)S(1)}, u32[]{:S(2)}, u32[]{:S(2)}) %collective-permute-start.12) | collective-permute-done | bytes 135200 | tf_op jit(solution)/shard_map/ppermute | solution.py:38
  50.0 1.8 %collective-permute-start.16 = (bf16[16,3072]{1,0:T(8,128)(2,1)S(1)}, bf16[16,3072]{1,0:T(8,128)(2,1)S(1)}, u32[]{:S(2)}, u32[]{:S(2)}) collective-permute-start(bf16[16,3072]{1,0:T(8,128)(2,1)S(1)} %get-tuple-element.87), channel_id=1, source_target_pairs={{0,2},{1,3},{2,0},{3,1},{4,6},{5,7},{6,4},{7,5},{8,10},{9,11},{10,... | collective-permute-start | bytes 294920 | tf_op jit(solution)/shard_map/ppermute | solution.py:38
  51.8 2.3 %collective-permute-start.17 = (bf16[16,3072]{1,0:T(8,128)(2,1)S(1)}, bf16[16,3072]{1,0:T(8,128)(2,1)S(1)}, u32[]{:S(2)}, u32[]{:S(2)}) collective-permute-start(bf16[16,3072]{1,0:T(8,128)(2,1)S(1)} %get-tuple-element.88), channel_id=1, source_target_pairs={{0,3},{1,2},{2,1},{3,0},{4,7},{5,6},{6,5},{7,4},{8,11},{9,10},{10,... | collective-permute-start | bytes 294920 | tf_op jit(solution)/shard_map/ppermute | solution.py:38
  54.1 3.7 %hold.7 = (bf16[1536,3072]{1,0:T(8,128)(2,1)S(1)}, bf16[64,3072]{1,0:T(8,128)(2,1)S(1)}, f32[8,128]{1,0:T(8,128)S(1)}) custom-call(f32[8,128]{1,0:T(8,128)S(1)} %get-tuple-element.80.refs_0_, bf16[1536,3072]{1,0:T(8,128)(2,1)} %refs_1_.7, bf16[64,3072]{1,0:T(8,128)(2,1)} %refs_2_.1), custom_call_target="tpu_custom_call" | custom-call | bytes 9830400 | tf_op jit(solution)/shard_map/hold/pallas_call | solution.py:62
  57.9 2.5 %collective-permute-done.16.refs_2_ = bf16[16,3072]{1,0:T(8,128)(2,1)S(1)} collective-permute-done((bf16[16,3072]{1,0:T(8,128)(2,1)S(1)}, bf16[16,3072]{1,0:T(8,128)(2,1)S(1)}, u32[]{:S(2)}, u32[]{:S(2)}) %collective-permute-start.16) | collective-permute-done | bytes 98336 | tf_op jit(solution)/shard_map/ppermute | solution.py:38
  62.7 1.5 %collective-permute-start.18 = (bf16[16,3072]{1,0:T(8,128)(2,1)S(1)}, bf16[16,3072]{1,0:T(8,128)(2,1)S(1)}, u32[]{:S(2)}, u32[]{:S(2)}) collective-permute-start(bf16[16,3072]{1,0:T(8,128)(2,1)S(1)} %get-tuple-element.90.refs_0_), channel_id=1, source_target_pairs={{0,8},{4,12},{8,0},{12,4},{16,24},{20,28},{24,16},{28,20},{1,9},{5... | collective-permute-start | bytes 294920 | tf_op jit(solution)/shard_map/ppermute | solution.py:38
  64.2 2.4 %collective-permute-done.20.refs_3_ = bf16[16,3072]{1,0:T(8,128)(2,1)S(1)} collective-permute-done((bf16[16,3072]{1,0:T(8,128)(2,1)S(1)}, bf16[16,3072]{1,0:T(8,128)(2,1)S(1)}, u32[]{:S(2)}, u32[]{:S(2)}) %collective-permute-start.20) | collective-permute-done | bytes 98336 | tf_op jit(solution)/shard_map/ppermute | solution.py:38
  67.6 1.7 %collective-permute-done.21.refs_1_ = bf16[4,16,3072]{2,1,0:T(8,128)(2,1)S(1)} collective-permute-done((bf16[4,16,3072]{2,1,0:T(8,128)(2,1)S(1)}, bf16[4,16,3072]{2,1,0:T(8,128)(2,1)S(1)}, u32[]{:S(2)}, u32[]{:S(2)}) %collective-permute-start.21) | collective-permute-done | bytes 393248 | tf_op jit(solution)/shard_map/ppermute | solution.py:38
  69.3 2.7 %mlp.1 = (f32[64,3072]{1,0:T(8,128)S(1)}, bf16[64,3072]{1,0:T(8,128)(2,1)S(1)}) custom-call(bf16[4,16,3072]{2,1,0:T(8,128)(2,1)S(1)} %join.3.refs_0_, bf16[4,16,3072]{2,1,0:T(8,128)(2,1)S(1)} %collective-permute-done.21.refs_1_, bf16[3072,1536]{1,0:T(8,128)(2,1)S(1)} %get-tuple-element.91.refs_2_, bf16[1536,3072]{1,0:T(8,128)(2,1)S(1)} %get-tuple-element.92.refs_3_), custom_call_target="tpu_custom_call" | custom-call | tf_op jit(solution)/shard_map/mlp/pallas_call | solution.py:455
  72.2 1.6 %collective-permute-done.22.refs_1_ = bf16[64,3072]{1,0:T(8,128)(2,1)S(1)} collective-permute-done((bf16[64,3072]{1,0:T(8,128)(2,1)S(1)}, bf16[64,3072]{1,0:T(8,128)(2,1)S(1)}, u32[]{:S(2)}, u32[]{:S(2)}) %collective-permute-start.22) | collective-permute-done | bytes 393248 | tf_op jit(solution)/shard_map/ppermute | solution.py:38
  78.8 3.3 %collective-permute-done.24.refs_2_ = bf16[16,3072]{1,0:T(8,128)(2,1)S(1)} collective-permute-done((bf16[16,3072]{1,0:T(8,128)(2,1)S(1)}, bf16[16,3072]{1,0:T(8,128)(2,1)S(1)}, u32[]{:S(2)}, u32[]{:S(2)}) %collective-permute-start.24) | collective-permute-done | bytes 98336 | tf_op jit(solution)/shard_map/ppermute | solution.py:38
  (48 shorter events, 24.4 us)
Async XLA Ops:
  2.0 8.1 %collective-permute-start = (bf16[4,64,768]{2,1,0:T(8,128)(2,1)S(1)}, bf16[4,64,768]{2,1,0:T(8,128)(2,1)S(1)}, u32[]{:S(2)}, u32[]{:S(2)}) collective-permute-start(bf16[4,64,768]{2,1,0:T(8,128)(2,1)S(1)} %get-tuple-element.54), channel_id=1, source_target_pairs={{0,4},{4,0},{8,12},{12,8},{16,20},{20,16},{24,28},{28,24},{1,5},{5... | collective-permute-start | bytes 1179656 | tf_op jit(solution)/shard_map/ppermute | solution.py:38
  2.6 9.4 %collective-permute-start.2 = (bf16[16,3200]{1,0:T(8,128)(2,1)S(1)}, bf16[16,3200]{1,0:T(8,128)(2,1)S(1)}, u32[]{:S(2)}, u32[]{:S(2)}) collective-permute-start(bf16[16,3200]{1,0:T(8,128)(2,1)S(1)} %get-tuple-element.55.refs_0_), channel_id=1, source_target_pairs={{0,2},{1,3},{2,0},{3,1},{4,6},{5,7},{6,4},{7,5},{8,10},{9,11},{10,... | collective-permute-start | bytes 307208 | tf_op jit(solution)/shard_map/ppermute | solution.py:38
  6.2 9.9 %collective-permute-start.1 = (bf16[16,3200]{1,0:T(8,128)(2,1)S(1)}, bf16[16,3200]{1,0:T(8,128)(2,1)S(1)}, u32[]{:S(2)}, u32[]{:S(2)}) collective-permute-start(bf16[16,3200]{1,0:T(8,128)(2,1)S(1)} %get-tuple-element.55.refs_0_), channel_id=1, source_target_pairs={{0,1},{1,0},{2,3},{3,2},{4,5},{5,4},{6,7},{7,6},{8,9},{9,8},{10,11... | collective-permute-start | bytes 307208 | tf_op jit(solution)/shard_map/ppermute | solution.py:38
  12.0 4.7 %collective-permute-start.3 = (bf16[16,3200]{1,0:T(8,128)(2,1)S(1)}, bf16[16,3200]{1,0:T(8,128)(2,1)S(1)}, u32[]{:S(2)}, u32[]{:S(2)}) collective-permute-start(bf16[16,3200]{1,0:T(8,128)(2,1)S(1)} %relay.1.refs_3_.refs_2_), channel_id=1, source_target_pairs={{0,1},{1,0},{2,3},{3,2},{4,5},{5,4},{6,7},{7,6},{8,9},{9,8},{10,11... | collective-permute-start | bytes 307208 | tf_op jit(solution)/shard_map/ppermute | solution.py:38
  12.7 18.4 %collective-permute-start.8 = (bf16[2,64,768]{2,1,0:T(8,128)(2,1)S(1)}, bf16[2,64,768]{2,1,0:T(8,128)(2,1)S(1)}, u32[]{:S(2)}, u32[]{:S(2)}) collective-permute-start(bf16[2,64,768]{2,1,0:T(8,128)(2,1)S(1)} %get-tuple-element.65), channel_id=1, source_target_pairs={{0,2},{1,3},{2,0},{3,1},{4,6},{5,7},{6,4},{7,5},{8,10},{9,11},{10,... | collective-permute-start | bytes 589832 | tf_op jit(solution)/shard_map/ppermute | solution.py:38
  19.4 8.4 %collective-permute-start.6 = (bf16[2,40,384]{2,1,0:T(8,128)(2,1)S(1)}, bf16[2,40,384]{2,1,0:T(8,128)(2,1)S(1)}, u32[]{:S(2)}, u32[]{:S(2)}) collective-permute-start(bf16[2,40,384]{2,1,0:T(8,128)(2,1)S(1)} %join.2.refs_0_), channel_id=1, source_target_pairs={{0,16},{4,20},{8,24},{12,28},{16,0},{20,4},{24,8},{28,12},{1,17},{... | collective-permute-start | bytes 184328 | tf_op jit(solution)/shard_map/ppermute | solution.py:38
  21.6 11.1 %collective-permute-start.10 = (bf16[2,64,768]{2,1,0:T(8,128)(2,1)S(1)}, bf16[2,64,768]{2,1,0:T(8,128)(2,1)S(1)}, u32[]{:S(2)}, u32[]{:S(2)}) collective-permute-start(bf16[2,64,768]{2,1,0:T(8,128)(2,1)S(1)} %get-tuple-element.70), channel_id=1, source_target_pairs={{0,1},{1,0},{2,3},{3,2},{4,5},{5,4},{6,7},{7,6},{8,9},{9,8},{10,11... | collective-permute-start | bytes 589832 | tf_op jit(solution)/shard_map/ppermute | solution.py:38
  22.4 13.2 %collective-permute-start.9 = (bf16[2,64,768]{2,1,0:T(8,128)(2,1)S(1)}, bf16[2,64,768]{2,1,0:T(8,128)(2,1)S(1)}, u32[]{:S(2)}, u32[]{:S(2)}) collective-permute-start(bf16[2,64,768]{2,1,0:T(8,128)(2,1)S(1)} %get-tuple-element.69), channel_id=1, source_target_pairs={{0,3},{1,2},{2,1},{3,0},{4,7},{5,6},{6,5},{7,4},{8,11},{9,10},{10,... | collective-permute-start | bytes 589832 | tf_op jit(solution)/shard_map/ppermute | solution.py:38
  26.4 4.7 %collective-permute-start.5 = (bf16[2,40,384]{2,1,0:T(8,128)(2,1)S(1)}, bf16[2,40,384]{2,1,0:T(8,128)(2,1)S(1)}, u32[]{:S(2)}, u32[]{:S(2)}) collective-permute-start(bf16[2,40,384]{2,1,0:T(8,128)(2,1)S(1)} %join.2.refs_0_), channel_id=1, source_target_pairs={{0,8},{4,12},{8,0},{12,4},{16,24},{20,28},{24,16},{28,20},{1,9},{5... | collective-permute-start | bytes 184328 | tf_op jit(solution)/shard_map/ppermute | solution.py:38
  27.9 4.2 %collective-permute-start.7 = (bf16[2,40,384]{2,1,0:T(8,128)(2,1)S(1)}, bf16[2,40,384]{2,1,0:T(8,128)(2,1)S(1)}, u32[]{:S(2)}, u32[]{:S(2)}) collective-permute-start(bf16[2,40,384]{2,1,0:T(8,128)(2,1)S(1)} %collective-permute-done.6.refs_2_), channel_id=1, source_target_pairs={{0,8},{4,12},{8,0},{12,4},{16,24},{20,28},{24,16},{28,20},{1,9},{5... | collective-permute-start | bytes 184328 | tf_op jit(solution)/shard_map/ppermute | solution.py:38
  37.9 7.2 %collective-permute-start.11 = (f32[88,384]{1,0:T(8,128)S(1)}, f32[88,384]{1,0:T(8,128)S(1)}, u32[]{:S(2)}, u32[]{:S(2)}) collective-permute-start(f32[88,384]{1,0:T(8,128)S(1)} %get-tuple-element.74), channel_id=1, source_target_pairs={{0,8},{4,12},{8,0},{12,4},{16,24},{20,28},{24,16},{28,20},{1,9},{5... | collective-permute-start | bytes 405512 | tf_op jit(solution)/shard_map/ppermute | solution.py:38
  39.4 7.5 %collective-permute-start.12 = (f32[88,384]{1,0:T(8,128)S(1)}, f32[88,384]{1,0:T(8,128)S(1)}, u32[]{:S(2)}, u32[]{:S(2)}) collective-permute-start(f32[88,384]{1,0:T(8,128)S(1)} %get-tuple-element.75), channel_id=1, source_target_pairs={{0,16},{4,20},{8,24},{12,28},{16,0},{20,4},{24,8},{28,12},{1,17},{... | collective-permute-start | bytes 405512 | tf_op jit(solution)/shard_map/ppermute | solution.py:38
  39.9 7.0 %collective-permute-start.13 = (f32[88,384]{1,0:T(8,128)S(1)}, f32[88,384]{1,0:T(8,128)S(1)}, u32[]{:S(2)}, u32[]{:S(2)}) collective-permute-start(f32[88,384]{1,0:T(8,128)S(1)} %get-tuple-element.76), channel_id=1, source_target_pairs={{0,24},{4,28},{8,16},{12,20},{16,8},{20,12},{24,0},{28,4},{1,25},{... | collective-permute-start | bytes 405512 | tf_op jit(solution)/shard_map/ppermute | solution.py:38
  49.7 8.2 %collective-permute-start.15 = (bf16[16,3072]{1,0:T(8,128)(2,1)S(1)}, bf16[16,3072]{1,0:T(8,128)(2,1)S(1)}, u32[]{:S(2)}, u32[]{:S(2)}) collective-permute-start(bf16[16,3072]{1,0:T(8,128)(2,1)S(1)} %get-tuple-element.86), channel_id=1, source_target_pairs={{0,1},{1,0},{2,3},{3,2},{4,5},{5,4},{6,7},{7,6},{8,9},{9,8},{10,11... | collective-permute-start | bytes 294920 | tf_op jit(solution)/shard_map/ppermute | solution.py:38
  50.0 10.4 %collective-permute-start.16 = (bf16[16,3072]{1,0:T(8,128)(2,1)S(1)}, bf16[16,3072]{1,0:T(8,128)(2,1)S(1)}, u32[]{:S(2)}, u32[]{:S(2)}) collective-permute-start(bf16[16,3072]{1,0:T(8,128)(2,1)S(1)} %get-tuple-element.87), channel_id=1, source_target_pairs={{0,2},{1,3},{2,0},{3,1},{4,6},{5,7},{6,4},{7,5},{8,10},{9,11},{10,... | collective-permute-start | bytes 294920 | tf_op jit(solution)/shard_map/ppermute | solution.py:38
  51.8 8.6 %collective-permute-start.17 = (bf16[16,3072]{1,0:T(8,128)(2,1)S(1)}, bf16[16,3072]{1,0:T(8,128)(2,1)S(1)}, u32[]{:S(2)}, u32[]{:S(2)}) collective-permute-start(bf16[16,3072]{1,0:T(8,128)(2,1)S(1)} %get-tuple-element.88), channel_id=1, source_target_pairs={{0,3},{1,2},{2,1},{3,0},{4,7},{5,6},{6,5},{7,4},{8,11},{9,10},{10,... | collective-permute-start | bytes 294920 | tf_op jit(solution)/shard_map/ppermute | solution.py:38
  60.7 6.0 %collective-permute-start.20 = (bf16[16,3072]{1,0:T(8,128)(2,1)S(1)}, bf16[16,3072]{1,0:T(8,128)(2,1)S(1)}, u32[]{:S(2)}, u32[]{:S(2)}) collective-permute-start(bf16[16,3072]{1,0:T(8,128)(2,1)S(1)} %get-tuple-element.90.refs_0_), channel_id=1, source_target_pairs={{0,24},{4,28},{8,16},{12,20},{16,8},{20,12},{24,0},{28,4},{1,25},{... | collective-permute-start | bytes 294920 | tf_op jit(solution)/shard_map/ppermute | solution.py:38
  61.9 5.6 %collective-permute-start.19 = (bf16[16,3072]{1,0:T(8,128)(2,1)S(1)}, bf16[16,3072]{1,0:T(8,128)(2,1)S(1)}, u32[]{:S(2)}, u32[]{:S(2)}) collective-permute-start(bf16[16,3072]{1,0:T(8,128)(2,1)S(1)} %get-tuple-element.90.refs_0_), channel_id=1, source_target_pairs={{0,16},{4,20},{8,24},{12,28},{16,0},{20,4},{24,8},{28,12},{1,17},{... | collective-permute-start | bytes 294920 | tf_op jit(solution)/shard_map/ppermute | solution.py:38
  62.7 4.8 %collective-permute-start.18 = (bf16[16,3072]{1,0:T(8,128)(2,1)S(1)}, bf16[16,3072]{1,0:T(8,128)(2,1)S(1)}, u32[]{:S(2)}, u32[]{:S(2)}) collective-permute-start(bf16[16,3072]{1,0:T(8,128)(2,1)S(1)} %get-tuple-element.90.refs_0_), channel_id=1, source_target_pairs={{0,8},{4,12},{8,0},{12,4},{16,24},{20,28},{24,16},{28,20},{1,9},{5... | collective-permute-start | bytes 294920 | tf_op jit(solution)/shard_map/ppermute | solution.py:38
  67.5 1.8 %collective-permute-start.21 = (bf16[4,16,3072]{2,1,0:T(8,128)(2,1)S(1)}, bf16[4,16,3072]{2,1,0:T(8,128)(2,1)S(1)}, u32[]{:S(2)}, u32[]{:S(2)}) collective-permute-start(bf16[4,16,3072]{2,1,0:T(8,128)(2,1)S(1)} %join.3.refs_0_), channel_id=1, source_target_pairs={{0,4},{4,0},{8,12},{12,8},{16,20},{20,16},{24,28},{28,24},{1,5},{5... | collective-permute-start | bytes 1179656 | tf_op jit(solution)/shard_map/ppermute | solution.py:38
  72.0 1.8 %collective-permute-start.22 = (bf16[64,3072]{1,0:T(8,128)(2,1)S(1)}, bf16[64,3072]{1,0:T(8,128)(2,1)S(1)}, u32[]{:S(2)}, u32[]{:S(2)}) collective-permute-start(bf16[64,3072]{1,0:T(8,128)(2,1)S(1)} %get-tuple-element.94), channel_id=1, source_target_pairs={{0,4},{4,0},{8,12},{12,8},{16,20},{20,16},{24,28},{28,24},{1,5},{5... | collective-permute-start | bytes 1179656 | tf_op jit(solution)/shard_map/ppermute | solution.py:38
  73.9 4.9 %collective-permute-start.23 = (bf16[16,3072]{1,0:T(8,128)(2,1)S(1)}, bf16[16,3072]{1,0:T(8,128)(2,1)S(1)}, u32[]{:S(2)}, u32[]{:S(2)}) collective-permute-start(bf16[16,3072]{1,0:T(8,128)(2,1)S(1)} %get-tuple-element.96), channel_id=1, source_target_pairs={{0,8},{4,12},{8,0},{12,4},{16,24},{20,28},{24,16},{28,20},{1,9},{5... | collective-permute-start | bytes 294920 | tf_op jit(solution)/shard_map/ppermute | solution.py:38
  75.3 6.7 %collective-permute-start.24 = (bf16[16,3072]{1,0:T(8,128)(2,1)S(1)}, bf16[16,3072]{1,0:T(8,128)(2,1)S(1)}, u32[]{:S(2)}, u32[]{:S(2)}) collective-permute-start(bf16[16,3072]{1,0:T(8,128)(2,1)S(1)} %get-tuple-element.97), channel_id=1, source_target_pairs={{0,16},{4,20},{8,24},{12,28},{16,0},{20,4},{24,8},{28,12},{1,17},{... | collective-permute-start | bytes 294920 | tf_op jit(solution)/shard_map/ppermute | solution.py:38
  76.2 5.8 %collective-permute-start.25 = (bf16[16,3072]{1,0:T(8,128)(2,1)S(1)}, bf16[16,3072]{1,0:T(8,128)(2,1)S(1)}, u32[]{:S(2)}, u32[]{:S(2)}) collective-permute-start(bf16[16,3072]{1,0:T(8,128)(2,1)S(1)} %get-tuple-element.98), channel_id=1, source_target_pairs={{0,24},{4,28},{8,16},{12,20},{16,8},{20,12},{24,0},{28,4},{1,25},{... | collective-permute-start | bytes 294920 | tf_op jit(solution)/shard_map/ppermute | solution.py:38
  (2 other events, 2.5 us)
where the time goes:
time: 83.3 us; the launch traced here: 83 us
  starting transfers between devices  33.7 us (40%)
  Pallas kernels  24.7 us (30%)
  waiting for transfers between devices  24.5 us (29%)
    ppermute x26, starting transfers between devices, trade(): lax.ppermute(x, axis, [(i, i ^ flip) for i in range(lax.axis_size(axis))])  33.7 us
    ppermute x26, waiting for transfers between devices, trade(): lax.ppermute(x, axis, [(i, i ^ flip) for i in range(lax.axis_size(axis))])  24.5 us
    pallas_call x4, Pallas kernels, hold(): pl.pallas_call(functools.partial(hold_kernel, count), in_specs=[VMEM_SPEC...  12.1 us
    pallas_call x1, Pallas kernels, mlp(): pl.pallas_call(functools.partial(mlp_kernel, len(rows)), out_shape=[jax.S...  2.7 us
    pallas_call x1, Pallas kernels, attend_last(): pl.pallas_call(functools.partial(attend_last_kernel, len(queries)), out_s...  2.3 us
    pallas_call x1, Pallas kernels, enter(): pl.pallas_call(functools.partial(enter_kernel, pair), in_specs=[ANY_SPEC]...  2.02 us
  transfers between devices with their start and end apart: 26, of which 15 were waited for; matrix products, arithmetic and copies ran while one was open for 0% of the time, Pallas kernels for 18%

commit v1 on v0

--- a/solution.py
+++ b/solution.py
@@ -11,7 +11,7 @@
 DH = 128
 OTHER = 8
 VMEM_SPEC = pl.BlockSpec(memory_space=pltpu.VMEM)
-TOKEN = jax.ShapeDtypeStruct((8, DH), jnp.float32)
+TOKEN = pltpu.VMEM((8, DH), jnp.float32)
 ANY_SPEC = pl.BlockSpec(memory_space=pl.ANY)
 
 
@@ -267,6 +267,18 @@
     return scores, jnp.concatenate(values, axis=0)
 
 
+def lanes_of(stats):
+    packed = stats[:8]
+    for at in range(8, stats.shape[0], 8):
+        packed = packed + pltpu.roll(stats[at : at + 8], at, axis=1)
+    return packed
+
+
+def rows_of(packed, rows):
+    parts = [packed] + [pltpu.roll(packed, DH - at, axis=1) for at in range(8, rows, 8)]
+    return jnp.concatenate(parts, axis=0)
+
+
 def stacked(refs):
     rows = [ref[core].astype(jnp.float32) for ref in refs for core in range(ref.shape[0])]
     return jnp.concatenate(rows, axis=0).astype(jnp.bfloat16)
@@ -303,7 +315,7 @@
             jax.ShapeDtypeStruct((count, half), jnp.float32),
             jax.ShapeDtypeStruct((count, DH), jnp.float32),
         ],
-        cost_estimate=pl.CostEstimate(flops=10**9, bytes_accessed=0, transcendentals=0),
+        cost_estimate=pl.CostEstimate(flops=0, bytes_accessed=0, transcendentals=0),
         compiler_params=pltpu.CompilerParams(vmem_limit_bytes=24 << 20),
         name="attend_first",
     )(*queries, *kv_parts)
@@ -315,7 +327,6 @@
     query_refs, kv_refs, out_refs = refs[:pieces], refs[pieces:-pieces], refs[-pieces:]
     cores, group, half = query_refs[0].shape
     rows = cores * group
-    pad = jnp.zeros((DH - rows, DH), jnp.float32)
     for at in range(0, pieces, 4):
         stop = min(at + 4, pieces)
         queries = stacked(query_refs[at:stop])
@@ -342,7 +353,7 @@
         for j in range(at, stop):
             own = stats[(j - at) * rows : (j - at + 1) * rows]
             out_refs[j][rows:, DH:] = jnp.zeros((8, half - DH), jnp.float32)
-            out_refs[j][rows:, :DH] = jnp.concatenate([own, pad], axis=0).T[:8]
+            out_refs[j][rows:, :DH] = lanes_of(own)
 
 
 def attend_last(after, first, queries, kv_parts):
@@ -362,9 +373,7 @@
     rows = group * len(out_refs)
     stats = []
     for ref in part_refs:
-        packed = ref[rows:, :DH]
-        packed = jnp.concatenate([packed, jnp.zeros((DH - 8, DH), jnp.float32)], axis=0)
-        stats.append(packed.T[:rows])
+        stats.append(rows_of(ref[rows:, :DH], rows))
     for head in range(half // DH):
         cols = slice(head * DH, (head + 1) * DH)
         maxima = [stat[:, 2 * head : 2 * head + 1] for stat in stats]
@@ -573,15 +582,13 @@
     sides = [trade(x, "blk", side) for side, x in enumerate(sides)]
     w_query, token = hold(normed, w_query)
     half_way = uly_size // 2
-    cuts = [[half_way, 0], [k for k in reversed(range(uly_size)) if k not in (0, 1, half_way)]]
+    cuts = [[half_way, 0], [k for k in reversed(range(uly_size)) if k not in (0, half_way)]]
     first, token = merge_kv(sides, cuts[0], [token])
     group_rows = double(normed, "uly", 1, uly_size, {half_way: lambda x: relay(x, token)})
     second, token = merge_kv(sides, cuts[1], group_rows[1:])
     kv_parts = [trade(x, "uly", k) for k, x in zip(cuts[0] + cuts[1], first + second)]
 
     queries, spread, token = project(token, group_rows, w_query, q_gain, group, pair)
-    last, _ = merge_kv(sides, [1], [token])
-    kv_parts.append(trade(last[0], "uly", 1))
     w_out, token = hold(token, w_out)
     queries = join([trade(x, "blk", side) for side, x in enumerate(queries)])
     queries = double(queries, "blk", pair, chips)

time: 83.3 us -> 83 us (level)
  starting transfers between devices: 33.7 us -> 34.7 us
    ppermute x26, starting transfers between devices: 33.7 us -> 34.7 us  [trade(): lax.ppermute(x, axis, [(i, i ^ flip) for i in range(lax.axis_size(axis))])]
  transfers between devices with their start and end apart: 26 -> 26, of which waited for: 15 -> 15; matrix products, arithmetic and copies ran while one was open for 0% -> 0% of each run, Pallas kernels for 18% -> 17%
where the time goes in v1:
time: 83 us; the launch traced here: 82.7 us
  starting transfers between devices  34.7 us (42%)
  Pallas kernels  24.1 us (29%)
  waiting for transfers between devices  23.7 us (29%)
    ppermute x26, starting transfers between devices, trade(): lax.ppermute(x, axis, [(i, i ^ flip) for i in range(lax.axis_size(axis))])  34.7 us
    ppermute x26, waiting for transfers between devices, trade(): lax.ppermute(x, axis, [(i, i ^ flip) for i in range(lax.axis_size(axis))])  23.7 us
    pallas_call x4, Pallas kernels, hold(): pl.pallas_call(functools.partial(hold_kernel, count), in_specs=[VMEM_SPEC...  12.1 us
    pallas_call x1, Pallas kernels, mlp(): pl.pallas_call(functools.partial(mlp_kernel, len(rows)), out_shape=[jax.S...  2.71 us
    pallas_call x1, Pallas kernels, attend_last(): pl.pallas_call(functools.partial(attend_last_kernel, len(queries)), out_s...  2.32 us
    pallas_call x1, Pallas kernels, enter(): pl.pallas_call(functools.partial(enter_kernel, pair), in_specs=[ANY_SPEC]...  2.02 us
  transfers between devices with their start and end apart: 26, of which 15 were waited for; matrix products, arithmetic and copies ran while one was open for 0% of the time, Pallas kernels for 17%

profile of v1, /device:TPU:0, one launch (start us, length us, event | category | flops | bytes accessed | tf_op | source)
XLA Modules:
  0.0 82.7 jit_solution(6625865536369620460)
XLA Ops:
  0.0 2.0 %enter.1 = (f32[16,3072]{1,0:T(8,128)S(1)}, bf16[16,3200]{1,0:T(8,128)(2,1)S(1)}, bf16[64,16]{1,0:T(8,128)(2,1)S(1)}, f32[6,3072]{1,0:T(8,128)S(1)}, bf16[4,64,7...) custom-call(s32[1,16]{1,0:T(1,128)} %bitcast.2, bf16[64,3072]{1,0:T(8,128)(2,1)} %hidden_hbm.1, f32[6,3072]{1,0:T(8,128)} %mod_hbm.1, ...), custom_call_target="tpu_custom_call" | custom-call | tf_op jit(solution)/shard_map/enter/pallas_call | solution.py:133
  2.6 3.7 %collective-permute-start.2 = (bf16[16,3200]{1,0:T(8,128)(2,1)S(1)}, bf16[16,3200]{1,0:T(8,128)(2,1)S(1)}, u32[]{:S(2)}, u32[]{:S(2)}) collective-permute-start(bf16[16,3200]{1,0:T(8,128)(2,1)S(1)} %get-tuple-element.55.refs_0_), channel_id=1, source_target_pairs={{0,2},{1,3},{2,0},{3,1},{4,6},{5,7},{6,4},{7,5},{8,10},{9,11},{10,... | collective-permute-start | bytes 307208 | tf_op jit(solution)/shard_map/ppermute | solution.py:38
  6.2 1.6 %collective-permute-start.1 = (bf16[16,3200]{1,0:T(8,128)(2,1)S(1)}, bf16[16,3200]{1,0:T(8,128)(2,1)S(1)}, u32[]{:S(2)}, u32[]{:S(2)}) collective-permute-start(bf16[16,3200]{1,0:T(8,128)(2,1)S(1)} %get-tuple-element.55.refs_0_), channel_id=1, source_target_pairs={{0,1},{1,0},{2,3},{3,2},{4,5},{5,4},{6,7},{7,6},{8,9},{9,8},{10,11... | collective-permute-start | bytes 307208 | tf_op jit(solution)/shard_map/ppermute | solution.py:38
  7.8 2.3 %hold.4 = (bf16[3072,768]{1,0:T(8,128)(2,1)S(1)}, f32[8,128]{1,0:T(8,128)S(1)}) custom-call(bf16[16,3200]{1,0:T(8,128)(2,1)S(1)} %get-tuple-element.55.refs_0_, bf16[3072,768]{1,0:T(8,128)(2,1)} %refs_1_.4), custom_call_target="tpu_custom_call" | custom-call | bytes 4718592 | tf_op jit(solution)/shard_map/hold/pallas_call | solution.py:62
  10.2 1.8 %collective-permute-done.2.x_ref = bf16[16,3200]{1,0:T(8,128)(2,1)S(1)} collective-permute-done((bf16[16,3200]{1,0:T(8,128)(2,1)S(1)}, bf16[16,3200]{1,0:T(8,128)(2,1)S(1)}, u32[]{:S(2)}, u32[]{:S(2)}) %collective-permute-start.2) | collective-permute-done | bytes 102432 | tf_op jit(solution)/shard_map/ppermute | solution.py:38
  12.7 3.4 %collective-permute-start.8 = (bf16[2,64,768]{2,1,0:T(8,128)(2,1)S(1)}, bf16[2,64,768]{2,1,0:T(8,128)(2,1)S(1)}, u32[]{:S(2)}, u32[]{:S(2)}) collective-permute-start(bf16[2,64,768]{2,1,0:T(8,128)(2,1)S(1)} %get-tuple-element.65), channel_id=1, source_target_pairs={{0,2},{1,3},{2,0},{3,1},{4,6},{5,7},{6,4},{7,5},{8,10},{9,11},{10,... | collective-permute-start | bytes 589832 | tf_op jit(solution)/shard_map/ppermute | solution.py:38
  16.8 4.9 %collective-permute-start.9 = (bf16[2,64,768]{2,1,0:T(8,128)(2,1)S(1)}, bf16[2,64,768]{2,1,0:T(8,128)(2,1)S(1)}, u32[]{:S(2)}, u32[]{:S(2)}) collective-permute-start(bf16[2,64,768]{2,1,0:T(8,128)(2,1)S(1)} %get-tuple-element.69), channel_id=1, source_target_pairs={{0,3},{1,2},{2,1},{3,0},{4,7},{5,6},{6,5},{7,4},{8,11},{9,10},{10,... | collective-permute-start | bytes 589832 | tf_op jit(solution)/shard_map/ppermute | solution.py:38
  24.3 1.5 %collective-permute-start.6 = (bf16[2,40,384]{2,1,0:T(8,128)(2,1)S(1)}, bf16[2,40,384]{2,1,0:T(8,128)(2,1)S(1)}, u32[]{:S(2)}, u32[]{:S(2)}) collective-permute-start(bf16[2,40,384]{2,1,0:T(8,128)(2,1)S(1)} %join.2.refs_0_), channel_id=1, source_target_pairs={{0,16},{4,20},{8,24},{12,28},{16,0},{20,4},{24,8},{28,12},{1,17},{... | collective-permute-start | bytes 184328 | tf_op jit(solution)/shard_map/ppermute | solution.py:38
  25.8 1.5 %collective-permute-start.5 = (bf16[2,40,384]{2,1,0:T(8,128)(2,1)S(1)}, bf16[2,40,384]{2,1,0:T(8,128)(2,1)S(1)}, u32[]{:S(2)}, u32[]{:S(2)}) collective-permute-start(bf16[2,40,384]{2,1,0:T(8,128)(2,1)S(1)} %join.2.refs_0_), channel_id=1, source_target_pairs={{0,8},{4,12},{8,0},{12,4},{16,24},{20,28},{24,16},{28,20},{1,9},{5... | collective-permute-start | bytes 184328 | tf_op jit(solution)/shard_map/ppermute | solution.py:38
  30.0 2.3 %hold.5 = (bf16[768,3072]{1,0:T(8,128)(2,1)S(1)}, f32[8,128]{1,0:T(8,128)S(1)}) custom-call(f32[8,128]{1,0:T(8,128)S(1)} %get-tuple-element.61.refs_0_, bf16[768,3072]{1,0:T(8,128)(2,1)} %refs_1_.5), custom_call_target="tpu_custom_call" | custom-call | bytes 4718592 | tf_op jit(solution)/shard_map/hold/pallas_call | solution.py:62
  33.4 2.3 %attend_last.1 = (f32[88,384]{1,0:T(8,128)S(1)}, f32[88,384]{1,0:T(8,128)S(1)}, f32[88,384]{1,0:T(8,128)S(1)}, f32[88,384]{1,0:T(8,128)S(1)}, f32[8,128]{1,0:T(8,128)S(1)}) custom-call(f32[8,128]{1,0:T(8,128)S(1)} %get-tuple-element.62.after_ref, f32[320,384]{1,0:T(8,128)S(1)} %get-tuple-element.67.sum_ref, f32[320,128]{1,0:T(8,128)S(1)} %get-tuple-element.68.stat_ref, ...), custom_call_target="tpu_custom_call" | custom-call | tf_op jit(solution)/shard_map/attend_last/pallas_call | solution.py:362
  35.7 1.6 %collective-permute-start.11 = (f32[88,384]{1,0:T(8,128)S(1)}, f32[88,384]{1,0:T(8,128)S(1)}, u32[]{:S(2)}, u32[]{:S(2)}) collective-permute-start(f32[88,384]{1,0:T(8,128)S(1)} %get-tuple-element.74), channel_id=1, source_target_pairs={{0,8},{4,12},{8,0},{12,4},{16,24},{20,28},{24,16},{28,20},{1,9},{5... | collective-permute-start | bytes 405512 | tf_op jit(solution)/shard_map/ppermute | solution.py:38
  37.3 1.5 %collective-permute-start.12 = (f32[88,384]{1,0:T(8,128)S(1)}, f32[88,384]{1,0:T(8,128)S(1)}, u32[]{:S(2)}, u32[]{:S(2)}) collective-permute-start(f32[88,384]{1,0:T(8,128)S(1)} %get-tuple-element.75), channel_id=1, source_target_pairs={{0,16},{4,20},{8,24},{12,28},{16,0},{20,4},{24,8},{28,12},{1,17},{... | collective-permute-start | bytes 405512 | tf_op jit(solution)/shard_map/ppermute | solution.py:38
  39.3 3.7 %hold.6 = (bf16[3072,1536]{1,0:T(8,128)(2,1)S(1)}, f32[8,128]{1,0:T(8,128)S(1)}) custom-call(f32[8,128]{1,0:T(8,128)S(1)} %get-tuple-element.71.refs_0_, bf16[3072,1536]{1,0:T(8,128)(2,1)} %refs_1_.6), custom_call_target="tpu_custom_call" | custom-call | bytes 9437184 | tf_op jit(solution)/shard_map/hold/pallas_call | solution.py:62
  43.0 2.3 %collective-permute-done.12.refs_2_ = f32[88,384]{1,0:T(8,128)S(1)} collective-permute-done((f32[88,384]{1,0:T(8,128)S(1)}, f32[88,384]{1,0:T(8,128)S(1)}, u32[]{:S(2)}, u32[]{:S(2)}) %collective-permute-start.12) | collective-permute-done | bytes 135200 | tf_op jit(solution)/shard_map/ppermute | solution.py:38
  48.0 1.6 %collective-permute-start.15 = (bf16[16,3072]{1,0:T(8,128)(2,1)S(1)}, bf16[16,3072]{1,0:T(8,128)(2,1)S(1)}, u32[]{:S(2)}, u32[]{:S(2)}) collective-permute-start(bf16[16,3072]{1,0:T(8,128)(2,1)S(1)} %get-tuple-element.86), channel_id=1, source_target_pairs={{0,1},{1,0},{2,3},{3,2},{4,5},{5,4},{6,7},{7,6},{8,9},{9,8},{10,11... | collective-permute-start | bytes 294920 | tf_op jit(solution)/shard_map/ppermute | solution.py:38
  50.1 2.4 %collective-permute-start.17 = (bf16[16,3072]{1,0:T(8,128)(2,1)S(1)}, bf16[16,3072]{1,0:T(8,128)(2,1)S(1)}, u32[]{:S(2)}, u32[]{:S(2)}) collective-permute-start(bf16[16,3072]{1,0:T(8,128)(2,1)S(1)} %get-tuple-element.88), channel_id=1, source_target_pairs={{0,3},{1,2},{2,1},{3,0},{4,7},{5,6},{6,5},{7,4},{8,11},{9,10},{10,... | collective-permute-start | bytes 294920 | tf_op jit(solution)/shard_map/ppermute | solution.py:38
  52.5 3.7 %hold.7 = (bf16[1536,3072]{1,0:T(8,128)(2,1)S(1)}, bf16[64,3072]{1,0:T(8,128)(2,1)S(1)}, f32[8,128]{1,0:T(8,128)S(1)}) custom-call(f32[8,128]{1,0:T(8,128)S(1)} %get-tuple-element.80.refs_0_, bf16[1536,3072]{1,0:T(8,128)(2,1)} %refs_1_.7, bf16[64,3072]{1,0:T(8,128)(2,1)} %refs_2_.1), custom_call_target="tpu_custom_call" | custom-call | bytes 9830400 | tf_op jit(solution)/shard_map/hold/pallas_call | solution.py:62
  56.2 3.9 %collective-permute-done.16.refs_2_ = bf16[16,3072]{1,0:T(8,128)(2,1)S(1)} collective-permute-done((bf16[16,3072]{1,0:T(8,128)(2,1)S(1)}, bf16[16,3072]{1,0:T(8,128)(2,1)S(1)}, u32[]{:S(2)}, u32[]{:S(2)}) %collective-permute-start.16) | collective-permute-done | bytes 98336 | tf_op jit(solution)/shard_map/ppermute | solution.py:38
  63.9 2.1 %collective-permute-done.20.refs_3_ = bf16[16,3072]{1,0:T(8,128)(2,1)S(1)} collective-permute-done((bf16[16,3072]{1,0:T(8,128)(2,1)S(1)}, bf16[16,3072]{1,0:T(8,128)(2,1)S(1)}, u32[]{:S(2)}, u32[]{:S(2)}) %collective-permute-start.20) | collective-permute-done | bytes 98336 | tf_op jit(solution)/shard_map/ppermute | solution.py:38
  67.3 1.7 %collective-permute-done.21.refs_1_ = bf16[4,16,3072]{2,1,0:T(8,128)(2,1)S(1)} collective-permute-done((bf16[4,16,3072]{2,1,0:T(8,128)(2,1)S(1)}, bf16[4,16,3072]{2,1,0:T(8,128)(2,1)S(1)}, u32[]{:S(2)}, u32[]{:S(2)}) %collective-permute-start.21) | collective-permute-done | bytes 393248 | tf_op jit(solution)/shard_map/ppermute | solution.py:38
  69.0 2.7 %mlp.1 = (f32[64,3072]{1,0:T(8,128)S(1)}, bf16[64,3072]{1,0:T(8,128)(2,1)S(1)}) custom-call(bf16[4,16,3072]{2,1,0:T(8,128)(2,1)S(1)} %join.3.refs_0_, bf16[4,16,3072]{2,1,0:T(8,128)(2,1)S(1)} %collective-permute-done.21.refs_1_, bf16[3072,1536]{1,0:T(8,128)(2,1)S(1)} %get-tuple-element.91.refs_2_, bf16[1536,3072]{1,0:T(8,128)(2,1)S(1)} %get-tuple-element.92.refs_3_), custom_call_target="tpu_custom_call" | custom-call | tf_op jit(solution)/shard_map/mlp/pallas_call | solution.py:464
  71.9 1.6 %collective-permute-done.22.refs_1_ = bf16[64,3072]{1,0:T(8,128)(2,1)S(1)} collective-permute-done((bf16[64,3072]{1,0:T(8,128)(2,1)S(1)}, bf16[64,3072]{1,0:T(8,128)(2,1)S(1)}, u32[]{:S(2)}, u32[]{:S(2)}) %collective-permute-start.22) | collective-permute-done | bytes 393248 | tf_op jit(solution)/shard_map/ppermute | solution.py:38
  78.4 3.3 %collective-permute-done.24.refs_2_ = bf16[16,3072]{1,0:T(8,128)(2,1)S(1)} collective-permute-done((bf16[16,3072]{1,0:T(8,128)(2,1)S(1)}, bf16[16,3072]{1,0:T(8,128)(2,1)S(1)}, u32[]{:S(2)}, u32[]{:S(2)}) %collective-permute-start.24) | collective-permute-done | bytes 98336 | tf_op jit(solution)/shard_map/ppermute | solution.py:38
  (47 shorter events, 23.2 us)
Async XLA Ops:
  2.0 8.1 %collective-permute-start = (bf16[4,64,768]{2,1,0:T(8,128)(2,1)S(1)}, bf16[4,64,768]{2,1,0:T(8,128)(2,1)S(1)}, u32[]{:S(2)}, u32[]{:S(2)}) collective-permute-start(bf16[4,64,768]{2,1,0:T(8,128)(2,1)S(1)} %get-tuple-element.54), channel_id=1, source_target_pairs={{0,4},{4,0},{8,12},{12,8},{16,20},{20,16},{24,28},{28,24},{1,5},{5... | collective-permute-start | bytes 1179656 | tf_op jit(solution)/shard_map/ppermute | solution.py:38
  2.6 9.4 %collective-permute-start.2 = (bf16[16,3200]{1,0:T(8,128)(2,1)S(1)}, bf16[16,3200]{1,0:T(8,128)(2,1)S(1)}, u32[]{:S(2)}, u32[]{:S(2)}) collective-permute-start(bf16[16,3200]{1,0:T(8,128)(2,1)S(1)} %get-tuple-element.55.refs_0_), channel_id=1, source_target_pairs={{0,2},{1,3},{2,0},{3,1},{4,6},{5,7},{6,4},{7,5},{8,10},{9,11},{10,... | collective-permute-start | bytes 307208 | tf_op jit(solution)/shard_map/ppermute | solution.py:38
  6.2 9.9 %collective-permute-start.1 = (bf16[16,3200]{1,0:T(8,128)(2,1)S(1)}, bf16[16,3200]{1,0:T(8,128)(2,1)S(1)}, u32[]{:S(2)}, u32[]{:S(2)}) collective-permute-start(bf16[16,3200]{1,0:T(8,128)(2,1)S(1)} %get-tuple-element.55.refs_0_), channel_id=1, source_target_pairs={{0,1},{1,0},{2,3},{3,2},{4,5},{5,4},{6,7},{7,6},{8,9},{9,8},{10,11... | collective-permute-start | bytes 307208 | tf_op jit(solution)/shard_map/ppermute | solution.py:38
  12.0 4.7 %collective-permute-start.3 = (bf16[16,3200]{1,0:T(8,128)(2,1)S(1)}, bf16[16,3200]{1,0:T(8,128)(2,1)S(1)}, u32[]{:S(2)}, u32[]{:S(2)}) collective-permute-start(bf16[16,3200]{1,0:T(8,128)(2,1)S(1)} %relay.1.refs_3_.refs_2_), channel_id=1, source_target_pairs={{0,1},{1,0},{2,3},{3,2},{4,5},{5,4},{6,7},{7,6},{8,9},{9,8},{10,11... | collective-permute-start | bytes 307208 | tf_op jit(solution)/shard_map/ppermute | solution.py:38
  12.7 19.7 %collective-permute-start.8 = (bf16[2,64,768]{2,1,0:T(8,128)(2,1)S(1)}, bf16[2,64,768]{2,1,0:T(8,128)(2,1)S(1)}, u32[]{:S(2)}, u32[]{:S(2)}) collective-permute-start(bf16[2,64,768]{2,1,0:T(8,128)(2,1)S(1)} %get-tuple-element.65), channel_id=1, source_target_pairs={{0,2},{1,3},{2,0},{3,1},{4,6},{5,7},{6,4},{7,5},{8,10},{9,11},{10,... | collective-permute-start | bytes 589832 | tf_op jit(solution)/shard_map/ppermute | solution.py:38
  16.8 16.6 %collective-permute-start.9 = (bf16[2,64,768]{2,1,0:T(8,128)(2,1)S(1)}, bf16[2,64,768]{2,1,0:T(8,128)(2,1)S(1)}, u32[]{:S(2)}, u32[]{:S(2)}) collective-permute-start(bf16[2,64,768]{2,1,0:T(8,128)(2,1)S(1)} %get-tuple-element.69), channel_id=1, source_target_pairs={{0,3},{1,2},{2,1},{3,0},{4,7},{5,6},{6,5},{7,4},{8,11},{9,10},{10,... | collective-permute-start | bytes 589832 | tf_op jit(solution)/shard_map/ppermute | solution.py:38
  21.6 11.8 %collective-permute-start.10 = (bf16[2,64,768]{2,1,0:T(8,128)(2,1)S(1)}, bf16[2,64,768]{2,1,0:T(8,128)(2,1)S(1)}, u32[]{:S(2)}, u32[]{:S(2)}) collective-permute-start(bf16[2,64,768]{2,1,0:T(8,128)(2,1)S(1)} %get-tuple-element.70), channel_id=1, source_target_pairs={{0,1},{1,0},{2,3},{3,2},{4,5},{5,4},{6,7},{7,6},{8,9},{9,8},{10,11... | collective-permute-start | bytes 589832 | tf_op jit(solution)/shard_map/ppermute | solution.py:38
  24.3 4.2 %collective-permute-start.6 = (bf16[2,40,384]{2,1,0:T(8,128)(2,1)S(1)}, bf16[2,40,384]{2,1,0:T(8,128)(2,1)S(1)}, u32[]{:S(2)}, u32[]{:S(2)}) collective-permute-start(bf16[2,40,384]{2,1,0:T(8,128)(2,1)S(1)} %join.2.refs_0_), channel_id=1, source_target_pairs={{0,16},{4,20},{8,24},{12,28},{16,0},{20,4},{24,8},{28,12},{1,17},{... | collective-permute-start | bytes 184328 | tf_op jit(solution)/shard_map/ppermute | solution.py:38
  25.8 6.5 %collective-permute-start.5 = (bf16[2,40,384]{2,1,0:T(8,128)(2,1)S(1)}, bf16[2,40,384]{2,1,0:T(8,128)(2,1)S(1)}, u32[]{:S(2)}, u32[]{:S(2)}) collective-permute-start(bf16[2,40,384]{2,1,0:T(8,128)(2,1)S(1)} %join.2.refs_0_), channel_id=1, source_target_pairs={{0,8},{4,12},{8,0},{12,4},{16,24},{20,28},{24,16},{28,20},{1,9},{5... | collective-permute-start | bytes 184328 | tf_op jit(solution)/shard_map/ppermute | solution.py:38
  28.5 4.2 %collective-permute-start.7 = (bf16[2,40,384]{2,1,0:T(8,128)(2,1)S(1)}, bf16[2,40,384]{2,1,0:T(8,128)(2,1)S(1)}, u32[]{:S(2)}, u32[]{:S(2)}) collective-permute-start(bf16[2,40,384]{2,1,0:T(8,128)(2,1)S(1)} %collective-permute-done.6.refs_2_), channel_id=1, source_target_pairs={{0,8},{4,12},{8,0},{12,4},{16,24},{20,28},{24,16},{28,20},{1,9},{5... | collective-permute-start | bytes 184328 | tf_op jit(solution)/shard_map/ppermute | solution.py:38
  35.7 7.3 %collective-permute-start.11 = (f32[88,384]{1,0:T(8,128)S(1)}, f32[88,384]{1,0:T(8,128)S(1)}, u32[]{:S(2)}, u32[]{:S(2)}) collective-permute-start(f32[88,384]{1,0:T(8,128)S(1)} %get-tuple-element.74), channel_id=1, source_target_pairs={{0,8},{4,12},{8,0},{12,4},{16,24},{20,28},{24,16},{28,20},{1,9},{5... | collective-permute-start | bytes 405512 | tf_op jit(solution)/shard_map/ppermute | solution.py:38
  37.3 7.9 %collective-permute-start.12 = (f32[88,384]{1,0:T(8,128)S(1)}, f32[88,384]{1,0:T(8,128)S(1)}, u32[]{:S(2)}, u32[]{:S(2)}) collective-permute-start(f32[88,384]{1,0:T(8,128)S(1)} %get-tuple-element.75), channel_id=1, source_target_pairs={{0,16},{4,20},{8,24},{12,28},{16,0},{20,4},{24,8},{28,12},{1,17},{... | collective-permute-start | bytes 405512 | tf_op jit(solution)/shard_map/ppermute | solution.py:38
  38.8 6.4 %collective-permute-start.13 = (f32[88,384]{1,0:T(8,128)S(1)}, f32[88,384]{1,0:T(8,128)S(1)}, u32[]{:S(2)}, u32[]{:S(2)}) collective-permute-start(f32[88,384]{1,0:T(8,128)S(1)} %get-tuple-element.76), channel_id=1, source_target_pairs={{0,24},{4,28},{8,16},{12,20},{16,8},{20,12},{24,0},{28,4},{1,25},{... | collective-permute-start | bytes 405512 | tf_op jit(solution)/shard_map/ppermute | solution.py:38
  48.0 8.2 %collective-permute-start.15 = (bf16[16,3072]{1,0:T(8,128)(2,1)S(1)}, bf16[16,3072]{1,0:T(8,128)(2,1)S(1)}, u32[]{:S(2)}, u32[]{:S(2)}) collective-permute-start(bf16[16,3072]{1,0:T(8,128)(2,1)S(1)} %get-tuple-element.86), channel_id=1, source_target_pairs={{0,1},{1,0},{2,3},{3,2},{4,5},{5,4},{6,7},{7,6},{8,9},{9,8},{10,11... | collective-permute-start | bytes 294920 | tf_op jit(solution)/shard_map/ppermute | solution.py:38
  49.7 10.4 %collective-permute-start.16 = (bf16[16,3072]{1,0:T(8,128)(2,1)S(1)}, bf16[16,3072]{1,0:T(8,128)(2,1)S(1)}, u32[]{:S(2)}, u32[]{:S(2)}) collective-permute-start(bf16[16,3072]{1,0:T(8,128)(2,1)S(1)} %get-tuple-element.87), channel_id=1, source_target_pairs={{0,2},{1,3},{2,0},{3,1},{4,6},{5,7},{6,4},{7,5},{8,10},{9,11},{10,... | collective-permute-start | bytes 294920 | tf_op jit(solution)/shard_map/ppermute | solution.py:38
  50.1 10.0 %collective-permute-start.17 = (bf16[16,3072]{1,0:T(8,128)(2,1)S(1)}, bf16[16,3072]{1,0:T(8,128)(2,1)S(1)}, u32[]{:S(2)}, u32[]{:S(2)}) collective-permute-start(bf16[16,3072]{1,0:T(8,128)(2,1)S(1)} %get-tuple-element.88), channel_id=1, source_target_pairs={{0,3},{1,2},{2,1},{3,0},{4,7},{5,6},{6,5},{7,4},{8,11},{9,10},{10,... | collective-permute-start | bytes 294920 | tf_op jit(solution)/shard_map/ppermute | solution.py:38
  60.4 5.7 %collective-permute-start.20 = (bf16[16,3072]{1,0:T(8,128)(2,1)S(1)}, bf16[16,3072]{1,0:T(8,128)(2,1)S(1)}, u32[]{:S(2)}, u32[]{:S(2)}) collective-permute-start(bf16[16,3072]{1,0:T(8,128)(2,1)S(1)} %get-tuple-element.90.refs_0_), channel_id=1, source_target_pairs={{0,24},{4,28},{8,16},{12,20},{16,8},{20,12},{24,0},{28,4},{1,25},{... | collective-permute-start | bytes 294920 | tf_op jit(solution)/shard_map/ppermute | solution.py:38
  61.3 5.7 %collective-permute-start.19 = (bf16[16,3072]{1,0:T(8,128)(2,1)S(1)}, bf16[16,3072]{1,0:T(8,128)(2,1)S(1)}, u32[]{:S(2)}, u32[]{:S(2)}) collective-permute-start(bf16[16,3072]{1,0:T(8,128)(2,1)S(1)} %get-tuple-element.90.refs_0_), channel_id=1, source_target_pairs={{0,16},{4,20},{8,24},{12,28},{16,0},{20,4},{24,8},{28,12},{1,17},{... | collective-permute-start | bytes 294920 | tf_op jit(solution)/shard_map/ppermute | solution.py:38
  62.5 4.6 %collective-permute-start.18 = (bf16[16,3072]{1,0:T(8,128)(2,1)S(1)}, bf16[16,3072]{1,0:T(8,128)(2,1)S(1)}, u32[]{:S(2)}, u32[]{:S(2)}) collective-permute-start(bf16[16,3072]{1,0:T(8,128)(2,1)S(1)} %get-tuple-element.90.refs_0_), channel_id=1, source_target_pairs={{0,8},{4,12},{8,0},{12,4},{16,24},{20,28},{24,16},{28,20},{1,9},{5... | collective-permute-start | bytes 294920 | tf_op jit(solution)/shard_map/ppermute | solution.py:38
  67.2 1.8 %collective-permute-start.21 = (bf16[4,16,3072]{2,1,0:T(8,128)(2,1)S(1)}, bf16[4,16,3072]{2,1,0:T(8,128)(2,1)S(1)}, u32[]{:S(2)}, u32[]{:S(2)}) collective-permute-start(bf16[4,16,3072]{2,1,0:T(8,128)(2,1)S(1)} %join.3.refs_0_), channel_id=1, source_target_pairs={{0,4},{4,0},{8,12},{12,8},{16,20},{20,16},{24,28},{28,24},{1,5},{5... | collective-permute-start | bytes 1179656 | tf_op jit(solution)/shard_map/ppermute | solution.py:38
  71.7 1.8 %collective-permute-start.22 = (bf16[64,3072]{1,0:T(8,128)(2,1)S(1)}, bf16[64,3072]{1,0:T(8,128)(2,1)S(1)}, u32[]{:S(2)}, u32[]{:S(2)}) collective-permute-start(bf16[64,3072]{1,0:T(8,128)(2,1)S(1)} %get-tuple-element.94), channel_id=1, source_target_pairs={{0,4},{4,0},{8,12},{12,8},{16,20},{20,16},{24,28},{28,24},{1,5},{5... | collective-permute-start | bytes 1179656 | tf_op jit(solution)/shard_map/ppermute | solution.py:38
  73.5 4.9 %collective-permute-start.23 = (bf16[16,3072]{1,0:T(8,128)(2,1)S(1)}, bf16[16,3072]{1,0:T(8,128)(2,1)S(1)}, u32[]{:S(2)}, u32[]{:S(2)}) collective-permute-start(bf16[16,3072]{1,0:T(8,128)(2,1)S(1)} %get-tuple-element.96), channel_id=1, source_target_pairs={{0,8},{4,12},{8,0},{12,4},{16,24},{20,28},{24,16},{28,20},{1,9},{5... | collective-permute-start | bytes 294920 | tf_op jit(solution)/shard_map/ppermute | solution.py:38
  75.0 6.7 %collective-permute-start.24 = (bf16[16,3072]{1,0:T(8,128)(2,1)S(1)}, bf16[16,3072]{1,0:T(8,128)(2,1)S(1)}, u32[]{:S(2)}, u32[]{:S(2)}) collective-permute-start(bf16[16,3072]{1,0:T(8,128)(2,1)S(1)} %get-tuple-element.97), channel_id=1, source_target_pairs={{0,16},{4,20},{8,24},{12,28},{16,0},{20,4},{24,8},{28,12},{1,17},{... | collective-permute-start | bytes 294920 | tf_op jit(solution)/shard_map/ppermute | solution.py:38
  76.1 5.7 %collective-permute-start.25 = (bf16[16,3072]{1,0:T(8,128)(2,1)S(1)}, bf16[16,3072]{1,0:T(8,128)(2,1)S(1)}, u32[]{:S(2)}, u32[]{:S(2)}) collective-permute-start(bf16[16,3072]{1,0:T(8,128)(2,1)S(1)} %get-tuple-element.98), channel_id=1, source_target_pairs={{0,24},{4,28},{8,16},{12,20},{16,8},{20,12},{24,0},{28,4},{1,25},{... | collective-permute-start | bytes 294920 | tf_op jit(solution)/shard_map/ppermute | solution.py:38
  (2 other events, 2.5 us)

commit v2 on v1

--- a/solution.py
+++ b/solution.py
@@ -284,26 +284,32 @@
     return jnp.concatenate(rows, axis=0).astype(jnp.bfloat16)
 
 
+def along_lanes(column):
+    return jnp.broadcast_to(column, (column.shape[0], DH))
+
+
+def weights_of(scores, maxima):
+    width = scores.shape[1]
+    return [jnp.exp(scores[:, at : at + DH] - maxima) for at in range(0, width, DH)]
+
+
 def attend_first_kernel(pieces, *refs):
-    query_refs, (*kv_refs, sum_ref, stat_ref) = refs[:pieces], refs[pieces:]
+    query_refs, (*kv_refs, sum_ref, max_ref, total_ref) = refs[:pieces], refs[pieces:]
     cores, group, half = query_refs[0].shape
     rows = cores * group
     for at in range(0, pieces, 4):
         queries = stacked(query_refs[at : at + 4])
         mine = slice(at * rows, at * rows + queries.shape[0])
-        lane = lax.broadcasted_iota(jnp.int32, (queries.shape[0], DH), 1)
-        stats = jnp.zeros((queries.shape[0], DH), jnp.float32)
         for head in range(half // DH):
+            cols = slice(head * DH, (head + 1) * DH)
             scores, values = head_scores(queries, kv_refs, head)
-            maxima = jnp.max(scores, axis=-1, keepdims=True)
-            weights = jnp.exp(scores - maxima)
-            total = jnp.sum(weights, axis=-1, keepdims=True)
-            sum_ref[mine, head * DH : (head + 1) * DH] = jnp.dot(
+            maxima = along_lanes(jnp.max(scores, axis=-1, keepdims=True))
+            weights = jnp.concatenate(weights_of(scores, maxima), axis=1)
+            max_ref[mine, cols] = maxima
+            total_ref[mine, cols] = along_lanes(jnp.sum(weights, axis=-1, keepdims=True))
+            sum_ref[mine, cols] = jnp.dot(
                 weights.astype(jnp.bfloat16), values, preferred_element_type=jnp.float32
             )
-            stats = jnp.where(lane == 2 * head, maxima, stats)
-            stats = jnp.where(lane == 2 * head + 1, total, stats)
-        stat_ref[mine, :] = stats
 
 
 def attend_first(queries, kv_parts):
@@ -311,17 +317,15 @@
     count = cores * group * len(queries)
     return pl.pallas_call(
         functools.partial(attend_first_kernel, len(queries)),
-        out_shape=[
-            jax.ShapeDtypeStruct((count, half), jnp.float32),
-            jax.ShapeDtypeStruct((count, DH), jnp.float32),
-        ],
+        out_specs=[VMEM_SPEC] * 3,
+        out_shape=[pltpu.VMEM((count, half), jnp.float32)] * 3,
         cost_estimate=pl.CostEstimate(flops=0, bytes_accessed=0, transcendentals=0),
         compiler_params=pltpu.CompilerParams(vmem_limit_bytes=24 << 20),
         name="attend_first",
     )(*queries, *kv_parts)
 
 
-def attend_last_kernel(pieces, after_ref, sum_ref, stat_ref, *refs):
+def attend_last_kernel(pieces, after_ref, sum_ref, max_ref, total_ref, *refs):
     *refs, token_ref = refs
     token_ref[...] = jnp.zeros_like(token_ref)
     query_refs, kv_refs, out_refs = refs[:pieces], refs[pieces:-pieces], refs[-pieces:]
@@ -331,18 +335,18 @@
         stop = min(at + 4, pieces)
         queries = stacked(query_refs[at:stop])
         mine = slice(at * rows, stop * rows)
-        before = stat_ref[mine, :]
-        lane = lax.broadcasted_iota(jnp.int32, before.shape, 1)
-        stats = jnp.zeros_like(before)
+        lane = lax.broadcasted_iota(jnp.int32, (queries.shape[0], DH), 1)
+        stats = jnp.zeros((queries.shape[0], DH), jnp.float32)
         for head in range(half // DH):
             cols = slice(head * DH, (head + 1) * DH)
             scores, values = head_scores(queries, kv_refs, head)
-            earlier = before[:, 2 * head : 2 * head + 1]
-            maxima = jnp.maximum(earlier, jnp.max(scores, axis=-1, keepdims=True))
-            weights = jnp.exp(scores - maxima)
+            earlier = max_ref[mine, cols]
+            maxima = along_lanes(jnp.max(scores, axis=-1, keepdims=True))
+            maxima = jnp.maximum(earlier, maxima)
+            weights = jnp.concatenate(weights_of(scores, maxima), axis=1)
             factor = jnp.exp(earlier - maxima)
-            total = before[:, 2 * head + 1 : 2 * head + 2] * factor
-            total = total + jnp.sum(weights, axis=-1, keepdims=True)
+            total = along_lanes(jnp.sum(weights, axis=-1, keepdims=True))
+            total = total_ref[mine, cols] * factor + total
             weighted = sum_ref[mine, cols] * factor + jnp.dot(
                 weights.astype(jnp.bfloat16), values, preferred_element_type=jnp.float32
             )
@@ -361,7 +365,8 @@
     rows = cores * group
     return pl.pallas_call(
         functools.partial(attend_last_kernel, len(queries)),
-        out_shape=[jax.ShapeDtypeStruct((rows + 8, half), jnp.float32)] * len(queries) + [TOKEN],
+        out_specs=[VMEM_SPEC] * (len(queries) + 1),
+        out_shape=[pltpu.VMEM((rows + 8, half), jnp.float32)] * len(queries) + [TOKEN],
         compiler_params=pltpu.CompilerParams(vmem_limit_bytes=24 << 20),
         name="attend_last",
     )(after, *first, *queries, *kv_parts)

time: 83 us -> 81.4 us (0.981)
  Pallas kernels: 24.1 us -> 22.5 us
    pallas_call x1, Pallas kernels: 2.32 us -> 0.74 us  [attend_last(): pl.pallas_call(functools.partial(attend_last_kernel, len(queries)), out_s...]
where the time goes in v2:
time: 81.4 us; the launch traced here: 81.1 us
  starting transfers between devices  34.7 us (43%)
  waiting for transfers between devices  23.7 us (29%)
  Pallas kernels  22.5 us (28%)
    ppermute x26, starting transfers between devices, trade(): lax.ppermute(x, axis, [(i, i ^ flip) for i in range(lax.axis_size(axis))])  34.7 us
    ppermute x26, waiting for transfers between devices, trade(): lax.ppermute(x, axis, [(i, i ^ flip) for i in range(lax.axis_size(axis))])  23.7 us
    pallas_call x4, Pallas kernels, hold(): pl.pallas_call(functools.partial(hold_kernel, count), in_specs=[VMEM_SPEC...  12.1 us
    pallas_call x1, Pallas kernels, mlp(): pl.pallas_call(functools.partial(mlp_kernel, len(rows)), out_shape=[jax.S...  2.7 us
    pallas_call x1, Pallas kernels, enter(): pl.pallas_call(functools.partial(enter_kernel, pair), in_specs=[ANY_SPEC]...  2.02 us
  transfers between devices with their start and end apart: 26, of which 15 were waited for; matrix products, arithmetic and copies ran while one was open for 0% of the time, Pallas kernels for 17%

profile of v2, /device:TPU:0, one launch (start us, length us, event | category | flops | bytes accessed | tf_op | source)
XLA Modules:
  0.0 81.1 jit_solution(10730097652333609216)
XLA Ops:
  0.0 2.0 %enter.1 = (f32[16,3072]{1,0:T(8,128)S(1)}, bf16[16,3200]{1,0:T(8,128)(2,1)S(1)}, bf16[64,16]{1,0:T(8,128)(2,1)S(1)}, f32[6,3072]{1,0:T(8,128)S(1)}, bf16[4,64,7...) custom-call(s32[1,16]{1,0:T(1,128)} %bitcast.2, bf16[64,3072]{1,0:T(8,128)(2,1)} %hidden_hbm.1, f32[6,3072]{1,0:T(8,128)} %mod_hbm.1, ...), custom_call_target="tpu_custom_call" | custom-call | tf_op jit(solution)/shard_map/enter/pallas_call | solution.py:133
  2.6 3.7 %collective-permute-start.2 = (bf16[16,3200]{1,0:T(8,128)(2,1)S(1)}, bf16[16,3200]{1,0:T(8,128)(2,1)S(1)}, u32[]{:S(2)}, u32[]{:S(2)}) collective-permute-start(bf16[16,3200]{1,0:T(8,128)(2,1)S(1)} %get-tuple-element.56.refs_0_), channel_id=1, source_target_pairs={{0,2},{1,3},{2,0},{3,1},{4,6},{5,7},{6,4},{7,5},{8,10},{9,11},{10,... | collective-permute-start | bytes 307208 | tf_op jit(solution)/shard_map/ppermute | solution.py:38
  6.2 1.6 %collective-permute-start.1 = (bf16[16,3200]{1,0:T(8,128)(2,1)S(1)}, bf16[16,3200]{1,0:T(8,128)(2,1)S(1)}, u32[]{:S(2)}, u32[]{:S(2)}) collective-permute-start(bf16[16,3200]{1,0:T(8,128)(2,1)S(1)} %get-tuple-element.56.refs_0_), channel_id=1, source_target_pairs={{0,1},{1,0},{2,3},{3,2},{4,5},{5,4},{6,7},{7,6},{8,9},{9,8},{10,11... | collective-permute-start | bytes 307208 | tf_op jit(solution)/shard_map/ppermute | solution.py:38
  7.8 2.3 %hold.4 = (bf16[3072,768]{1,0:T(8,128)(2,1)S(1)}, f32[8,128]{1,0:T(8,128)S(1)}) custom-call(bf16[16,3200]{1,0:T(8,128)(2,1)S(1)} %get-tuple-element.56.refs_0_, bf16[3072,768]{1,0:T(8,128)(2,1)} %refs_1_.4), custom_call_target="tpu_custom_call" | custom-call | bytes 4718592 | tf_op jit(solution)/shard_map/hold/pallas_call | solution.py:62
  10.2 1.8 %collective-permute-done.2.x_ref = bf16[16,3200]{1,0:T(8,128)(2,1)S(1)} collective-permute-done((bf16[16,3200]{1,0:T(8,128)(2,1)S(1)}, bf16[16,3200]{1,0:T(8,128)(2,1)S(1)}, u32[]{:S(2)}, u32[]{:S(2)}) %collective-permute-start.2) | collective-permute-done | bytes 102432 | tf_op jit(solution)/shard_map/ppermute | solution.py:38
  12.7 3.4 %collective-permute-start.8 = (bf16[2,64,768]{2,1,0:T(8,128)(2,1)S(1)}, bf16[2,64,768]{2,1,0:T(8,128)(2,1)S(1)}, u32[]{:S(2)}, u32[]{:S(2)}) collective-permute-start(bf16[2,64,768]{2,1,0:T(8,128)(2,1)S(1)} %get-tuple-element.66), channel_id=1, source_target_pairs={{0,2},{1,3},{2,0},{3,1},{4,6},{5,7},{6,4},{7,5},{8,10},{9,11},{10,... | collective-permute-start | bytes 589832 | tf_op jit(solution)/shard_map/ppermute | solution.py:38
  16.8 4.9 %collective-permute-start.9 = (bf16[2,64,768]{2,1,0:T(8,128)(2,1)S(1)}, bf16[2,64,768]{2,1,0:T(8,128)(2,1)S(1)}, u32[]{:S(2)}, u32[]{:S(2)}) collective-permute-start(bf16[2,64,768]{2,1,0:T(8,128)(2,1)S(1)} %get-tuple-element.71), channel_id=1, source_target_pairs={{0,3},{1,2},{2,1},{3,0},{4,7},{5,6},{6,5},{7,4},{8,11},{9,10},{10,... | collective-permute-start | bytes 589832 | tf_op jit(solution)/shard_map/ppermute | solution.py:38
  24.3 1.5 %collective-permute-start.6 = (bf16[2,40,384]{2,1,0:T(8,128)(2,1)S(1)}, bf16[2,40,384]{2,1,0:T(8,128)(2,1)S(1)}, u32[]{:S(2)}, u32[]{:S(2)}) collective-permute-start(bf16[2,40,384]{2,1,0:T(8,128)(2,1)S(1)} %join.2.refs_0_), channel_id=1, source_target_pairs={{0,16},{4,20},{8,24},{12,28},{16,0},{20,4},{24,8},{28,12},{1,17},{... | collective-permute-start | bytes 184328 | tf_op jit(solution)/shard_map/ppermute | solution.py:38
  25.8 1.5 %collective-permute-start.5 = (bf16[2,40,384]{2,1,0:T(8,128)(2,1)S(1)}, bf16[2,40,384]{2,1,0:T(8,128)(2,1)S(1)}, u32[]{:S(2)}, u32[]{:S(2)}) collective-permute-start(bf16[2,40,384]{2,1,0:T(8,128)(2,1)S(1)} %join.2.refs_0_), channel_id=1, source_target_pairs={{0,8},{4,12},{8,0},{12,4},{16,24},{20,28},{24,16},{28,20},{1,9},{5... | collective-permute-start | bytes 184328 | tf_op jit(solution)/shard_map/ppermute | solution.py:38
  28.5 1.5 %collective-permute-start.7 = (bf16[2,40,384]{2,1,0:T(8,128)(2,1)S(1)}, bf16[2,40,384]{2,1,0:T(8,128)(2,1)S(1)}, u32[]{:S(2)}, u32[]{:S(2)}) collective-permute-start(bf16[2,40,384]{2,1,0:T(8,128)(2,1)S(1)} %collective-permute-done.6.refs_2_), channel_id=1, source_target_pairs={{0,8},{4,12},{8,0},{12,4},{16,24},{20,28},{24,16},{28,20},{1,9},{5... | collective-permute-start | bytes 184328 | tf_op jit(solution)/shard_map/ppermute | solution.py:38
  30.0 2.3 %hold.5 = (bf16[768,3072]{1,0:T(8,128)(2,1)S(1)}, f32[8,128]{1,0:T(8,128)S(1)}) custom-call(f32[8,128]{1,0:T(8,128)S(1)} %get-tuple-element.62.refs_0_, bf16[768,3072]{1,0:T(8,128)(2,1)} %refs_1_.5), custom_call_target="tpu_custom_call" | custom-call | bytes 4718592 | tf_op jit(solution)/shard_map/hold/pallas_call | solution.py:62
  34.1 1.5 %collective-permute-start.11 = (f32[88,384]{1,0:T(8,128)S(1)}, f32[88,384]{1,0:T(8,128)S(1)}, u32[]{:S(2)}, u32[]{:S(2)}) collective-permute-start(f32[88,384]{1,0:T(8,128)S(1)} %get-tuple-element.76), channel_id=1, source_target_pairs={{0,8},{4,12},{8,0},{12,4},{16,24},{20,28},{24,16},{28,20},{1,9},{5... | collective-permute-start | bytes 405512 | tf_op jit(solution)/shard_map/ppermute | solution.py:38
  35.7 1.5 %collective-permute-start.12 = (f32[88,384]{1,0:T(8,128)S(1)}, f32[88,384]{1,0:T(8,128)S(1)}, u32[]{:S(2)}, u32[]{:S(2)}) collective-permute-start(f32[88,384]{1,0:T(8,128)S(1)} %get-tuple-element.77), channel_id=1, source_target_pairs={{0,16},{4,20},{8,24},{12,28},{16,0},{20,4},{24,8},{28,12},{1,17},{... | collective-permute-start | bytes 405512 | tf_op jit(solution)/shard_map/ppermute | solution.py:38
  37.7 3.7 %hold.6 = (bf16[3072,1536]{1,0:T(8,128)(2,1)S(1)}, f32[8,128]{1,0:T(8,128)S(1)}) custom-call(f32[8,128]{1,0:T(8,128)S(1)} %get-tuple-element.73.refs_0_, bf16[3072,1536]{1,0:T(8,128)(2,1)} %refs_1_.6), custom_call_target="tpu_custom_call" | custom-call | bytes 9437184 | tf_op jit(solution)/shard_map/hold/pallas_call | solution.py:62
  41.4 2.3 %collective-permute-done.12.refs_2_ = f32[88,384]{1,0:T(8,128)S(1)} collective-permute-done((f32[88,384]{1,0:T(8,128)S(1)}, f32[88,384]{1,0:T(8,128)S(1)}, u32[]{:S(2)}, u32[]{:S(2)}) %collective-permute-start.12) | collective-permute-done | bytes 135200 | tf_op jit(solution)/shard_map/ppermute | solution.py:38
  46.4 1.6 %collective-permute-start.15 = (bf16[16,3072]{1,0:T(8,128)(2,1)S(1)}, bf16[16,3072]{1,0:T(8,128)(2,1)S(1)}, u32[]{:S(2)}, u32[]{:S(2)}) collective-permute-start(bf16[16,3072]{1,0:T(8,128)(2,1)S(1)} %get-tuple-element.88), channel_id=1, source_target_pairs={{0,1},{1,0},{2,3},{3,2},{4,5},{5,4},{6,7},{7,6},{8,9},{9,8},{10,11... | collective-permute-start | bytes 294920 | tf_op jit(solution)/shard_map/ppermute | solution.py:38
  48.5 2.4 %collective-permute-start.17 = (bf16[16,3072]{1,0:T(8,128)(2,1)S(1)}, bf16[16,3072]{1,0:T(8,128)(2,1)S(1)}, u32[]{:S(2)}, u32[]{:S(2)}) collective-permute-start(bf16[16,3072]{1,0:T(8,128)(2,1)S(1)} %get-tuple-element.90), channel_id=1, source_target_pairs={{0,3},{1,2},{2,1},{3,0},{4,7},{5,6},{6,5},{7,4},{8,11},{9,10},{10,... | collective-permute-start | bytes 294920 | tf_op jit(solution)/shard_map/ppermute | solution.py:38
  50.9 3.7 %hold.7 = (bf16[1536,3072]{1,0:T(8,128)(2,1)S(1)}, bf16[64,3072]{1,0:T(8,128)(2,1)S(1)}, f32[8,128]{1,0:T(8,128)S(1)}) custom-call(f32[8,128]{1,0:T(8,128)S(1)} %get-tuple-element.82.refs_0_, bf16[1536,3072]{1,0:T(8,128)(2,1)} %refs_1_.7, bf16[64,3072]{1,0:T(8,128)(2,1)} %refs_2_.1), custom_call_target="tpu_custom_call" | custom-call | bytes 9830400 | tf_op jit(solution)/shard_map/hold/pallas_call | solution.py:62
  54.6 3.9 %collective-permute-done.16.refs_2_ = bf16[16,3072]{1,0:T(8,128)(2,1)S(1)} collective-permute-done((bf16[16,3072]{1,0:T(8,128)(2,1)S(1)}, bf16[16,3072]{1,0:T(8,128)(2,1)S(1)}, u32[]{:S(2)}, u32[]{:S(2)}) %collective-permute-start.16) | collective-permute-done | bytes 98336 | tf_op jit(solution)/shard_map/ppermute | solution.py:38
  62.3 2.1 %collective-permute-done.20.refs_3_ = bf16[16,3072]{1,0:T(8,128)(2,1)S(1)} collective-permute-done((bf16[16,3072]{1,0:T(8,128)(2,1)S(1)}, bf16[16,3072]{1,0:T(8,128)(2,1)S(1)}, u32[]{:S(2)}, u32[]{:S(2)}) %collective-permute-start.20) | collective-permute-done | bytes 98336 | tf_op jit(solution)/shard_map/ppermute | solution.py:38
  65.6 1.7 %collective-permute-done.21.refs_1_ = bf16[4,16,3072]{2,1,0:T(8,128)(2,1)S(1)} collective-permute-done((bf16[4,16,3072]{2,1,0:T(8,128)(2,1)S(1)}, bf16[4,16,3072]{2,1,0:T(8,128)(2,1)S(1)}, u32[]{:S(2)}, u32[]{:S(2)}) %collective-permute-start.21) | collective-permute-done | bytes 393248 | tf_op jit(solution)/shard_map/ppermute | solution.py:38
  67.3 2.7 %mlp.1 = (f32[64,3072]{1,0:T(8,128)S(1)}, bf16[64,3072]{1,0:T(8,128)(2,1)S(1)}) custom-call(bf16[4,16,3072]{2,1,0:T(8,128)(2,1)S(1)} %join.3.refs_0_, bf16[4,16,3072]{2,1,0:T(8,128)(2,1)S(1)} %collective-permute-done.21.refs_1_, bf16[3072,1536]{1,0:T(8,128)(2,1)S(1)} %get-tuple-element.93.refs_2_, bf16[1536,3072]{1,0:T(8,128)(2,1)S(1)} %get-tuple-element.94.refs_3_), custom_call_target="tpu_custom_call" | custom-call | tf_op jit(solution)/shard_map/mlp/pallas_call | solution.py:469
  70.3 1.6 %collective-permute-done.22.refs_1_ = bf16[64,3072]{1,0:T(8,128)(2,1)S(1)} collective-permute-done((bf16[64,3072]{1,0:T(8,128)(2,1)S(1)}, bf16[64,3072]{1,0:T(8,128)(2,1)S(1)}, u32[]{:S(2)}, u32[]{:S(2)}) %collective-permute-start.22) | collective-permute-done | bytes 393248 | tf_op jit(solution)/shard_map/ppermute | solution.py:38
  76.8 3.3 %collective-permute-done.24.refs_2_ = bf16[16,3072]{1,0:T(8,128)(2,1)S(1)} collective-permute-done((bf16[16,3072]{1,0:T(8,128)(2,1)S(1)}, bf16[16,3072]{1,0:T(8,128)(2,1)S(1)}, u32[]{:S(2)}, u32[]{:S(2)}) %collective-permute-start.24) | collective-permute-done | bytes 98336 | tf_op jit(solution)/shard_map/ppermute | solution.py:38
  (47 shorter events, 22.4 us)
Async XLA Ops:
  2.0 8.1 %collective-permute-start = (bf16[4,64,768]{2,1,0:T(8,128)(2,1)S(1)}, bf16[4,64,768]{2,1,0:T(8,128)(2,1)S(1)}, u32[]{:S(2)}, u32[]{:S(2)}) collective-permute-start(bf16[4,64,768]{2,1,0:T(8,128)(2,1)S(1)} %get-tuple-element.55), channel_id=1, source_target_pairs={{0,4},{4,0},{8,12},{12,8},{16,20},{20,16},{24,28},{28,24},{1,5},{5... | collective-permute-start | bytes 1179656 | tf_op jit(solution)/shard_map/ppermute | solution.py:38
  2.6 9.4 %collective-permute-start.2 = (bf16[16,3200]{1,0:T(8,128)(2,1)S(1)}, bf16[16,3200]{1,0:T(8,128)(2,1)S(1)}, u32[]{:S(2)}, u32[]{:S(2)}) collective-permute-start(bf16[16,3200]{1,0:T(8,128)(2,1)S(1)} %get-tuple-element.56.refs_0_), channel_id=1, source_target_pairs={{0,2},{1,3},{2,0},{3,1},{4,6},{5,7},{6,4},{7,5},{8,10},{9,11},{10,... | collective-permute-start | bytes 307208 | tf_op jit(solution)/shard_map/ppermute | solution.py:38
  6.2 9.9 %collective-permute-start.1 = (bf16[16,3200]{1,0:T(8,128)(2,1)S(1)}, bf16[16,3200]{1,0:T(8,128)(2,1)S(1)}, u32[]{:S(2)}, u32[]{:S(2)}) collective-permute-start(bf16[16,3200]{1,0:T(8,128)(2,1)S(1)} %get-tuple-element.56.refs_0_), channel_id=1, source_target_pairs={{0,1},{1,0},{2,3},{3,2},{4,5},{5,4},{6,7},{7,6},{8,9},{9,8},{10,11... | collective-permute-start | bytes 307208 | tf_op jit(solution)/shard_map/ppermute | solution.py:38
  12.0 4.7 %collective-permute-start.3 = (bf16[16,3200]{1,0:T(8,128)(2,1)S(1)}, bf16[16,3200]{1,0:T(8,128)(2,1)S(1)}, u32[]{:S(2)}, u32[]{:S(2)}) collective-permute-start(bf16[16,3200]{1,0:T(8,128)(2,1)S(1)} %relay.1.refs_3_.refs_2_), channel_id=1, source_target_pairs={{0,1},{1,0},{2,3},{3,2},{4,5},{5,4},{6,7},{7,6},{8,9},{9,8},{10,11... | collective-permute-start | bytes 307208 | tf_op jit(solution)/shard_map/ppermute | solution.py:38
  12.7 19.7 %collective-permute-start.8 = (bf16[2,64,768]{2,1,0:T(8,128)(2,1)S(1)}, bf16[2,64,768]{2,1,0:T(8,128)(2,1)S(1)}, u32[]{:S(2)}, u32[]{:S(2)}) collective-permute-start(bf16[2,64,768]{2,1,0:T(8,128)(2,1)S(1)} %get-tuple-element.66), channel_id=1, source_target_pairs={{0,2},{1,3},{2,0},{3,1},{4,6},{5,7},{6,4},{7,5},{8,10},{9,11},{10,... | collective-permute-start | bytes 589832 | tf_op jit(solution)/shard_map/ppermute | solution.py:38
  16.8 16.6 %collective-permute-start.9 = (bf16[2,64,768]{2,1,0:T(8,128)(2,1)S(1)}, bf16[2,64,768]{2,1,0:T(8,128)(2,1)S(1)}, u32[]{:S(2)}, u32[]{:S(2)}) collective-permute-start(bf16[2,64,768]{2,1,0:T(8,128)(2,1)S(1)} %get-tuple-element.71), channel_id=1, source_target_pairs={{0,3},{1,2},{2,1},{3,0},{4,7},{5,6},{6,5},{7,4},{8,11},{9,10},{10,... | collective-permute-start | bytes 589832 | tf_op jit(solution)/shard_map/ppermute | solution.py:38
  21.6 11.8 %collective-permute-start.10 = (bf16[2,64,768]{2,1,0:T(8,128)(2,1)S(1)}, bf16[2,64,768]{2,1,0:T(8,128)(2,1)S(1)}, u32[]{:S(2)}, u32[]{:S(2)}) collective-permute-start(bf16[2,64,768]{2,1,0:T(8,128)(2,1)S(1)} %get-tuple-element.72), channel_id=1, source_target_pairs={{0,1},{1,0},{2,3},{3,2},{4,5},{5,4},{6,7},{7,6},{8,9},{9,8},{10,11... | collective-permute-start | bytes 589832 | tf_op jit(solution)/shard_map/ppermute | solution.py:38
  24.3 4.2 %collective-permute-start.6 = (bf16[2,40,384]{2,1,0:T(8,128)(2,1)S(1)}, bf16[2,40,384]{2,1,0:T(8,128)(2,1)S(1)}, u32[]{:S(2)}, u32[]{:S(2)}) collective-permute-start(bf16[2,40,384]{2,1,0:T(8,128)(2,1)S(1)} %join.2.refs_0_), channel_id=1, source_target_pairs={{0,16},{4,20},{8,24},{12,28},{16,0},{20,4},{24,8},{28,12},{1,17},{... | collective-permute-start | bytes 184328 | tf_op jit(solution)/shard_map/ppermute | solution.py:38
  25.8 6.5 %collective-permute-start.5 = (bf16[2,40,384]{2,1,0:T(8,128)(2,1)S(1)}, bf16[2,40,384]{2,1,0:T(8,128)(2,1)S(1)}, u32[]{:S(2)}, u32[]{:S(2)}) collective-permute-start(bf16[2,40,384]{2,1,0:T(8,128)(2,1)S(1)} %join.2.refs_0_), channel_id=1, source_target_pairs={{0,8},{4,12},{8,0},{12,4},{16,24},{20,28},{24,16},{28,20},{1,9},{5... | collective-permute-start | bytes 184328 | tf_op jit(solution)/shard_map/ppermute | solution.py:38
  28.5 4.2 %collective-permute-start.7 = (bf16[2,40,384]{2,1,0:T(8,128)(2,1)S(1)}, bf16[2,40,384]{2,1,0:T(8,128)(2,1)S(1)}, u32[]{:S(2)}, u32[]{:S(2)}) collective-permute-start(bf16[2,40,384]{2,1,0:T(8,128)(2,1)S(1)} %collective-permute-done.6.refs_2_), channel_id=1, source_target_pairs={{0,8},{4,12},{8,0},{12,4},{16,24},{20,28},{24,16},{28,20},{1,9},{5... | collective-permute-start | bytes 184328 | tf_op jit(solution)/shard_map/ppermute | solution.py:38
  34.1 7.2 %collective-permute-start.11 = (f32[88,384]{1,0:T(8,128)S(1)}, f32[88,384]{1,0:T(8,128)S(1)}, u32[]{:S(2)}, u32[]{:S(2)}) collective-permute-start(f32[88,384]{1,0:T(8,128)S(1)} %get-tuple-element.76), channel_id=1, source_target_pairs={{0,8},{4,12},{8,0},{12,4},{16,24},{20,28},{24,16},{28,20},{1,9},{5... | collective-permute-start | bytes 405512 | tf_op jit(solution)/shard_map/ppermute | solution.py:38
  35.7 7.9 %collective-permute-start.12 = (f32[88,384]{1,0:T(8,128)S(1)}, f32[88,384]{1,0:T(8,128)S(1)}, u32[]{:S(2)}, u32[]{:S(2)}) collective-permute-start(f32[88,384]{1,0:T(8,128)S(1)} %get-tuple-element.77), channel_id=1, source_target_pairs={{0,16},{4,20},{8,24},{12,28},{16,0},{20,4},{24,8},{28,12},{1,17},{... | collective-permute-start | bytes 405512 | tf_op jit(solution)/shard_map/ppermute | solution.py:38
  37.2 6.4 %collective-permute-start.13 = (f32[88,384]{1,0:T(8,128)S(1)}, f32[88,384]{1,0:T(8,128)S(1)}, u32[]{:S(2)}, u32[]{:S(2)}) collective-permute-start(f32[88,384]{1,0:T(8,128)S(1)} %get-tuple-element.78), channel_id=1, source_target_pairs={{0,24},{4,28},{8,16},{12,20},{16,8},{20,12},{24,0},{28,4},{1,25},{... | collective-permute-start | bytes 405512 | tf_op jit(solution)/shard_map/ppermute | solution.py:38
  46.4 8.2 %collective-permute-start.15 = (bf16[16,3072]{1,0:T(8,128)(2,1)S(1)}, bf16[16,3072]{1,0:T(8,128)(2,1)S(1)}, u32[]{:S(2)}, u32[]{:S(2)}) collective-permute-start(bf16[16,3072]{1,0:T(8,128)(2,1)S(1)} %get-tuple-element.88), channel_id=1, source_target_pairs={{0,1},{1,0},{2,3},{3,2},{4,5},{5,4},{6,7},{7,6},{8,9},{9,8},{10,11... | collective-permute-start | bytes 294920 | tf_op jit(solution)/shard_map/ppermute | solution.py:38
  48.0 10.4 %collective-permute-start.16 = (bf16[16,3072]{1,0:T(8,128)(2,1)S(1)}, bf16[16,3072]{1,0:T(8,128)(2,1)S(1)}, u32[]{:S(2)}, u32[]{:S(2)}) collective-permute-start(bf16[16,3072]{1,0:T(8,128)(2,1)S(1)} %get-tuple-element.89), channel_id=1, source_target_pairs={{0,2},{1,3},{2,0},{3,1},{4,6},{5,7},{6,4},{7,5},{8,10},{9,11},{10,... | collective-permute-start | bytes 294920 | tf_op jit(solution)/shard_map/ppermute | solution.py:38
  48.5 10.0 %collective-permute-start.17 = (bf16[16,3072]{1,0:T(8,128)(2,1)S(1)}, bf16[16,3072]{1,0:T(8,128)(2,1)S(1)}, u32[]{:S(2)}, u32[]{:S(2)}) collective-permute-start(bf16[16,3072]{1,0:T(8,128)(2,1)S(1)} %get-tuple-element.90), channel_id=1, source_target_pairs={{0,3},{1,2},{2,1},{3,0},{4,7},{5,6},{6,5},{7,4},{8,11},{9,10},{10,... | collective-permute-start | bytes 294920 | tf_op jit(solution)/shard_map/ppermute | solution.py:38
  58.8 5.7 %collective-permute-start.20 = (bf16[16,3072]{1,0:T(8,128)(2,1)S(1)}, bf16[16,3072]{1,0:T(8,128)(2,1)S(1)}, u32[]{:S(2)}, u32[]{:S(2)}) collective-permute-start(bf16[16,3072]{1,0:T(8,128)(2,1)S(1)} %get-tuple-element.92.refs_0_), channel_id=1, source_target_pairs={{0,24},{4,28},{8,16},{12,20},{16,8},{20,12},{24,0},{28,4},{1,25},{... | collective-permute-start | bytes 294920 | tf_op jit(solution)/shard_map/ppermute | solution.py:38
  59.7 5.7 %collective-permute-start.19 = (bf16[16,3072]{1,0:T(8,128)(2,1)S(1)}, bf16[16,3072]{1,0:T(8,128)(2,1)S(1)}, u32[]{:S(2)}, u32[]{:S(2)}) collective-permute-start(bf16[16,3072]{1,0:T(8,128)(2,1)S(1)} %get-tuple-element.92.refs_0_), channel_id=1, source_target_pairs={{0,16},{4,20},{8,24},{12,28},{16,0},{20,4},{24,8},{28,12},{1,17},{... | collective-permute-start | bytes 294920 | tf_op jit(solution)/shard_map/ppermute | solution.py:38
  60.9 4.6 %collective-permute-start.18 = (bf16[16,3072]{1,0:T(8,128)(2,1)S(1)}, bf16[16,3072]{1,0:T(8,128)(2,1)S(1)}, u32[]{:S(2)}, u32[]{:S(2)}) collective-permute-start(bf16[16,3072]{1,0:T(8,128)(2,1)S(1)} %get-tuple-element.92.refs_0_), channel_id=1, source_target_pairs={{0,8},{4,12},{8,0},{12,4},{16,24},{20,28},{24,16},{28,20},{1,9},{5... | collective-permute-start | bytes 294920 | tf_op jit(solution)/shard_map/ppermute | solution.py:38
  65.6 1.8 %collective-permute-start.21 = (bf16[4,16,3072]{2,1,0:T(8,128)(2,1)S(1)}, bf16[4,16,3072]{2,1,0:T(8,128)(2,1)S(1)}, u32[]{:S(2)}, u32[]{:S(2)}) collective-permute-start(bf16[4,16,3072]{2,1,0:T(8,128)(2,1)S(1)} %join.3.refs_0_), channel_id=1, source_target_pairs={{0,4},{4,0},{8,12},{12,8},{16,20},{20,16},{24,28},{28,24},{1,5},{5... | collective-permute-start | bytes 1179656 | tf_op jit(solution)/shard_map/ppermute | solution.py:38
  70.1 1.8 %collective-permute-start.22 = (bf16[64,3072]{1,0:T(8,128)(2,1)S(1)}, bf16[64,3072]{1,0:T(8,128)(2,1)S(1)}, u32[]{:S(2)}, u32[]{:S(2)}) collective-permute-start(bf16[64,3072]{1,0:T(8,128)(2,1)S(1)} %get-tuple-element.96), channel_id=1, source_target_pairs={{0,4},{4,0},{8,12},{12,8},{16,20},{20,16},{24,28},{28,24},{1,5},{5... | collective-permute-start | bytes 1179656 | tf_op jit(solution)/shard_map/ppermute | solution.py:38
  71.9 4.9 %collective-permute-start.23 = (bf16[16,3072]{1,0:T(8,128)(2,1)S(1)}, bf16[16,3072]{1,0:T(8,128)(2,1)S(1)}, u32[]{:S(2)}, u32[]{:S(2)}) collective-permute-start(bf16[16,3072]{1,0:T(8,128)(2,1)S(1)} %get-tuple-element.98), channel_id=1, source_target_pairs={{0,8},{4,12},{8,0},{12,4},{16,24},{20,28},{24,16},{28,20},{1,9},{5... | collective-permute-start | bytes 294920 | tf_op jit(solution)/shard_map/ppermute | solution.py:38
  73.4 6.7 %collective-permute-start.24 = (bf16[16,3072]{1,0:T(8,128)(2,1)S(1)}, bf16[16,3072]{1,0:T(8,128)(2,1)S(1)}, u32[]{:S(2)}, u32[]{:S(2)}) collective-permute-start(bf16[16,3072]{1,0:T(8,128)(2,1)S(1)} %get-tuple-element.99), channel_id=1, source_target_pairs={{0,16},{4,20},{8,24},{12,28},{16,0},{20,4},{24,8},{28,12},{1,17},{... | collective-permute-start | bytes 294920 | tf_op jit(solution)/shard_map/ppermute | solution.py:38
  74.4 5.7 %collective-permute-start.25 = (bf16[16,3072]{1,0:T(8,128)(2,1)S(1)}, bf16[16,3072]{1,0:T(8,128)(2,1)S(1)}, u32[]{:S(2)}, u32[]{:S(2)}) collective-permute-start(bf16[16,3072]{1,0:T(8,128)(2,1)S(1)} %get-tuple-element.100), channel_id=1, source_target_pairs={{0,24},{4,28},{8,16},{12,20},{16,8},{20,12},{24,0},{28,4},{1,25},{... | collective-permute-start | bytes 294920 | tf_op jit(solution)/shard_map/ppermute | solution.py:38
  (2 other events, 2.5 us)

commit v3 on v2

--- a/solution.py
+++ b/solution.py
@@ -13,6 +13,10 @@
 VMEM_SPEC = pl.BlockSpec(memory_space=pltpu.VMEM)
 TOKEN = pltpu.VMEM((8, DH), jnp.float32)
 ANY_SPEC = pl.BlockSpec(memory_space=pl.ANY)
+
+
+def far_first(parts):
+    return parts[:1] + parts[:0:-1]
 
 
 def double(x, axis, scale, count, on_arrival=()):
@@ -372,22 +376,25 @@
     )(after, *first, *queries, *kv_parts)
 
 
+def column(stats, at):
+    lane = lax.broadcasted_iota(jnp.int32, stats.shape, 1)
+    return along_lanes(jnp.sum(jnp.where(lane == at, stats, 0.0), axis=-1, keepdims=True))
+
+
 def combine_kernel(pieces, after_ref, *refs):
     part_refs, out_refs = refs[:pieces], refs[pieces:]
     group, half = out_refs[0].shape
     rows = group * len(out_refs)
-    stats = []
-    for ref in part_refs:
-        stats.append(rows_of(ref[rows:, :DH], rows))
+    stats = [rows_of(ref[rows:, :DH], rows) for ref in part_refs]
     for head in range(half // DH):
         cols = slice(head * DH, (head + 1) * DH)
-        maxima = [stat[:, 2 * head : 2 * head + 1] for stat in stats]
+        maxima = [column(stat, 2 * head) for stat in stats]
         top = functools.reduce(jnp.maximum, maxima)
         total = jnp.zeros_like(top)
         attended = jnp.zeros((rows, DH), jnp.float32)
         for ref, stat, maximum in zip(part_refs, stats, maxima):
             factor = jnp.exp(maximum - top)
-            total = total + stat[:, 2 * head + 1 : 2 * head + 2] * factor
+            total = total + column(stat, 2 * head + 1) * factor
             attended = attended + ref[:rows, cols] * factor
         attended = attended / total
         for side, out_ref in enumerate(out_refs):
@@ -600,12 +607,12 @@
     first = attend_first(queries, kv_parts[:2])
     *parts, token = attend_last(token, first, queries, kv_parts[2:])
     w_up, token = hold(token, w_up)
-    parts = [trade(x, "blk", j * pair) for j, x in enumerate(parts)]
+    parts = far_first([trade(x, "blk", j * pair) for j, x in enumerate(parts)])
     attended = combine(token, parts, group, pair)
     attended = [trade(x, "blk", side) for side, x in enumerate(attended)]
     *terms, token = output(spread, attended, w_out, slots, uly_size)
     w_down, cached, token = hold(token, w_down, cached_out)
-    terms = [trade(x, "uly", k) for k, x in enumerate(terms)]
+    terms = far_first([trade(x, "uly", k) for k, x in enumerate(terms)])
     after_attn, norm_mlp = renorm(token, rows_in, modulation, terms)
 
     rows = [join([trade(norm_mlp, "blk", j * pair) for j in range(chips)])]
@@ -613,7 +620,7 @@
         rows.append(trade(rows[0], "blk", 1))
     down = mlp(rows, w_up, w_down, pair)
     down = [trade(x, "blk", side) for side, x in enumerate(down)]
-    terms = [trade(x, "blk", j * pair) for j, x in enumerate(fold(down, slots))]
+    terms = far_first([trade(x, "blk", j * pair) for j, x in enumerate(fold(down, slots))])
     return finish(select, cached, after_attn, modulation, terms)
 
 

time: 81.4 us -> 81 us (level)
  transfers between devices with their start and end apart: 26 -> 26, of which waited for: 15 -> 16; matrix products, arithmetic and copies ran while one was open for 0% -> 0% of each run, Pallas kernels for 17% -> 18%
where the time goes in v3:
time: 81 us; the launch traced here: 80.8 us
  starting transfers between devices  34.7 us (43%)
  waiting for transfers between devices  23.4 us (29%)
  Pallas kernels  22.5 us (28%)
    ppermute x26, starting transfers between devices, trade(): lax.ppermute(x, axis, [(i, i ^ flip) for i in range(lax.axis_size(axis))])  34.7 us
    ppermute x26, waiting for transfers between devices, trade(): lax.ppermute(x, axis, [(i, i ^ flip) for i in range(lax.axis_size(axis))])  23.4 us
    pallas_call x4, Pallas kernels, hold(): pl.pallas_call(functools.partial(hold_kernel, count), in_specs=[VMEM_SPEC...  12.1 us
    pallas_call x1, Pallas kernels, mlp(): pl.pallas_call(functools.partial(mlp_kernel, len(rows)), out_shape=[jax.S...  2.7 us
    pallas_call x1, Pallas kernels, enter(): pl.pallas_call(functools.partial(enter_kernel, pair), in_specs=[ANY_SPEC]...  2.02 us
  transfers between devices with their start and end apart: 26, of which 16 were waited for; matrix products, arithmetic and copies ran while one was open for 0% of the time, Pallas kernels for 18%

profile of v3, /device:TPU:0, one launch (start us, length us, event | category | flops | bytes accessed | tf_op | source)
XLA Modules:
  0.0 80.8 jit_solution(8995520332547710700)
XLA Ops:
  0.0 2.0 %enter.1 = (f32[16,3072]{1,0:T(8,128)S(1)}, bf16[16,3200]{1,0:T(8,128)(2,1)S(1)}, bf16[64,16]{1,0:T(8,128)(2,1)S(1)}, f32[6,3072]{1,0:T(8,128)S(1)}, bf16[4,64,7...) custom-call(s32[1,16]{1,0:T(1,128)} %bitcast.2, bf16[64,3072]{1,0:T(8,128)(2,1)} %hidden_hbm.1, f32[6,3072]{1,0:T(8,128)} %mod_hbm.1, ...), custom_call_target="tpu_custom_call" | custom-call | tf_op jit(solution)/shard_map/enter/pallas_call | solution.py:137
  2.6 3.7 %collective-permute-start.2 = (bf16[16,3200]{1,0:T(8,128)(2,1)S(1)}, bf16[16,3200]{1,0:T(8,128)(2,1)S(1)}, u32[]{:S(2)}, u32[]{:S(2)}) collective-permute-start(bf16[16,3200]{1,0:T(8,128)(2,1)S(1)} %get-tuple-element.56.refs_0_), channel_id=1, source_target_pairs={{0,2},{1,3},{2,0},{3,1},{4,6},{5,7},{6,4},{7,5},{8,10},{9,11},{10,... | collective-permute-start | bytes 307208 | tf_op jit(solution)/shard_map/ppermute | solution.py:42
  6.2 1.6 %collective-permute-start.1 = (bf16[16,3200]{1,0:T(8,128)(2,1)S(1)}, bf16[16,3200]{1,0:T(8,128)(2,1)S(1)}, u32[]{:S(2)}, u32[]{:S(2)}) collective-permute-start(bf16[16,3200]{1,0:T(8,128)(2,1)S(1)} %get-tuple-element.56.refs_0_), channel_id=1, source_target_pairs={{0,1},{1,0},{2,3},{3,2},{4,5},{5,4},{6,7},{7,6},{8,9},{9,8},{10,11... | collective-permute-start | bytes 307208 | tf_op jit(solution)/shard_map/ppermute | solution.py:42
  7.8 2.3 %hold.4 = (bf16[3072,768]{1,0:T(8,128)(2,1)S(1)}, f32[8,128]{1,0:T(8,128)S(1)}) custom-call(bf16[16,3200]{1,0:T(8,128)(2,1)S(1)} %get-tuple-element.56.refs_0_, bf16[3072,768]{1,0:T(8,128)(2,1)} %refs_1_.4), custom_call_target="tpu_custom_call" | custom-call | bytes 4718592 | tf_op jit(solution)/shard_map/hold/pallas_call | solution.py:66
  10.2 1.8 %collective-permute-done.2.x_ref = bf16[16,3200]{1,0:T(8,128)(2,1)S(1)} collective-permute-done((bf16[16,3200]{1,0:T(8,128)(2,1)S(1)}, bf16[16,3200]{1,0:T(8,128)(2,1)S(1)}, u32[]{:S(2)}, u32[]{:S(2)}) %collective-permute-start.2) | collective-permute-done | bytes 102432 | tf_op jit(solution)/shard_map/ppermute | solution.py:42
  12.7 3.4 %collective-permute-start.8 = (bf16[2,64,768]{2,1,0:T(8,128)(2,1)S(1)}, bf16[2,64,768]{2,1,0:T(8,128)(2,1)S(1)}, u32[]{:S(2)}, u32[]{:S(2)}) collective-permute-start(bf16[2,64,768]{2,1,0:T(8,128)(2,1)S(1)} %get-tuple-element.66), channel_id=1, source_target_pairs={{0,2},{1,3},{2,0},{3,1},{4,6},{5,7},{6,4},{7,5},{8,10},{9,11},{10,... | collective-permute-start | bytes 589832 | tf_op jit(solution)/shard_map/ppermute | solution.py:42
  16.8 4.9 %collective-permute-start.9 = (bf16[2,64,768]{2,1,0:T(8,128)(2,1)S(1)}, bf16[2,64,768]{2,1,0:T(8,128)(2,1)S(1)}, u32[]{:S(2)}, u32[]{:S(2)}) collective-permute-start(bf16[2,64,768]{2,1,0:T(8,128)(2,1)S(1)} %get-tuple-element.71), channel_id=1, source_target_pairs={{0,3},{1,2},{2,1},{3,0},{4,7},{5,6},{6,5},{7,4},{8,11},{9,10},{10,... | collective-permute-start | bytes 589832 | tf_op jit(solution)/shard_map/ppermute | solution.py:42
  24.3 1.5 %collective-permute-start.6 = (bf16[2,40,384]{2,1,0:T(8,128)(2,1)S(1)}, bf16[2,40,384]{2,1,0:T(8,128)(2,1)S(1)}, u32[]{:S(2)}, u32[]{:S(2)}) collective-permute-start(bf16[2,40,384]{2,1,0:T(8,128)(2,1)S(1)} %join.2.refs_0_), channel_id=1, source_target_pairs={{0,16},{4,20},{8,24},{12,28},{16,0},{20,4},{24,8},{28,12},{1,17},{... | collective-permute-start | bytes 184328 | tf_op jit(solution)/shard_map/ppermute | solution.py:42
  30.0 2.3 %hold.5 = (bf16[768,3072]{1,0:T(8,128)(2,1)S(1)}, f32[8,128]{1,0:T(8,128)S(1)}) custom-call(f32[8,128]{1,0:T(8,128)S(1)} %get-tuple-element.62.refs_0_, bf16[768,3072]{1,0:T(8,128)(2,1)} %refs_1_.5), custom_call_target="tpu_custom_call" | custom-call | bytes 4718592 | tf_op jit(solution)/shard_map/hold/pallas_call | solution.py:66
  34.1 2.5 %collective-permute-start.11 = (f32[88,384]{1,0:T(8,128)S(1)}, f32[88,384]{1,0:T(8,128)S(1)}, u32[]{:S(2)}, u32[]{:S(2)}) collective-permute-start(f32[88,384]{1,0:T(8,128)S(1)} %get-tuple-element.76), channel_id=1, source_target_pairs={{0,24},{4,28},{8,16},{12,20},{16,8},{20,12},{24,0},{28,4},{1,25},{... | collective-permute-start | bytes 405512 | tf_op jit(solution)/shard_map/ppermute | solution.py:42
  37.7 3.7 %hold.6 = (bf16[3072,1536]{1,0:T(8,128)(2,1)S(1)}, f32[8,128]{1,0:T(8,128)S(1)}) custom-call(f32[8,128]{1,0:T(8,128)S(1)} %get-tuple-element.73.refs_0_, bf16[3072,1536]{1,0:T(8,128)(2,1)} %refs_1_.6), custom_call_target="tpu_custom_call" | custom-call | bytes 9437184 | tf_op jit(solution)/shard_map/hold/pallas_call | solution.py:66
  41.4 1.9 %collective-permute-done.12.refs_2_ = f32[88,384]{1,0:T(8,128)S(1)} collective-permute-done((f32[88,384]{1,0:T(8,128)S(1)}, f32[88,384]{1,0:T(8,128)S(1)}, u32[]{:S(2)}, u32[]{:S(2)}) %collective-permute-start.12) | collective-permute-done | bytes 135200 | tf_op jit(solution)/shard_map/ppermute | solution.py:42
  46.8 1.8 %collective-permute-start.16 = (bf16[16,3072]{1,0:T(8,128)(2,1)S(1)}, bf16[16,3072]{1,0:T(8,128)(2,1)S(1)}, u32[]{:S(2)}, u32[]{:S(2)}) collective-permute-start(bf16[16,3072]{1,0:T(8,128)(2,1)S(1)} %get-tuple-element.89), channel_id=1, source_target_pairs={{0,2},{1,3},{2,0},{3,1},{4,6},{5,7},{6,4},{7,5},{8,10},{9,11},{10,... | collective-permute-start | bytes 294920 | tf_op jit(solution)/shard_map/ppermute | solution.py:42
  48.6 2.0 %collective-permute-start.17 = (bf16[16,3072]{1,0:T(8,128)(2,1)S(1)}, bf16[16,3072]{1,0:T(8,128)(2,1)S(1)}, u32[]{:S(2)}, u32[]{:S(2)}) collective-permute-start(bf16[16,3072]{1,0:T(8,128)(2,1)S(1)} %get-tuple-element.90), channel_id=1, source_target_pairs={{0,1},{1,0},{2,3},{3,2},{4,5},{5,4},{6,7},{7,6},{8,9},{9,8},{10,11... | collective-permute-start | bytes 294920 | tf_op jit(solution)/shard_map/ppermute | solution.py:42
  50.6 3.7 %hold.7 = (bf16[1536,3072]{1,0:T(8,128)(2,1)S(1)}, bf16[64,3072]{1,0:T(8,128)(2,1)S(1)}, f32[8,128]{1,0:T(8,128)S(1)}) custom-call(f32[8,128]{1,0:T(8,128)S(1)} %get-tuple-element.82.refs_0_, bf16[1536,3072]{1,0:T(8,128)(2,1)} %refs_1_.7, bf16[64,3072]{1,0:T(8,128)(2,1)} %refs_2_.1), custom_call_target="tpu_custom_call" | custom-call | bytes 9830400 | tf_op jit(solution)/shard_map/hold/pallas_call | solution.py:66
  54.3 3.5 %collective-permute-done.16.refs_2_ = bf16[16,3072]{1,0:T(8,128)(2,1)S(1)} collective-permute-done((bf16[16,3072]{1,0:T(8,128)(2,1)S(1)}, bf16[16,3072]{1,0:T(8,128)(2,1)S(1)}, u32[]{:S(2)}, u32[]{:S(2)}) %collective-permute-start.16) | collective-permute-done | bytes 98336 | tf_op jit(solution)/shard_map/ppermute | solution.py:42
  58.1 1.7 %collective-permute-start.20 = (bf16[16,3072]{1,0:T(8,128)(2,1)S(1)}, bf16[16,3072]{1,0:T(8,128)(2,1)S(1)}, u32[]{:S(2)}, u32[]{:S(2)}) collective-permute-start(bf16[16,3072]{1,0:T(8,128)(2,1)S(1)} %get-tuple-element.92.refs_0_), channel_id=1, source_target_pairs={{0,24},{4,28},{8,16},{12,20},{16,8},{20,12},{24,0},{28,4},{1,25},{... | collective-permute-start | bytes 294920 | tf_op jit(solution)/shard_map/ppermute | solution.py:42
  61.6 3.1 %collective-permute-done.20.refs_3_ = bf16[16,3072]{1,0:T(8,128)(2,1)S(1)} collective-permute-done((bf16[16,3072]{1,0:T(8,128)(2,1)S(1)}, bf16[16,3072]{1,0:T(8,128)(2,1)S(1)}, u32[]{:S(2)}, u32[]{:S(2)}) %collective-permute-start.20) | collective-permute-done | bytes 98336 | tf_op jit(solution)/shard_map/ppermute | solution.py:42
  65.6 1.7 %collective-permute-done.21.refs_1_ = bf16[4,16,3072]{2,1,0:T(8,128)(2,1)S(1)} collective-permute-done((bf16[4,16,3072]{2,1,0:T(8,128)(2,1)S(1)}, bf16[4,16,3072]{2,1,0:T(8,128)(2,1)S(1)}, u32[]{:S(2)}, u32[]{:S(2)}) %collective-permute-start.21) | collective-permute-done | bytes 393248 | tf_op jit(solution)/shard_map/ppermute | solution.py:42
  67.3 2.7 %mlp.1 = (f32[64,3072]{1,0:T(8,128)S(1)}, bf16[64,3072]{1,0:T(8,128)(2,1)S(1)}) custom-call(bf16[4,16,3072]{2,1,0:T(8,128)(2,1)S(1)} %join.3.refs_0_, bf16[4,16,3072]{2,1,0:T(8,128)(2,1)S(1)} %collective-permute-done.21.refs_1_, bf16[3072,1536]{1,0:T(8,128)(2,1)S(1)} %get-tuple-element.93.refs_2_, bf16[1536,3072]{1,0:T(8,128)(2,1)S(1)} %get-tuple-element.94.refs_3_), custom_call_target="tpu_custom_call" | custom-call | tf_op jit(solution)/shard_map/mlp/pallas_call | solution.py:476
  70.2 1.6 %collective-permute-done.22.refs_1_ = bf16[64,3072]{1,0:T(8,128)(2,1)S(1)} collective-permute-done((bf16[64,3072]{1,0:T(8,128)(2,1)S(1)}, bf16[64,3072]{1,0:T(8,128)(2,1)S(1)}, u32[]{:S(2)}, u32[]{:S(2)}) %collective-permute-start.22) | collective-permute-done | bytes 393248 | tf_op jit(solution)/shard_map/ppermute | solution.py:42
  71.8 1.6 %collective-permute-start.23 = (bf16[16,3072]{1,0:T(8,128)(2,1)S(1)}, bf16[16,3072]{1,0:T(8,128)(2,1)S(1)}, u32[]{:S(2)}, u32[]{:S(2)}) collective-permute-start(bf16[16,3072]{1,0:T(8,128)(2,1)S(1)} %get-tuple-element.98), channel_id=1, source_target_pairs={{0,24},{4,28},{8,16},{12,20},{16,8},{20,12},{24,0},{28,4},{1,25},{... | collective-permute-start | bytes 294920 | tf_op jit(solution)/shard_map/ppermute | solution.py:42
  75.4 2.8 %collective-permute-done.23.refs_1_ = bf16[16,3072]{1,0:T(8,128)(2,1)S(1)} collective-permute-done((bf16[16,3072]{1,0:T(8,128)(2,1)S(1)}, bf16[16,3072]{1,0:T(8,128)(2,1)S(1)}, u32[]{:S(2)}, u32[]{:S(2)}) %collective-permute-start.23) | collective-permute-done | bytes 98336 | tf_op jit(solution)/shard_map/ppermute | solution.py:42
  78.2 1.6 %collective-permute-done.24.refs_2_ = bf16[16,3072]{1,0:T(8,128)(2,1)S(1)} collective-permute-done((bf16[16,3072]{1,0:T(8,128)(2,1)S(1)}, bf16[16,3072]{1,0:T(8,128)(2,1)S(1)}, u32[]{:S(2)}, u32[]{:S(2)}) %collective-permute-start.24) | collective-permute-done | bytes 98336 | tf_op jit(solution)/shard_map/ppermute | solution.py:42
  (47 shorter events, 21.2 us)
Async XLA Ops:
  2.0 8.1 %collective-permute-start = (bf16[4,64,768]{2,1,0:T(8,128)(2,1)S(1)}, bf16[4,64,768]{2,1,0:T(8,128)(2,1)S(1)}, u32[]{:S(2)}, u32[]{:S(2)}) collective-permute-start(bf16[4,64,768]{2,1,0:T(8,128)(2,1)S(1)} %get-tuple-element.55), channel_id=1, source_target_pairs={{0,4},{4,0},{8,12},{12,8},{16,20},{20,16},{24,28},{28,24},{1,5},{5... | collective-permute-start | bytes 1179656 | tf_op jit(solution)/shard_map/ppermute | solution.py:42
  2.6 9.4 %collective-permute-start.2 = (bf16[16,3200]{1,0:T(8,128)(2,1)S(1)}, bf16[16,3200]{1,0:T(8,128)(2,1)S(1)}, u32[]{:S(2)}, u32[]{:S(2)}) collective-permute-start(bf16[16,3200]{1,0:T(8,128)(2,1)S(1)} %get-tuple-element.56.refs_0_), channel_id=1, source_target_pairs={{0,2},{1,3},{2,0},{3,1},{4,6},{5,7},{6,4},{7,5},{8,10},{9,11},{10,... | collective-permute-start | bytes 307208 | tf_op jit(solution)/shard_map/ppermute | solution.py:42
  6.2 9.9 %collective-permute-start.1 = (bf16[16,3200]{1,0:T(8,128)(2,1)S(1)}, bf16[16,3200]{1,0:T(8,128)(2,1)S(1)}, u32[]{:S(2)}, u32[]{:S(2)}) collective-permute-start(bf16[16,3200]{1,0:T(8,128)(2,1)S(1)} %get-tuple-element.56.refs_0_), channel_id=1, source_target_pairs={{0,1},{1,0},{2,3},{3,2},{4,5},{5,4},{6,7},{7,6},{8,9},{9,8},{10,11... | collective-permute-start | bytes 307208 | tf_op jit(solution)/shard_map/ppermute | solution.py:42
  12.0 4.7 %collective-permute-start.3 = (bf16[16,3200]{1,0:T(8,128)(2,1)S(1)}, bf16[16,3200]{1,0:T(8,128)(2,1)S(1)}, u32[]{:S(2)}, u32[]{:S(2)}) collective-permute-start(bf16[16,3200]{1,0:T(8,128)(2,1)S(1)} %relay.1.refs_3_.refs_2_), channel_id=1, source_target_pairs={{0,1},{1,0},{2,3},{3,2},{4,5},{5,4},{6,7},{7,6},{8,9},{9,8},{10,11... | collective-permute-start | bytes 307208 | tf_op jit(solution)/shard_map/ppermute | solution.py:42
  12.7 19.7 %collective-permute-start.8 = (bf16[2,64,768]{2,1,0:T(8,128)(2,1)S(1)}, bf16[2,64,768]{2,1,0:T(8,128)(2,1)S(1)}, u32[]{:S(2)}, u32[]{:S(2)}) collective-permute-start(bf16[2,64,768]{2,1,0:T(8,128)(2,1)S(1)} %get-tuple-element.66), channel_id=1, source_target_pairs={{0,2},{1,3},{2,0},{3,1},{4,6},{5,7},{6,4},{7,5},{8,10},{9,11},{10,... | collective-permute-start | bytes 589832 | tf_op jit(solution)/shard_map/ppermute | solution.py:42
  16.8 16.6 %collective-permute-start.9 = (bf16[2,64,768]{2,1,0:T(8,128)(2,1)S(1)}, bf16[2,64,768]{2,1,0:T(8,128)(2,1)S(1)}, u32[]{:S(2)}, u32[]{:S(2)}) collective-permute-start(bf16[2,64,768]{2,1,0:T(8,128)(2,1)S(1)} %get-tuple-element.71), channel_id=1, source_target_pairs={{0,3},{1,2},{2,1},{3,0},{4,7},{5,6},{6,5},{7,4},{8,11},{9,10},{10,... | collective-permute-start | bytes 589832 | tf_op jit(solution)/shard_map/ppermute | solution.py:42
  21.6 11.8 %collective-permute-start.10 = (bf16[2,64,768]{2,1,0:T(8,128)(2,1)S(1)}, bf16[2,64,768]{2,1,0:T(8,128)(2,1)S(1)}, u32[]{:S(2)}, u32[]{:S(2)}) collective-permute-start(bf16[2,64,768]{2,1,0:T(8,128)(2,1)S(1)} %get-tuple-element.72), channel_id=1, source_target_pairs={{0,1},{1,0},{2,3},{3,2},{4,5},{5,4},{6,7},{7,6},{8,9},{9,8},{10,11... | collective-permute-start | bytes 589832 | tf_op jit(solution)/shard_map/ppermute | solution.py:42
  24.3 4.2 %collective-permute-start.6 = (bf16[2,40,384]{2,1,0:T(8,128)(2,1)S(1)}, bf16[2,40,384]{2,1,0:T(8,128)(2,1)S(1)}, u32[]{:S(2)}, u32[]{:S(2)}) collective-permute-start(bf16[2,40,384]{2,1,0:T(8,128)(2,1)S(1)} %join.2.refs_0_), channel_id=1, source_target_pairs={{0,16},{4,20},{8,24},{12,28},{16,0},{20,4},{24,8},{28,12},{1,17},{... | collective-permute-start | bytes 184328 | tf_op jit(solution)/shard_map/ppermute | solution.py:42
  25.8 6.5 %collective-permute-start.5 = (bf16[2,40,384]{2,1,0:T(8,128)(2,1)S(1)}, bf16[2,40,384]{2,1,0:T(8,128)(2,1)S(1)}, u32[]{:S(2)}, u32[]{:S(2)}) collective-permute-start(bf16[2,40,384]{2,1,0:T(8,128)(2,1)S(1)} %join.2.refs_0_), channel_id=1, source_target_pairs={{0,8},{4,12},{8,0},{12,4},{16,24},{20,28},{24,16},{28,20},{1,9},{5... | collective-permute-start | bytes 184328 | tf_op jit(solution)/shard_map/ppermute | solution.py:42
  28.5 4.2 %collective-permute-start.7 = (bf16[2,40,384]{2,1,0:T(8,128)(2,1)S(1)}, bf16[2,40,384]{2,1,0:T(8,128)(2,1)S(1)}, u32[]{:S(2)}, u32[]{:S(2)}) collective-permute-start(bf16[2,40,384]{2,1,0:T(8,128)(2,1)S(1)} %collective-permute-done.6.refs_2_), channel_id=1, source_target_pairs={{0,8},{4,12},{8,0},{12,4},{16,24},{20,28},{24,16},{28,20},{1,9},{5... | collective-permute-start | bytes 184328 | tf_op jit(solution)/shard_map/ppermute | solution.py:42
  34.1 7.2 %collective-permute-start.11 = (f32[88,384]{1,0:T(8,128)S(1)}, f32[88,384]{1,0:T(8,128)S(1)}, u32[]{:S(2)}, u32[]{:S(2)}) collective-permute-start(f32[88,384]{1,0:T(8,128)S(1)} %get-tuple-element.76), channel_id=1, source_target_pairs={{0,24},{4,28},{8,16},{12,20},{16,8},{20,12},{24,0},{28,4},{1,25},{... | collective-permute-start | bytes 405512 | tf_op jit(solution)/shard_map/ppermute | solution.py:42
  36.6 6.7 %collective-permute-start.12 = (f32[88,384]{1,0:T(8,128)S(1)}, f32[88,384]{1,0:T(8,128)S(1)}, u32[]{:S(2)}, u32[]{:S(2)}) collective-permute-start(f32[88,384]{1,0:T(8,128)S(1)} %get-tuple-element.77), channel_id=1, source_target_pairs={{0,16},{4,20},{8,24},{12,28},{16,0},{20,4},{24,8},{28,12},{1,17},{... | collective-permute-start | bytes 405512 | tf_op jit(solution)/shard_map/ppermute | solution.py:42
  37.1 6.2 %collective-permute-start.13 = (f32[88,384]{1,0:T(8,128)S(1)}, f32[88,384]{1,0:T(8,128)S(1)}, u32[]{:S(2)}, u32[]{:S(2)}) collective-permute-start(f32[88,384]{1,0:T(8,128)S(1)} %get-tuple-element.78), channel_id=1, source_target_pairs={{0,8},{4,12},{8,0},{12,4},{16,24},{20,28},{24,16},{28,20},{1,9},{5... | collective-permute-start | bytes 405512 | tf_op jit(solution)/shard_map/ppermute | solution.py:42
  46.1 8.2 %collective-permute-start.15 = (bf16[16,3072]{1,0:T(8,128)(2,1)S(1)}, bf16[16,3072]{1,0:T(8,128)(2,1)S(1)}, u32[]{:S(2)}, u32[]{:S(2)}) collective-permute-start(bf16[16,3072]{1,0:T(8,128)(2,1)S(1)} %get-tuple-element.88), channel_id=1, source_target_pairs={{0,3},{1,2},{2,1},{3,0},{4,7},{5,6},{6,5},{7,4},{8,11},{9,10},{10,... | collective-permute-start | bytes 294920 | tf_op jit(solution)/shard_map/ppermute | solution.py:42
  46.8 10.9 %collective-permute-start.16 = (bf16[16,3072]{1,0:T(8,128)(2,1)S(1)}, bf16[16,3072]{1,0:T(8,128)(2,1)S(1)}, u32[]{:S(2)}, u32[]{:S(2)}) collective-permute-start(bf16[16,3072]{1,0:T(8,128)(2,1)S(1)} %get-tuple-element.89), channel_id=1, source_target_pairs={{0,2},{1,3},{2,0},{3,1},{4,6},{5,7},{6,4},{7,5},{8,10},{9,11},{10,... | collective-permute-start | bytes 294920 | tf_op jit(solution)/shard_map/ppermute | solution.py:42
  48.6 9.2 %collective-permute-start.17 = (bf16[16,3072]{1,0:T(8,128)(2,1)S(1)}, bf16[16,3072]{1,0:T(8,128)(2,1)S(1)}, u32[]{:S(2)}, u32[]{:S(2)}) collective-permute-start(bf16[16,3072]{1,0:T(8,128)(2,1)S(1)} %get-tuple-element.90), channel_id=1, source_target_pairs={{0,1},{1,0},{2,3},{3,2},{4,5},{5,4},{6,7},{7,6},{8,9},{9,8},{10,11... | collective-permute-start | bytes 294920 | tf_op jit(solution)/shard_map/ppermute | solution.py:42
  58.1 6.7 %collective-permute-start.20 = (bf16[16,3072]{1,0:T(8,128)(2,1)S(1)}, bf16[16,3072]{1,0:T(8,128)(2,1)S(1)}, u32[]{:S(2)}, u32[]{:S(2)}) collective-permute-start(bf16[16,3072]{1,0:T(8,128)(2,1)S(1)} %get-tuple-element.92.refs_0_), channel_id=1, source_target_pairs={{0,24},{4,28},{8,16},{12,20},{16,8},{20,12},{24,0},{28,4},{1,25},{... | collective-permute-start | bytes 294920 | tf_op jit(solution)/shard_map/ppermute | solution.py:42
  59.7 5.4 %collective-permute-start.19 = (bf16[16,3072]{1,0:T(8,128)(2,1)S(1)}, bf16[16,3072]{1,0:T(8,128)(2,1)S(1)}, u32[]{:S(2)}, u32[]{:S(2)}) collective-permute-start(bf16[16,3072]{1,0:T(8,128)(2,1)S(1)} %get-tuple-element.92.refs_0_), channel_id=1, source_target_pairs={{0,16},{4,20},{8,24},{12,28},{16,0},{20,4},{24,8},{28,12},{1,17},{... | collective-permute-start | bytes 294920 | tf_op jit(solution)/shard_map/ppermute | solution.py:42
  60.8 4.6 %collective-permute-start.18 = (bf16[16,3072]{1,0:T(8,128)(2,1)S(1)}, bf16[16,3072]{1,0:T(8,128)(2,1)S(1)}, u32[]{:S(2)}, u32[]{:S(2)}) collective-permute-start(bf16[16,3072]{1,0:T(8,128)(2,1)S(1)} %get-tuple-element.92.refs_0_), channel_id=1, source_target_pairs={{0,8},{4,12},{8,0},{12,4},{16,24},{20,28},{24,16},{28,20},{1,9},{5... | collective-permute-start | bytes 294920 | tf_op jit(solution)/shard_map/ppermute | solution.py:42
  65.5 1.8 %collective-permute-start.21 = (bf16[4,16,3072]{2,1,0:T(8,128)(2,1)S(1)}, bf16[4,16,3072]{2,1,0:T(8,128)(2,1)S(1)}, u32[]{:S(2)}, u32[]{:S(2)}) collective-permute-start(bf16[4,16,3072]{2,1,0:T(8,128)(2,1)S(1)} %join.3.refs_0_), channel_id=1, source_target_pairs={{0,4},{4,0},{8,12},{12,8},{16,20},{20,16},{24,28},{28,24},{1,5},{5... | collective-permute-start | bytes 1179656 | tf_op jit(solution)/shard_map/ppermute | solution.py:42
  70.0 1.8 %collective-permute-start.22 = (bf16[64,3072]{1,0:T(8,128)(2,1)S(1)}, bf16[64,3072]{1,0:T(8,128)(2,1)S(1)}, u32[]{:S(2)}, u32[]{:S(2)}) collective-permute-start(bf16[64,3072]{1,0:T(8,128)(2,1)S(1)} %get-tuple-element.96), channel_id=1, source_target_pairs={{0,4},{4,0},{8,12},{12,8},{16,20},{20,16},{24,28},{28,24},{1,5},{5... | collective-permute-start | bytes 1179656 | tf_op jit(solution)/shard_map/ppermute | solution.py:42
  71.8 6.4 %collective-permute-start.23 = (bf16[16,3072]{1,0:T(8,128)(2,1)S(1)}, bf16[16,3072]{1,0:T(8,128)(2,1)S(1)}, u32[]{:S(2)}, u32[]{:S(2)}) collective-permute-start(bf16[16,3072]{1,0:T(8,128)(2,1)S(1)} %get-tuple-element.98), channel_id=1, source_target_pairs={{0,24},{4,28},{8,16},{12,20},{16,8},{20,12},{24,0},{28,4},{1,25},{... | collective-permute-start | bytes 294920 | tf_op jit(solution)/shard_map/ppermute | solution.py:42
  73.5 6.3 %collective-permute-start.24 = (bf16[16,3072]{1,0:T(8,128)(2,1)S(1)}, bf16[16,3072]{1,0:T(8,128)(2,1)S(1)}, u32[]{:S(2)}, u32[]{:S(2)}) collective-permute-start(bf16[16,3072]{1,0:T(8,128)(2,1)S(1)} %get-tuple-element.99), channel_id=1, source_target_pairs={{0,16},{4,20},{8,24},{12,28},{16,0},{20,4},{24,8},{28,12},{1,17},{... | collective-permute-start | bytes 294920 | tf_op jit(solution)/shard_map/ppermute | solution.py:42
  74.3 5.4 %collective-permute-start.25 = (bf16[16,3072]{1,0:T(8,128)(2,1)S(1)}, bf16[16,3072]{1,0:T(8,128)(2,1)S(1)}, u32[]{:S(2)}, u32[]{:S(2)}) collective-permute-start(bf16[16,3072]{1,0:T(8,128)(2,1)S(1)} %get-tuple-element.100), channel_id=1, source_target_pairs={{0,8},{4,12},{8,0},{12,4},{16,24},{20,28},{24,16},{28,20},{1,9},{5... | collective-permute-start | bytes 294920 | tf_op jit(solution)/shard_map/ppermute | solution.py:42
  (2 other events, 2.5 us)

commit v4 on v3

--- a/solution.py
+++ b/solution.py
@@ -217,23 +217,21 @@
     spread = jnp.where((rank == lane) & (flags.astype(jnp.float32) > 0.0), 1.0, 0.0)
     spread = spread.astype(jnp.bfloat16)
     spread_ref[...] = spread
-    live_rows = lax.dot_general(
-        spread[:, :group],
-        rows[:, :width],
-        (((0,), (0,)), ((), ())),
-        preferred_element_type=jnp.float32,
-    ).astype(jnp.bfloat16)
-    projected = jnp.dot(live_rows, w_ref[...], preferred_element_type=jnp.float32)
+    projected = jnp.dot(rows[:, :width], w_ref[...], preferred_element_type=jnp.float32)
     copy.wait()
     for start in range(0, projected.shape[1], DH):
         head = projected[:, start : start + DH]
         squares = jnp.mean(head * head, axis=-1, keepdims=True)
-        heads_ref[:, start : start + DH] = (
-            head * lax.rsqrt(squares + 1e-06) * (gain_ref[...] / math.sqrt(DH))
-        )
+        head = head * lax.rsqrt(squares + 1e-06) * (gain_ref[...] / math.sqrt(DH))
+        heads_ref[:, start : start + DH] = head.astype(jnp.bfloat16)
     for side, query_ref in enumerate(query_refs):
         start = pl.multiple_of((core ^ side) * half, DH)
-        query_ref[...] = heads_ref[:, pl.ds(start, half)].astype(jnp.bfloat16)
+        query_ref[...] = lax.dot_general(
+            spread[:, :group],
+            heads_ref[:, pl.ds(start, half)],
+            (((0,), (0,)), ((), ())),
+            preferred_element_type=jnp.float32,
+        ).astype(jnp.bfloat16)
 
 
 def project(after, rows, w_query, q_gain, group, pair):
@@ -245,7 +243,7 @@
         in_specs=[VMEM_SPEC] * (len(rows) + 2) + [ANY_SPEC],
         out_shape=[query] * pair + [jax.ShapeDtypeStruct((everyone, DH), jnp.bfloat16), TOKEN],
         scratch_shapes=[
-            pltpu.VMEM((group, w_query.shape[1]), jnp.float32),
+            pltpu.VMEM((everyone, w_query.shape[1]), jnp.bfloat16),
             pltpu.VMEM((1, DH), jnp.float32),
             pltpu.SemaphoreType.DMA,
         ],
@@ -411,42 +409,66 @@
     )(after, *parts)
 
 
-def output_kernel(sides, spread_ref, *refs):
-    side_refs, w_ref, (*out_refs, token_ref) = refs[:sides], refs[sides], refs[sides + 1 :]
-    token_ref[...] = jnp.zeros_like(token_ref)
-    group, half = side_refs[0].shape
-    slots, width = out_refs[0].shape
-    spread = spread_ref[:, :group]
-    attended = [
-        jnp.dot(spread, ref[...], preferred_element_type=jnp.float32).astype(jnp.bfloat16)
-        for ref in side_refs
-    ]
-    core = my_core(sides)
-    starts = [pl.multiple_of((core ^ side) * half, DH) for side in range(sides)]
+def output_terms(side, pair, spread_ref, attended_ref, w_ref):
+    group, half = attended_ref.shape
+    width = w_ref.shape[1]
+    attended = jnp.dot(
+        spread_ref[:, :group], attended_ref[...], preferred_element_type=jnp.float32
+    ).astype(jnp.bfloat16)
+    start = pl.multiple_of((my_core(pair) ^ side) * half, DH)
     step = math.gcd(width, 1024)
     for col in range(0, width, step):
-        terms = jnp.zeros((spread.shape[0], step), jnp.float32)
-        for start, side in zip(starts, attended):
-            terms = terms + jnp.dot(
-                side, w_ref[pl.ds(start, half), col : col + step], preferred_element_type=jnp.float32
-            )
+        cols = slice(col, col + step)
+        yield cols, jnp.dot(
+            attended, w_ref[pl.ds(start, half), cols], preferred_element_type=jnp.float32
+        )
+
+
+def output_first_kernel(pair, spread_ref, attended_ref, w_ref, out_ref):
+    for cols, terms in output_terms(0, pair, spread_ref, attended_ref, w_ref):
+        out_ref[:, cols] = terms
+
+
+def output_first(spread, attended, w_out, pair):
+    return pl.pallas_call(
+        functools.partial(output_first_kernel, pair),
+        out_specs=VMEM_SPEC,
+        out_shape=pltpu.VMEM((spread.shape[0], w_out.shape[1]), jnp.float32),
+        cost_estimate=pl.CostEstimate(flops=10**8, bytes_accessed=0, transcendentals=0),
+        compiler_params=pltpu.CompilerParams(vmem_limit_bytes=16 << 20),
+        name="output_first",
+    )(spread, attended, w_out)
+
+
+def output_last_kernel(pair, spread_ref, first_ref, *refs):
+    *attended_refs, w_ref = refs[:pair]
+    *out_refs, token_ref = refs[pair:]
+    token_ref[...] = jnp.zeros_like(token_ref)
+    slots = out_refs[0].shape[0]
+
+    def write(cols, terms):
         for k, out_ref in enumerate(out_refs):
-            piece = terms[k * slots : (k + 1) * slots]
-            out_ref[:, col : col + step] = piece.astype(out_ref.dtype)
-
-
-def output(spread, sides, w_out, slots, parts):
+            out_ref[:, cols] = terms[k * slots : (k + 1) * slots].astype(out_ref.dtype)
+
+    if not attended_refs:
+        write(slice(None), first_ref[...])
+    for attended_ref in attended_refs:
+        for cols, terms in output_terms(1, pair, spread_ref, attended_ref, w_ref):
+            write(cols, first_ref[:, cols] + terms)
+
+
+def output_last(spread, first, others, w_out, slots, parts):
     width = w_out.shape[1]
     return pl.pallas_call(
-        functools.partial(output_kernel, len(sides)),
+        functools.partial(output_last_kernel, len(others) + 1),
         out_shape=[
             jax.ShapeDtypeStruct((slots, width), jnp.bfloat16 if k else jnp.float32)
             for k in range(parts)
         ]
         + [TOKEN],
         compiler_params=pltpu.CompilerParams(vmem_limit_bytes=16 << 20),
-        name="output",
-    )(spread, *sides, w_out)
+        name="output_last",
+    )(spread, first, *others, w_out)
 
 
 def mlp_kernel(pieces, *refs):
@@ -456,11 +478,11 @@
     rows = [ref[j] for ref in row_refs for j in range(ref.shape[0])]
     rows = jnp.concatenate(rows, axis=0)
     count = out_refs[0].shape[0]
-    step = math.gcd(hidden, 512)
+    step = math.gcd(hidden, 768)
     for col in range(0, hidden, step):
         lifted = jnp.dot(rows, up_ref[:, col : col + step], preferred_element_type=jnp.float32)
         act_ref[:, col : col + step] = jax.nn.gelu(lifted, approximate=True).astype(jnp.bfloat16)
-    step = math.gcd(width, 512)
+    step = math.gcd(width, 1024)
     for col in range(0, width, step):
         down = jnp.dot(
             act_ref[...], down_ref[:, col : col + step], preferred_element_type=jnp.float32
@@ -609,8 +631,10 @@
     w_up, token = hold(token, w_up)
     parts = far_first([trade(x, "blk", j * pair) for j, x in enumerate(parts)])
     attended = combine(token, parts, group, pair)
-    attended = [trade(x, "blk", side) for side, x in enumerate(attended)]
-    *terms, token = output(spread, attended, w_out, slots, uly_size)
+    mine, *others = attended
+    others = [trade(x, "blk", 1) for x in others]
+    terms = output_first(spread, mine, w_out, pair)
+    *terms, token = output_last(spread, terms, others, w_out, slots, uly_size)
     w_down, cached, token = hold(token, w_down, cached_out)
     terms = far_first([trade(x, "uly", k) for k, x in enumerate(terms)])
     after_attn, norm_mlp = renorm(token, rows_in, modulation, terms)

time: 81 us -> 80.9 us (level)
  transfers between devices with their start and end apart: 26 -> 26, of which waited for: 16 -> 16; matrix products, arithmetic and copies ran while one was open for 0% -> 0% of each run, Pallas kernels for 18% -> 19%
where the time goes in v4:
time: 80.9 us; the launch traced here: 80.7 us
  starting transfers between devices  34.7 us (43%)
  Pallas kernels  23 us (28%)
  waiting for transfers between devices  22.8 us (28%)
    ppermute x26, starting transfers between devices, trade(): lax.ppermute(x, axis, [(i, i ^ flip) for i in range(lax.axis_size(axis))])  34.7 us
    ppermute x26, waiting for transfers between devices, trade(): lax.ppermute(x, axis, [(i, i ^ flip) for i in range(lax.axis_size(axis))])  22.8 us
    pallas_call x4, Pallas kernels, hold(): pl.pallas_call(functools.partial(hold_kernel, count), in_specs=[VMEM_SPEC...  12.1 us
    pallas_call x1, Pallas kernels, mlp(): pl.pallas_call(functools.partial(mlp_kernel, len(rows)), out_shape=[jax.S...  2.71 us
    pallas_call x1, Pallas kernels, enter(): pl.pallas_call(functools.partial(enter_kernel, pair), in_specs=[ANY_SPEC]...  2.02 us
    pallas_call x1, Pallas kernels, project(): pl.pallas_call(functools.partial(project_kernel, len(rows)), in_specs=[VM...  1.74 us
  transfers between devices with their start and end apart: 26, of which 16 were waited for; matrix products, arithmetic and copies ran while one was open for 0% of the time, Pallas kernels for 19%

profile of v4, /device:TPU:0, one launch (start us, length us, event | category | flops | bytes accessed | tf_op | source)
XLA Modules:
  0.0 80.7 jit_solution(9006774437145789207)
XLA Ops:
  0.0 2.0 %enter.1 = (f32[16,3072]{1,0:T(8,128)S(1)}, bf16[16,3200]{1,0:T(8,128)(2,1)S(1)}, bf16[64,16]{1,0:T(8,128)(2,1)S(1)}, f32[6,3072]{1,0:T(8,128)S(1)}, bf16[4,64,7...) custom-call(s32[1,16]{1,0:T(1,128)} %bitcast.2, bf16[64,3072]{1,0:T(8,128)(2,1)} %hidden_hbm.1, f32[6,3072]{1,0:T(8,128)} %mod_hbm.1, ...), custom_call_target="tpu_custom_call" | custom-call | tf_op jit(solution)/shard_map/enter/pallas_call | solution.py:137
  2.6 3.7 %collective-permute-start.2 = (bf16[16,3200]{1,0:T(8,128)(2,1)S(1)}, bf16[16,3200]{1,0:T(8,128)(2,1)S(1)}, u32[]{:S(2)}, u32[]{:S(2)}) collective-permute-start(bf16[16,3200]{1,0:T(8,128)(2,1)S(1)} %get-tuple-element.56.refs_0_), channel_id=1, source_target_pairs={{0,2},{1,3},{2,0},{3,1},{4,6},{5,7},{6,4},{7,5},{8,10},{9,11},{10,... | collective-permute-start | bytes 307208 | tf_op jit(solution)/shard_map/ppermute | solution.py:42
  6.2 1.6 %collective-permute-start.1 = (bf16[16,3200]{1,0:T(8,128)(2,1)S(1)}, bf16[16,3200]{1,0:T(8,128)(2,1)S(1)}, u32[]{:S(2)}, u32[]{:S(2)}) collective-permute-start(bf16[16,3200]{1,0:T(8,128)(2,1)S(1)} %get-tuple-element.56.refs_0_), channel_id=1, source_target_pairs={{0,1},{1,0},{2,3},{3,2},{4,5},{5,4},{6,7},{7,6},{8,9},{9,8},{10,11... | collective-permute-start | bytes 307208 | tf_op jit(solution)/shard_map/ppermute | solution.py:42
  7.8 2.3 %hold.4 = (bf16[3072,768]{1,0:T(8,128)(2,1)S(1)}, f32[8,128]{1,0:T(8,128)S(1)}) custom-call(bf16[16,3200]{1,0:T(8,128)(2,1)S(1)} %get-tuple-element.56.refs_0_, bf16[3072,768]{1,0:T(8,128)(2,1)} %refs_1_.4), custom_call_target="tpu_custom_call" | custom-call | bytes 4718592 | tf_op jit(solution)/shard_map/hold/pallas_call | solution.py:66
  10.2 1.8 %collective-permute-done.2.x_ref = bf16[16,3200]{1,0:T(8,128)(2,1)S(1)} collective-permute-done((bf16[16,3200]{1,0:T(8,128)(2,1)S(1)}, bf16[16,3200]{1,0:T(8,128)(2,1)S(1)}, u32[]{:S(2)}, u32[]{:S(2)}) %collective-permute-start.2) | collective-permute-done | bytes 102432 | tf_op jit(solution)/shard_map/ppermute | solution.py:42
  12.7 3.4 %collective-permute-start.8 = (bf16[2,64,768]{2,1,0:T(8,128)(2,1)S(1)}, bf16[2,64,768]{2,1,0:T(8,128)(2,1)S(1)}, u32[]{:S(2)}, u32[]{:S(2)}) collective-permute-start(bf16[2,64,768]{2,1,0:T(8,128)(2,1)S(1)} %get-tuple-element.66), channel_id=1, source_target_pairs={{0,2},{1,3},{2,0},{3,1},{4,6},{5,7},{6,4},{7,5},{8,10},{9,11},{10,... | collective-permute-start | bytes 589832 | tf_op jit(solution)/shard_map/ppermute | solution.py:42
  16.8 4.9 %collective-permute-start.9 = (bf16[2,64,768]{2,1,0:T(8,128)(2,1)S(1)}, bf16[2,64,768]{2,1,0:T(8,128)(2,1)S(1)}, u32[]{:S(2)}, u32[]{:S(2)}) collective-permute-start(bf16[2,64,768]{2,1,0:T(8,128)(2,1)S(1)} %get-tuple-element.71), channel_id=1, source_target_pairs={{0,3},{1,2},{2,1},{3,0},{4,7},{5,6},{6,5},{7,4},{8,11},{9,10},{10,... | collective-permute-start | bytes 589832 | tf_op jit(solution)/shard_map/ppermute | solution.py:42
  21.6 1.7 %project.1 = (bf16[40,384]{1,0:T(8,128)(2,1)S(1)}, bf16[40,384]{1,0:T(8,128)(2,1)S(1)}, bf16[64,128]{1,0:T(8,128)(2,1)S(1)}, f32[8,128]{1,0:T(8,128)S(1)}) custom-call(f32[8,128]{1,0:T(8,128)S(1)} %get-tuple-element.59.after_ref, bf16[16,3200]{1,0:T(8,128)(2,1)S(1)} %get-tuple-element.56.refs_0_, ...), custom_call_target="tpu_custom_call" | custom-call | tf_op jit(solution)/shard_map/project/pallas_call | solution.py:241
  30.4 2.3 %hold.5 = (bf16[768,3072]{1,0:T(8,128)(2,1)S(1)}, f32[8,128]{1,0:T(8,128)S(1)}) custom-call(f32[8,128]{1,0:T(8,128)S(1)} %get-tuple-element.62.refs_0_, bf16[768,3072]{1,0:T(8,128)(2,1)} %refs_1_.5), custom_call_target="tpu_custom_call" | custom-call | bytes 4718592 | tf_op jit(solution)/shard_map/hold/pallas_call | solution.py:66
  34.5 2.5 %collective-permute-start.11 = (f32[88,384]{1,0:T(8,128)S(1)}, f32[88,384]{1,0:T(8,128)S(1)}, u32[]{:S(2)}, u32[]{:S(2)}) collective-permute-start(f32[88,384]{1,0:T(8,128)S(1)} %get-tuple-element.76), channel_id=1, source_target_pairs={{0,24},{4,28},{8,16},{12,20},{16,8},{20,12},{24,0},{28,4},{1,25},{... | collective-permute-start | bytes 405512 | tf_op jit(solution)/shard_map/ppermute | solution.py:42
  38.0 3.7 %hold.6 = (bf16[3072,1536]{1,0:T(8,128)(2,1)S(1)}, f32[8,128]{1,0:T(8,128)S(1)}) custom-call(f32[8,128]{1,0:T(8,128)S(1)} %get-tuple-element.73.refs_0_, bf16[3072,1536]{1,0:T(8,128)(2,1)} %refs_1_.6), custom_call_target="tpu_custom_call" | custom-call | bytes 9437184 | tf_op jit(solution)/shard_map/hold/pallas_call | solution.py:66
  41.7 1.6 %collective-permute-done.12.refs_2_ = f32[88,384]{1,0:T(8,128)S(1)} collective-permute-done((f32[88,384]{1,0:T(8,128)S(1)}, f32[88,384]{1,0:T(8,128)S(1)}, u32[]{:S(2)}, u32[]{:S(2)}) %collective-permute-start.12) | collective-permute-done | bytes 135200 | tf_op jit(solution)/shard_map/ppermute | solution.py:42
  46.4 2.1 %collective-permute-start.16 = (bf16[16,3072]{1,0:T(8,128)(2,1)S(1)}, bf16[16,3072]{1,0:T(8,128)(2,1)S(1)}, u32[]{:S(2)}, u32[]{:S(2)}) collective-permute-start(bf16[16,3072]{1,0:T(8,128)(2,1)S(1)} %get-tuple-element.89), channel_id=1, source_target_pairs={{0,2},{1,3},{2,0},{3,1},{4,6},{5,7},{6,4},{7,5},{8,10},{9,11},{10,... | collective-permute-start | bytes 294920 | tf_op jit(solution)/shard_map/ppermute | solution.py:42
  48.5 1.6 %collective-permute-start.17 = (bf16[16,3072]{1,0:T(8,128)(2,1)S(1)}, bf16[16,3072]{1,0:T(8,128)(2,1)S(1)}, u32[]{:S(2)}, u32[]{:S(2)}) collective-permute-start(bf16[16,3072]{1,0:T(8,128)(2,1)S(1)} %get-tuple-element.90), channel_id=1, source_target_pairs={{0,1},{1,0},{2,3},{3,2},{4,5},{5,4},{6,7},{7,6},{8,9},{9,8},{10,11... | collective-permute-start | bytes 294920 | tf_op jit(solution)/shard_map/ppermute | solution.py:42
  50.2 3.7 %hold.7 = (bf16[1536,3072]{1,0:T(8,128)(2,1)S(1)}, bf16[64,3072]{1,0:T(8,128)(2,1)S(1)}, f32[8,128]{1,0:T(8,128)S(1)}) custom-call(f32[8,128]{1,0:T(8,128)S(1)} %get-tuple-element.82.refs_0_, bf16[1536,3072]{1,0:T(8,128)(2,1)} %refs_1_.7, bf16[64,3072]{1,0:T(8,128)(2,1)} %refs_2_.1), custom_call_target="tpu_custom_call" | custom-call | bytes 9830400 | tf_op jit(solution)/shard_map/hold/pallas_call | solution.py:66
  53.9 3.8 %collective-permute-done.16.refs_2_ = bf16[16,3072]{1,0:T(8,128)(2,1)S(1)} collective-permute-done((bf16[16,3072]{1,0:T(8,128)(2,1)S(1)}, bf16[16,3072]{1,0:T(8,128)(2,1)S(1)}, u32[]{:S(2)}, u32[]{:S(2)}) %collective-permute-start.16) | collective-permute-done | bytes 98336 | tf_op jit(solution)/shard_map/ppermute | solution.py:42
  58.0 1.7 %collective-permute-start.20 = (bf16[16,3072]{1,0:T(8,128)(2,1)S(1)}, bf16[16,3072]{1,0:T(8,128)(2,1)S(1)}, u32[]{:S(2)}, u32[]{:S(2)}) collective-permute-start(bf16[16,3072]{1,0:T(8,128)(2,1)S(1)} %get-tuple-element.92.refs_0_), channel_id=1, source_target_pairs={{0,24},{4,28},{8,16},{12,20},{16,8},{20,12},{24,0},{28,4},{1,25},{... | collective-permute-start | bytes 294920 | tf_op jit(solution)/shard_map/ppermute | solution.py:42
  61.5 3.1 %collective-permute-done.20.refs_3_ = bf16[16,3072]{1,0:T(8,128)(2,1)S(1)} collective-permute-done((bf16[16,3072]{1,0:T(8,128)(2,1)S(1)}, bf16[16,3072]{1,0:T(8,128)(2,1)S(1)}, u32[]{:S(2)}, u32[]{:S(2)}) %collective-permute-start.20) | collective-permute-done | bytes 98336 | tf_op jit(solution)/shard_map/ppermute | solution.py:42
  65.5 1.7 %collective-permute-done.21.refs_1_ = bf16[4,16,3072]{2,1,0:T(8,128)(2,1)S(1)} collective-permute-done((bf16[4,16,3072]{2,1,0:T(8,128)(2,1)S(1)}, bf16[4,16,3072]{2,1,0:T(8,128)(2,1)S(1)}, u32[]{:S(2)}, u32[]{:S(2)}) %collective-permute-start.21) | collective-permute-done | bytes 393248 | tf_op jit(solution)/shard_map/ppermute | solution.py:42
  67.2 2.7 %mlp.1 = (f32[64,3072]{1,0:T(8,128)S(1)}, bf16[64,3072]{1,0:T(8,128)(2,1)S(1)}) custom-call(bf16[4,16,3072]{2,1,0:T(8,128)(2,1)S(1)} %join.3.refs_0_, bf16[4,16,3072]{2,1,0:T(8,128)(2,1)S(1)} %collective-permute-done.21.refs_1_, bf16[3072,1536]{1,0:T(8,128)(2,1)S(1)} %get-tuple-element.93.refs_2_, bf16[1536,3072]{1,0:T(8,128)(2,1)S(1)} %get-tuple-element.94.refs_3_), custom_call_target="tpu_custom_call" | custom-call | tf_op jit(solution)/shard_map/mlp/pallas_call | solution.py:498
  70.1 1.6 %collective-permute-done.22.refs_1_ = bf16[64,3072]{1,0:T(8,128)(2,1)S(1)} collective-permute-done((bf16[64,3072]{1,0:T(8,128)(2,1)S(1)}, bf16[64,3072]{1,0:T(8,128)(2,1)S(1)}, u32[]{:S(2)}, u32[]{:S(2)}) %collective-permute-start.22) | collective-permute-done | bytes 393248 | tf_op jit(solution)/shard_map/ppermute | solution.py:42
  71.8 1.7 %collective-permute-start.23 = (bf16[16,3072]{1,0:T(8,128)(2,1)S(1)}, bf16[16,3072]{1,0:T(8,128)(2,1)S(1)}, u32[]{:S(2)}, u32[]{:S(2)}) collective-permute-start(bf16[16,3072]{1,0:T(8,128)(2,1)S(1)} %get-tuple-element.98), channel_id=1, source_target_pairs={{0,24},{4,28},{8,16},{12,20},{16,8},{20,12},{24,0},{28,4},{1,25},{... | collective-permute-start | bytes 294920 | tf_op jit(solution)/shard_map/ppermute | solution.py:42
  75.3 2.8 %collective-permute-done.23.refs_1_ = bf16[16,3072]{1,0:T(8,128)(2,1)S(1)} collective-permute-done((bf16[16,3072]{1,0:T(8,128)(2,1)S(1)}, bf16[16,3072]{1,0:T(8,128)(2,1)S(1)}, u32[]{:S(2)}, u32[]{:S(2)}) %collective-permute-start.23) | collective-permute-done | bytes 98336 | tf_op jit(solution)/shard_map/ppermute | solution.py:42
  78.1 1.6 %collective-permute-done.24.refs_2_ = bf16[16,3072]{1,0:T(8,128)(2,1)S(1)} collective-permute-done((bf16[16,3072]{1,0:T(8,128)(2,1)S(1)}, bf16[16,3072]{1,0:T(8,128)(2,1)S(1)}, u32[]{:S(2)}, u32[]{:S(2)}) %collective-permute-start.24) | collective-permute-done | bytes 98336 | tf_op jit(solution)/shard_map/ppermute | solution.py:42
  (48 shorter events, 21.0 us)
Async XLA Ops:
  2.0 8.1 %collective-permute-start = (bf16[4,64,768]{2,1,0:T(8,128)(2,1)S(1)}, bf16[4,64,768]{2,1,0:T(8,128)(2,1)S(1)}, u32[]{:S(2)}, u32[]{:S(2)}) collective-permute-start(bf16[4,64,768]{2,1,0:T(8,128)(2,1)S(1)} %get-tuple-element.55), channel_id=1, source_target_pairs={{0,4},{4,0},{8,12},{12,8},{16,20},{20,16},{24,28},{28,24},{1,5},{5... | collective-permute-start | bytes 1179656 | tf_op jit(solution)/shard_map/ppermute | solution.py:42
  2.6 9.4 %collective-permute-start.2 = (bf16[16,3200]{1,0:T(8,128)(2,1)S(1)}, bf16[16,3200]{1,0:T(8,128)(2,1)S(1)}, u32[]{:S(2)}, u32[]{:S(2)}) collective-permute-start(bf16[16,3200]{1,0:T(8,128)(2,1)S(1)} %get-tuple-element.56.refs_0_), channel_id=1, source_target_pairs={{0,2},{1,3},{2,0},{3,1},{4,6},{5,7},{6,4},{7,5},{8,10},{9,11},{10,... | collective-permute-start | bytes 307208 | tf_op jit(solution)/shard_map/ppermute | solution.py:42
  6.2 9.9 %collective-permute-start.1 = (bf16[16,3200]{1,0:T(8,128)(2,1)S(1)}, bf16[16,3200]{1,0:T(8,128)(2,1)S(1)}, u32[]{:S(2)}, u32[]{:S(2)}) collective-permute-start(bf16[16,3200]{1,0:T(8,128)(2,1)S(1)} %get-tuple-element.56.refs_0_), channel_id=1, source_target_pairs={{0,1},{1,0},{2,3},{3,2},{4,5},{5,4},{6,7},{7,6},{8,9},{9,8},{10,11... | collective-permute-start | bytes 307208 | tf_op jit(solution)/shard_map/ppermute | solution.py:42
  12.0 4.7 %collective-permute-start.3 = (bf16[16,3200]{1,0:T(8,128)(2,1)S(1)}, bf16[16,3200]{1,0:T(8,128)(2,1)S(1)}, u32[]{:S(2)}, u32[]{:S(2)}) collective-permute-start(bf16[16,3200]{1,0:T(8,128)(2,1)S(1)} %relay.1.refs_3_.refs_2_), channel_id=1, source_target_pairs={{0,1},{1,0},{2,3},{3,2},{4,5},{5,4},{6,7},{7,6},{8,9},{9,8},{10,11... | collective-permute-start | bytes 307208 | tf_op jit(solution)/shard_map/ppermute | solution.py:42
  12.7 20.0 %collective-permute-start.8 = (bf16[2,64,768]{2,1,0:T(8,128)(2,1)S(1)}, bf16[2,64,768]{2,1,0:T(8,128)(2,1)S(1)}, u32[]{:S(2)}, u32[]{:S(2)}) collective-permute-start(bf16[2,64,768]{2,1,0:T(8,128)(2,1)S(1)} %get-tuple-element.66), channel_id=1, source_target_pairs={{0,2},{1,3},{2,0},{3,1},{4,6},{5,7},{6,4},{7,5},{8,10},{9,11},{10,... | collective-permute-start | bytes 589832 | tf_op jit(solution)/shard_map/ppermute | solution.py:42
  16.8 16.9 %collective-permute-start.9 = (bf16[2,64,768]{2,1,0:T(8,128)(2,1)S(1)}, bf16[2,64,768]{2,1,0:T(8,128)(2,1)S(1)}, u32[]{:S(2)}, u32[]{:S(2)}) collective-permute-start(bf16[2,64,768]{2,1,0:T(8,128)(2,1)S(1)} %get-tuple-element.71), channel_id=1, source_target_pairs={{0,3},{1,2},{2,1},{3,0},{4,7},{5,6},{6,5},{7,4},{8,11},{9,10},{10,... | collective-permute-start | bytes 589832 | tf_op jit(solution)/shard_map/ppermute | solution.py:42
  21.6 12.1 %collective-permute-start.10 = (bf16[2,64,768]{2,1,0:T(8,128)(2,1)S(1)}, bf16[2,64,768]{2,1,0:T(8,128)(2,1)S(1)}, u32[]{:S(2)}, u32[]{:S(2)}) collective-permute-start(bf16[2,64,768]{2,1,0:T(8,128)(2,1)S(1)} %get-tuple-element.72), channel_id=1, source_target_pairs={{0,1},{1,0},{2,3},{3,2},{4,5},{5,4},{6,7},{7,6},{8,9},{9,8},{10,11... | collective-permute-start | bytes 589832 | tf_op jit(solution)/shard_map/ppermute | solution.py:42
  24.6 4.2 %collective-permute-start.6 = (bf16[2,40,384]{2,1,0:T(8,128)(2,1)S(1)}, bf16[2,40,384]{2,1,0:T(8,128)(2,1)S(1)}, u32[]{:S(2)}, u32[]{:S(2)}) collective-permute-start(bf16[2,40,384]{2,1,0:T(8,128)(2,1)S(1)} %join.2.refs_0_), channel_id=1, source_target_pairs={{0,16},{4,20},{8,24},{12,28},{16,0},{20,4},{24,8},{28,12},{1,17},{... | collective-permute-start | bytes 184328 | tf_op jit(solution)/shard_map/ppermute | solution.py:42
  26.2 6.5 %collective-permute-start.5 = (bf16[2,40,384]{2,1,0:T(8,128)(2,1)S(1)}, bf16[2,40,384]{2,1,0:T(8,128)(2,1)S(1)}, u32[]{:S(2)}, u32[]{:S(2)}) collective-permute-start(bf16[2,40,384]{2,1,0:T(8,128)(2,1)S(1)} %join.2.refs_0_), channel_id=1, source_target_pairs={{0,8},{4,12},{8,0},{12,4},{16,24},{20,28},{24,16},{28,20},{1,9},{5... | collective-permute-start | bytes 184328 | tf_op jit(solution)/shard_map/ppermute | solution.py:42
  28.9 4.2 %collective-permute-start.7 = (bf16[2,40,384]{2,1,0:T(8,128)(2,1)S(1)}, bf16[2,40,384]{2,1,0:T(8,128)(2,1)S(1)}, u32[]{:S(2)}, u32[]{:S(2)}) collective-permute-start(bf16[2,40,384]{2,1,0:T(8,128)(2,1)S(1)} %collective-permute-done.6.refs_2_), channel_id=1, source_target_pairs={{0,8},{4,12},{8,0},{12,4},{16,24},{20,28},{24,16},{28,20},{1,9},{5... | collective-permute-start | bytes 184328 | tf_op jit(solution)/shard_map/ppermute | solution.py:42
  34.5 7.2 %collective-permute-start.11 = (f32[88,384]{1,0:T(8,128)S(1)}, f32[88,384]{1,0:T(8,128)S(1)}, u32[]{:S(2)}, u32[]{:S(2)}) collective-permute-start(f32[88,384]{1,0:T(8,128)S(1)} %get-tuple-element.76), channel_id=1, source_target_pairs={{0,24},{4,28},{8,16},{12,20},{16,8},{20,12},{24,0},{28,4},{1,25},{... | collective-permute-start | bytes 405512 | tf_op jit(solution)/shard_map/ppermute | solution.py:42
  37.0 6.3 %collective-permute-start.12 = (f32[88,384]{1,0:T(8,128)S(1)}, f32[88,384]{1,0:T(8,128)S(1)}, u32[]{:S(2)}, u32[]{:S(2)}) collective-permute-start(f32[88,384]{1,0:T(8,128)S(1)} %get-tuple-element.77), channel_id=1, source_target_pairs={{0,16},{4,20},{8,24},{12,28},{16,0},{20,4},{24,8},{28,12},{1,17},{... | collective-permute-start | bytes 405512 | tf_op jit(solution)/shard_map/ppermute | solution.py:42
  37.5 5.9 %collective-permute-start.13 = (f32[88,384]{1,0:T(8,128)S(1)}, f32[88,384]{1,0:T(8,128)S(1)}, u32[]{:S(2)}, u32[]{:S(2)}) collective-permute-start(f32[88,384]{1,0:T(8,128)S(1)} %get-tuple-element.78), channel_id=1, source_target_pairs={{0,8},{4,12},{8,0},{12,4},{16,24},{20,28},{24,16},{28,20},{1,9},{5... | collective-permute-start | bytes 405512 | tf_op jit(solution)/shard_map/ppermute | solution.py:42
  45.7 8.2 %collective-permute-start.15 = (bf16[16,3072]{1,0:T(8,128)(2,1)S(1)}, bf16[16,3072]{1,0:T(8,128)(2,1)S(1)}, u32[]{:S(2)}, u32[]{:S(2)}) collective-permute-start(bf16[16,3072]{1,0:T(8,128)(2,1)S(1)} %get-tuple-element.88), channel_id=1, source_target_pairs={{0,3},{1,2},{2,1},{3,0},{4,7},{5,6},{6,5},{7,4},{8,11},{9,10},{10,... | collective-permute-start | bytes 294920 | tf_op jit(solution)/shard_map/ppermute | solution.py:42
  46.4 11.3 %collective-permute-start.16 = (bf16[16,3072]{1,0:T(8,128)(2,1)S(1)}, bf16[16,3072]{1,0:T(8,128)(2,1)S(1)}, u32[]{:S(2)}, u32[]{:S(2)}) collective-permute-start(bf16[16,3072]{1,0:T(8,128)(2,1)S(1)} %get-tuple-element.89), channel_id=1, source_target_pairs={{0,2},{1,3},{2,0},{3,1},{4,6},{5,7},{6,4},{7,5},{8,10},{9,11},{10,... | collective-permute-start | bytes 294920 | tf_op jit(solution)/shard_map/ppermute | solution.py:42
  48.5 9.2 %collective-permute-start.17 = (bf16[16,3072]{1,0:T(8,128)(2,1)S(1)}, bf16[16,3072]{1,0:T(8,128)(2,1)S(1)}, u32[]{:S(2)}, u32[]{:S(2)}) collective-permute-start(bf16[16,3072]{1,0:T(8,128)(2,1)S(1)} %get-tuple-element.90), channel_id=1, source_target_pairs={{0,1},{1,0},{2,3},{3,2},{4,5},{5,4},{6,7},{7,6},{8,9},{9,8},{10,11... | collective-permute-start | bytes 294920 | tf_op jit(solution)/shard_map/ppermute | solution.py:42
  58.0 6.7 %collective-permute-start.20 = (bf16[16,3072]{1,0:T(8,128)(2,1)S(1)}, bf16[16,3072]{1,0:T(8,128)(2,1)S(1)}, u32[]{:S(2)}, u32[]{:S(2)}) collective-permute-start(bf16[16,3072]{1,0:T(8,128)(2,1)S(1)} %get-tuple-element.92.refs_0_), channel_id=1, source_target_pairs={{0,24},{4,28},{8,16},{12,20},{16,8},{20,12},{24,0},{28,4},{1,25},{... | collective-permute-start | bytes 294920 | tf_op jit(solution)/shard_map/ppermute | solution.py:42
  59.6 5.4 %collective-permute-start.19 = (bf16[16,3072]{1,0:T(8,128)(2,1)S(1)}, bf16[16,3072]{1,0:T(8,128)(2,1)S(1)}, u32[]{:S(2)}, u32[]{:S(2)}) collective-permute-start(bf16[16,3072]{1,0:T(8,128)(2,1)S(1)} %get-tuple-element.92.refs_0_), channel_id=1, source_target_pairs={{0,16},{4,20},{8,24},{12,28},{16,0},{20,4},{24,8},{28,12},{1,17},{... | collective-permute-start | bytes 294920 | tf_op jit(solution)/shard_map/ppermute | solution.py:42
  60.8 4.6 %collective-permute-start.18 = (bf16[16,3072]{1,0:T(8,128)(2,1)S(1)}, bf16[16,3072]{1,0:T(8,128)(2,1)S(1)}, u32[]{:S(2)}, u32[]{:S(2)}) collective-permute-start(bf16[16,3072]{1,0:T(8,128)(2,1)S(1)} %get-tuple-element.92.refs_0_), channel_id=1, source_target_pairs={{0,8},{4,12},{8,0},{12,4},{16,24},{20,28},{24,16},{28,20},{1,9},{5... | collective-permute-start | bytes 294920 | tf_op jit(solution)/shard_map/ppermute | solution.py:42
  65.4 1.8 %collective-permute-start.21 = (bf16[4,16,3072]{2,1,0:T(8,128)(2,1)S(1)}, bf16[4,16,3072]{2,1,0:T(8,128)(2,1)S(1)}, u32[]{:S(2)}, u32[]{:S(2)}) collective-permute-start(bf16[4,16,3072]{2,1,0:T(8,128)(2,1)S(1)} %join.3.refs_0_), channel_id=1, source_target_pairs={{0,4},{4,0},{8,12},{12,8},{16,20},{20,16},{24,28},{28,24},{1,5},{5... | collective-permute-start | bytes 1179656 | tf_op jit(solution)/shard_map/ppermute | solution.py:42
  69.9 1.8 %collective-permute-start.22 = (bf16[64,3072]{1,0:T(8,128)(2,1)S(1)}, bf16[64,3072]{1,0:T(8,128)(2,1)S(1)}, u32[]{:S(2)}, u32[]{:S(2)}) collective-permute-start(bf16[64,3072]{1,0:T(8,128)(2,1)S(1)} %get-tuple-element.96), channel_id=1, source_target_pairs={{0,4},{4,0},{8,12},{12,8},{16,20},{20,16},{24,28},{28,24},{1,5},{5... | collective-permute-start | bytes 1179656 | tf_op jit(solution)/shard_map/ppermute | solution.py:42
  71.8 6.4 %collective-permute-start.23 = (bf16[16,3072]{1,0:T(8,128)(2,1)S(1)}, bf16[16,3072]{1,0:T(8,128)(2,1)S(1)}, u32[]{:S(2)}, u32[]{:S(2)}) collective-permute-start(bf16[16,3072]{1,0:T(8,128)(2,1)S(1)} %get-tuple-element.98), channel_id=1, source_target_pairs={{0,24},{4,28},{8,16},{12,20},{16,8},{20,12},{24,0},{28,4},{1,25},{... | collective-permute-start | bytes 294920 | tf_op jit(solution)/shard_map/ppermute | solution.py:42
  73.4 6.3 %collective-permute-start.24 = (bf16[16,3072]{1,0:T(8,128)(2,1)S(1)}, bf16[16,3072]{1,0:T(8,128)(2,1)S(1)}, u32[]{:S(2)}, u32[]{:S(2)}) collective-permute-start(bf16[16,3072]{1,0:T(8,128)(2,1)S(1)} %get-tuple-element.99), channel_id=1, source_target_pairs={{0,16},{4,20},{8,24},{12,28},{16,0},{20,4},{24,8},{28,12},{1,17},{... | collective-permute-start | bytes 294920 | tf_op jit(solution)/shard_map/ppermute | solution.py:42
  74.3 5.4 %collective-permute-start.25 = (bf16[16,3072]{1,0:T(8,128)(2,1)S(1)}, bf16[16,3072]{1,0:T(8,128)(2,1)S(1)}, u32[]{:S(2)}, u32[]{:S(2)}) collective-permute-start(bf16[16,3072]{1,0:T(8,128)(2,1)S(1)} %get-tuple-element.100), channel_id=1, source_target_pairs={{0,8},{4,12},{8,0},{12,4},{16,24},{20,28},{24,16},{28,20},{1,9},{5... | collective-permute-start | bytes 294920 | tf_op jit(solution)/shard_map/ppermute | solution.py:42
  (2 other events, 2.5 us)

commit v5 on v4

--- a/solution.py
+++ b/solution.py
@@ -217,21 +217,23 @@
     spread = jnp.where((rank == lane) & (flags.astype(jnp.float32) > 0.0), 1.0, 0.0)
     spread = spread.astype(jnp.bfloat16)
     spread_ref[...] = spread
-    projected = jnp.dot(rows[:, :width], w_ref[...], preferred_element_type=jnp.float32)
+    live_rows = lax.dot_general(
+        spread[:, :group],
+        rows[:, :width],
+        (((0,), (0,)), ((), ())),
+        preferred_element_type=jnp.float32,
+    ).astype(jnp.bfloat16)
+    projected = jnp.dot(live_rows, w_ref[...], preferred_element_type=jnp.float32)
     copy.wait()
     for start in range(0, projected.shape[1], DH):
         head = projected[:, start : start + DH]
         squares = jnp.mean(head * head, axis=-1, keepdims=True)
-        head = head * lax.rsqrt(squares + 1e-06) * (gain_ref[...] / math.sqrt(DH))
-        heads_ref[:, start : start + DH] = head.astype(jnp.bfloat16)
+        heads_ref[:, start : start + DH] = (
+            head * lax.rsqrt(squares + 1e-06) * (gain_ref[...] / math.sqrt(DH))
+        )
     for side, query_ref in enumerate(query_refs):
         start = pl.multiple_of((core ^ side) * half, DH)
-        query_ref[...] = lax.dot_general(
-            spread[:, :group],
-            heads_ref[:, pl.ds(start, half)],
-            (((0,), (0,)), ((), ())),
-            preferred_element_type=jnp.float32,
-        ).astype(jnp.bfloat16)
+        query_ref[...] = heads_ref[:, pl.ds(start, half)].astype(jnp.bfloat16)
 
 
 def project(after, rows, w_query, q_gain, group, pair):
@@ -243,7 +245,7 @@
         in_specs=[VMEM_SPEC] * (len(rows) + 2) + [ANY_SPEC],
         out_shape=[query] * pair + [jax.ShapeDtypeStruct((everyone, DH), jnp.bfloat16), TOKEN],
         scratch_shapes=[
-            pltpu.VMEM((everyone, w_query.shape[1]), jnp.bfloat16),
+            pltpu.VMEM((group, w_query.shape[1]), jnp.float32),
             pltpu.VMEM((1, DH), jnp.float32),
             pltpu.SemaphoreType.DMA,
         ],
@@ -616,7 +618,7 @@
     sides = [trade(x, "blk", side) for side, x in enumerate(sides)]
     w_query, token = hold(normed, w_query)
     half_way = uly_size // 2
-    cuts = [[half_way, 0], [k for k in reversed(range(uly_size)) if k not in (0, half_way)]]
+    cuts = [[half_way, 0], [k for k in range(uly_size) if k not in (0, half_way)]]
     first, token = merge_kv(sides, cuts[0], [token])
     group_rows = double(normed, "uly", 1, uly_size, {half_way: lambda x: relay(x, token)})
     second, token = merge_kv(sides, cuts[1], group_rows[1:])

time: 80.9 us -> 80.1 us (level)
  no operation moved by 1% of the time
where the time goes in v5:
time: 80.1 us; the launch traced here: 79.8 us
  starting transfers between devices  34.8 us (43%)
  Pallas kernels  22.7 us (28%)
  waiting for transfers between devices  22.2 us (28%)
    ppermute x26, starting transfers between devices, trade(): lax.ppermute(x, axis, [(i, i ^ flip) for i in range(lax.axis_size(axis))])  34.8 us
    ppermute x26, waiting for transfers between devices, trade(): lax.ppermute(x, axis, [(i, i ^ flip) for i in range(lax.axis_size(axis))])  22.2 us
    pallas_call x4, Pallas kernels, hold(): pl.pallas_call(functools.partial(hold_kernel, count), in_specs=[VMEM_SPEC...  12.1 us
    pallas_call x1, Pallas kernels, mlp(): pl.pallas_call(functools.partial(mlp_kernel, len(rows)), out_shape=[jax.S...  2.7 us
    pallas_call x1, Pallas kernels, enter(): pl.pallas_call(functools.partial(enter_kernel, pair), in_specs=[ANY_SPEC]...  2.02 us
  transfers between devices with their start and end apart: 26, of which 16 were waited for; matrix products, arithmetic and copies ran while one was open for 0% of the time, Pallas kernels for 19%

profile of v5, /device:TPU:0, one launch (start us, length us, event | category | flops | bytes accessed | tf_op | source)
XLA Modules:
  0.0 79.8 jit_solution(10572984038876849865)
XLA Ops:
  0.0 2.0 %enter.1 = (f32[16,3072]{1,0:T(8,128)S(1)}, bf16[16,3200]{1,0:T(8,128)(2,1)S(1)}, bf16[64,16]{1,0:T(8,128)(2,1)S(1)}, f32[6,3072]{1,0:T(8,128)S(1)}, bf16[4,64,7...) custom-call(s32[1,16]{1,0:T(1,128)} %bitcast.2, bf16[64,3072]{1,0:T(8,128)(2,1)} %hidden_hbm.1, f32[6,3072]{1,0:T(8,128)} %mod_hbm.1, ...), custom_call_target="tpu_custom_call" | custom-call | tf_op jit(solution)/shard_map/enter/pallas_call | solution.py:137
  2.6 3.7 %collective-permute-start.2 = (bf16[16,3200]{1,0:T(8,128)(2,1)S(1)}, bf16[16,3200]{1,0:T(8,128)(2,1)S(1)}, u32[]{:S(2)}, u32[]{:S(2)}) collective-permute-start(bf16[16,3200]{1,0:T(8,128)(2,1)S(1)} %get-tuple-element.56.refs_0_), channel_id=1, source_target_pairs={{0,2},{1,3},{2,0},{3,1},{4,6},{5,7},{6,4},{7,5},{8,10},{9,11},{10,... | collective-permute-start | bytes 307208 | tf_op jit(solution)/shard_map/ppermute | solution.py:42
  6.2 1.6 %collective-permute-start.1 = (bf16[16,3200]{1,0:T(8,128)(2,1)S(1)}, bf16[16,3200]{1,0:T(8,128)(2,1)S(1)}, u32[]{:S(2)}, u32[]{:S(2)}) collective-permute-start(bf16[16,3200]{1,0:T(8,128)(2,1)S(1)} %get-tuple-element.56.refs_0_), channel_id=1, source_target_pairs={{0,1},{1,0},{2,3},{3,2},{4,5},{5,4},{6,7},{7,6},{8,9},{9,8},{10,11... | collective-permute-start | bytes 307208 | tf_op jit(solution)/shard_map/ppermute | solution.py:42
  7.8 2.3 %hold.4 = (bf16[3072,768]{1,0:T(8,128)(2,1)S(1)}, f32[8,128]{1,0:T(8,128)S(1)}) custom-call(bf16[16,3200]{1,0:T(8,128)(2,1)S(1)} %get-tuple-element.56.refs_0_, bf16[3072,768]{1,0:T(8,128)(2,1)} %refs_1_.4), custom_call_target="tpu_custom_call" | custom-call | bytes 4718592 | tf_op jit(solution)/shard_map/hold/pallas_call | solution.py:66
  10.2 1.8 %collective-permute-done.2.x_ref = bf16[16,3200]{1,0:T(8,128)(2,1)S(1)} collective-permute-done((bf16[16,3200]{1,0:T(8,128)(2,1)S(1)}, bf16[16,3200]{1,0:T(8,128)(2,1)S(1)}, u32[]{:S(2)}, u32[]{:S(2)}) %collective-permute-start.2) | collective-permute-done | bytes 102432 | tf_op jit(solution)/shard_map/ppermute | solution.py:42
  12.7 3.4 %collective-permute-start.8 = (bf16[2,64,768]{2,1,0:T(8,128)(2,1)S(1)}, bf16[2,64,768]{2,1,0:T(8,128)(2,1)S(1)}, u32[]{:S(2)}, u32[]{:S(2)}) collective-permute-start(bf16[2,64,768]{2,1,0:T(8,128)(2,1)S(1)} %get-tuple-element.66), channel_id=1, source_target_pairs={{0,2},{1,3},{2,0},{3,1},{4,6},{5,7},{6,4},{7,5},{8,10},{9,11},{10,... | collective-permute-start | bytes 589832 | tf_op jit(solution)/shard_map/ppermute | solution.py:42
  17.6 4.1 %collective-permute-start.10 = (bf16[2,64,768]{2,1,0:T(8,128)(2,1)S(1)}, bf16[2,64,768]{2,1,0:T(8,128)(2,1)S(1)}, u32[]{:S(2)}, u32[]{:S(2)}) collective-permute-start(bf16[2,64,768]{2,1,0:T(8,128)(2,1)S(1)} %get-tuple-element.72), channel_id=1, source_target_pairs={{0,3},{1,2},{2,1},{3,0},{4,7},{5,6},{6,5},{7,4},{8,11},{9,10},{10,... | collective-permute-start | bytes 589832 | tf_op jit(solution)/shard_map/ppermute | solution.py:42
  24.4 1.5 %collective-permute-start.6 = (bf16[2,40,384]{2,1,0:T(8,128)(2,1)S(1)}, bf16[2,40,384]{2,1,0:T(8,128)(2,1)S(1)}, u32[]{:S(2)}, u32[]{:S(2)}) collective-permute-start(bf16[2,40,384]{2,1,0:T(8,128)(2,1)S(1)} %join.2.refs_0_), channel_id=1, source_target_pairs={{0,16},{4,20},{8,24},{12,28},{16,0},{20,4},{24,8},{28,12},{1,17},{... | collective-permute-start | bytes 184328 | tf_op jit(solution)/shard_map/ppermute | solution.py:42
  25.9 1.5 %collective-permute-start.5 = (bf16[2,40,384]{2,1,0:T(8,128)(2,1)S(1)}, bf16[2,40,384]{2,1,0:T(8,128)(2,1)S(1)}, u32[]{:S(2)}, u32[]{:S(2)}) collective-permute-start(bf16[2,40,384]{2,1,0:T(8,128)(2,1)S(1)} %join.2.refs_0_), channel_id=1, source_target_pairs={{0,8},{4,12},{8,0},{12,4},{16,24},{20,28},{24,16},{28,20},{1,9},{5... | collective-permute-start | bytes 184328 | tf_op jit(solution)/shard_map/ppermute | solution.py:42
  28.6 1.5 %collective-permute-start.7 = (bf16[2,40,384]{2,1,0:T(8,128)(2,1)S(1)}, bf16[2,40,384]{2,1,0:T(8,128)(2,1)S(1)}, u32[]{:S(2)}, u32[]{:S(2)}) collective-permute-start(bf16[2,40,384]{2,1,0:T(8,128)(2,1)S(1)} %collective-permute-done.6.refs_2_), channel_id=1, source_target_pairs={{0,8},{4,12},{8,0},{12,4},{16,24},{20,28},{24,16},{28,20},{1,9},{5... | collective-permute-start | bytes 184328 | tf_op jit(solution)/shard_map/ppermute | solution.py:42
  30.1 2.3 %hold.5 = (bf16[768,3072]{1,0:T(8,128)(2,1)S(1)}, f32[8,128]{1,0:T(8,128)S(1)}) custom-call(f32[8,128]{1,0:T(8,128)S(1)} %get-tuple-element.62.refs_0_, bf16[768,3072]{1,0:T(8,128)(2,1)} %refs_1_.5), custom_call_target="tpu_custom_call" | custom-call | bytes 4718592 | tf_op jit(solution)/shard_map/hold/pallas_call | solution.py:66
  34.2 2.5 %collective-permute-start.11 = (f32[88,384]{1,0:T(8,128)S(1)}, f32[88,384]{1,0:T(8,128)S(1)}, u32[]{:S(2)}, u32[]{:S(2)}) collective-permute-start(f32[88,384]{1,0:T(8,128)S(1)} %get-tuple-element.76), channel_id=1, source_target_pairs={{0,24},{4,28},{8,16},{12,20},{16,8},{20,12},{24,0},{28,4},{1,25},{... | collective-permute-start | bytes 405512 | tf_op jit(solution)/shard_map/ppermute | solution.py:42
  37.7 3.7 %hold.6 = (bf16[3072,1536]{1,0:T(8,128)(2,1)S(1)}, f32[8,128]{1,0:T(8,128)S(1)}) custom-call(f32[8,128]{1,0:T(8,128)S(1)} %get-tuple-element.73.refs_0_, bf16[3072,1536]{1,0:T(8,128)(2,1)} %refs_1_.6), custom_call_target="tpu_custom_call" | custom-call | bytes 9437184 | tf_op jit(solution)/shard_map/hold/pallas_call | solution.py:66
  44.7 1.9 %collective-permute-start.15 = (bf16[16,3072]{1,0:T(8,128)(2,1)S(1)}, bf16[16,3072]{1,0:T(8,128)(2,1)S(1)}, u32[]{:S(2)}, u32[]{:S(2)}) collective-permute-start(bf16[16,3072]{1,0:T(8,128)(2,1)S(1)} %get-tuple-element.88), channel_id=1, source_target_pairs={{0,3},{1,2},{2,1},{3,0},{4,7},{5,6},{6,5},{7,4},{8,11},{9,10},{10,... | collective-permute-start | bytes 294920 | tf_op jit(solution)/shard_map/ppermute | solution.py:42
  47.4 1.8 %collective-permute-start.17 = (bf16[16,3072]{1,0:T(8,128)(2,1)S(1)}, bf16[16,3072]{1,0:T(8,128)(2,1)S(1)}, u32[]{:S(2)}, u32[]{:S(2)}) collective-permute-start(bf16[16,3072]{1,0:T(8,128)(2,1)S(1)} %get-tuple-element.90), channel_id=1, source_target_pairs={{0,1},{1,0},{2,3},{3,2},{4,5},{5,4},{6,7},{7,6},{8,9},{9,8},{10,11... | collective-permute-start | bytes 294920 | tf_op jit(solution)/shard_map/ppermute | solution.py:42
  49.2 3.7 %hold.7 = (bf16[1536,3072]{1,0:T(8,128)(2,1)S(1)}, bf16[64,3072]{1,0:T(8,128)(2,1)S(1)}, f32[8,128]{1,0:T(8,128)S(1)}) custom-call(f32[8,128]{1,0:T(8,128)S(1)} %get-tuple-element.82.refs_0_, bf16[1536,3072]{1,0:T(8,128)(2,1)} %refs_1_.7, bf16[64,3072]{1,0:T(8,128)(2,1)} %refs_2_.1), custom_call_target="tpu_custom_call" | custom-call | bytes 9830400 | tf_op jit(solution)/shard_map/hold/pallas_call | solution.py:66
  52.9 3.6 %collective-permute-done.16.refs_2_ = bf16[16,3072]{1,0:T(8,128)(2,1)S(1)} collective-permute-done((bf16[16,3072]{1,0:T(8,128)(2,1)S(1)}, bf16[16,3072]{1,0:T(8,128)(2,1)S(1)}, u32[]{:S(2)}, u32[]{:S(2)}) %collective-permute-start.16) | collective-permute-done | bytes 98336 | tf_op jit(solution)/shard_map/ppermute | solution.py:42
  56.8 1.7 %collective-permute-start.20 = (bf16[16,3072]{1,0:T(8,128)(2,1)S(1)}, bf16[16,3072]{1,0:T(8,128)(2,1)S(1)}, u32[]{:S(2)}, u32[]{:S(2)}) collective-permute-start(bf16[16,3072]{1,0:T(8,128)(2,1)S(1)} %get-tuple-element.92.refs_0_), channel_id=1, source_target_pairs={{0,24},{4,28},{8,16},{12,20},{16,8},{20,12},{24,0},{28,4},{1,25},{... | collective-permute-start | bytes 294920 | tf_op jit(solution)/shard_map/ppermute | solution.py:42
  60.4 3.0 %collective-permute-done.20.refs_3_ = bf16[16,3072]{1,0:T(8,128)(2,1)S(1)} collective-permute-done((bf16[16,3072]{1,0:T(8,128)(2,1)S(1)}, bf16[16,3072]{1,0:T(8,128)(2,1)S(1)}, u32[]{:S(2)}, u32[]{:S(2)}) %collective-permute-start.20) | collective-permute-done | bytes 98336 | tf_op jit(solution)/shard_map/ppermute | solution.py:42
  64.6 1.7 %collective-permute-done.21.refs_1_ = bf16[4,16,3072]{2,1,0:T(8,128)(2,1)S(1)} collective-permute-done((bf16[4,16,3072]{2,1,0:T(8,128)(2,1)S(1)}, bf16[4,16,3072]{2,1,0:T(8,128)(2,1)S(1)}, u32[]{:S(2)}, u32[]{:S(2)}) %collective-permute-start.21) | collective-permute-done | bytes 393248 | tf_op jit(solution)/shard_map/ppermute | solution.py:42
  66.3 2.7 %mlp.1 = (f32[64,3072]{1,0:T(8,128)S(1)}, bf16[64,3072]{1,0:T(8,128)(2,1)S(1)}) custom-call(bf16[4,16,3072]{2,1,0:T(8,128)(2,1)S(1)} %join.3.refs_0_, bf16[4,16,3072]{2,1,0:T(8,128)(2,1)S(1)} %collective-permute-done.21.refs_1_, bf16[3072,1536]{1,0:T(8,128)(2,1)S(1)} %get-tuple-element.93.refs_2_, bf16[1536,3072]{1,0:T(8,128)(2,1)S(1)} %get-tuple-element.94.refs_3_), custom_call_target="tpu_custom_call" | custom-call | tf_op jit(solution)/shard_map/mlp/pallas_call | solution.py:500
  69.2 1.6 %collective-permute-done.22.refs_1_ = bf16[64,3072]{1,0:T(8,128)(2,1)S(1)} collective-permute-done((bf16[64,3072]{1,0:T(8,128)(2,1)S(1)}, bf16[64,3072]{1,0:T(8,128)(2,1)S(1)}, u32[]{:S(2)}, u32[]{:S(2)}) %collective-permute-start.22) | collective-permute-done | bytes 393248 | tf_op jit(solution)/shard_map/ppermute | solution.py:42
  70.9 1.5 %collective-permute-start.23 = (bf16[16,3072]{1,0:T(8,128)(2,1)S(1)}, bf16[16,3072]{1,0:T(8,128)(2,1)S(1)}, u32[]{:S(2)}, u32[]{:S(2)}) collective-permute-start(bf16[16,3072]{1,0:T(8,128)(2,1)S(1)} %get-tuple-element.98), channel_id=1, source_target_pairs={{0,24},{4,28},{8,16},{12,20},{16,8},{20,12},{24,0},{28,4},{1,25},{... | collective-permute-start | bytes 294920 | tf_op jit(solution)/shard_map/ppermute | solution.py:42
  74.4 3.0 %collective-permute-done.23.refs_1_ = bf16[16,3072]{1,0:T(8,128)(2,1)S(1)} collective-permute-done((bf16[16,3072]{1,0:T(8,128)(2,1)S(1)}, bf16[16,3072]{1,0:T(8,128)(2,1)S(1)}, u32[]{:S(2)}, u32[]{:S(2)}) %collective-permute-start.23) | collective-permute-done | bytes 98336 | tf_op jit(solution)/shard_map/ppermute | solution.py:42
  (48 shorter events, 21.5 us)
Async XLA Ops:
  2.0 8.1 %collective-permute-start = (bf16[4,64,768]{2,1,0:T(8,128)(2,1)S(1)}, bf16[4,64,768]{2,1,0:T(8,128)(2,1)S(1)}, u32[]{:S(2)}, u32[]{:S(2)}) collective-permute-start(bf16[4,64,768]{2,1,0:T(8,128)(2,1)S(1)} %get-tuple-element.55), channel_id=1, source_target_pairs={{0,4},{4,0},{8,12},{12,8},{16,20},{20,16},{24,28},{28,24},{1,5},{5... | collective-permute-start | bytes 1179656 | tf_op jit(solution)/shard_map/ppermute | solution.py:42
  2.6 9.4 %collective-permute-start.2 = (bf16[16,3200]{1,0:T(8,128)(2,1)S(1)}, bf16[16,3200]{1,0:T(8,128)(2,1)S(1)}, u32[]{:S(2)}, u32[]{:S(2)}) collective-permute-start(bf16[16,3200]{1,0:T(8,128)(2,1)S(1)} %get-tuple-element.56.refs_0_), channel_id=1, source_target_pairs={{0,2},{1,3},{2,0},{3,1},{4,6},{5,7},{6,4},{7,5},{8,10},{9,11},{10,... | collective-permute-start | bytes 307208 | tf_op jit(solution)/shard_map/ppermute | solution.py:42
  6.2 9.9 %collective-permute-start.1 = (bf16[16,3200]{1,0:T(8,128)(2,1)S(1)}, bf16[16,3200]{1,0:T(8,128)(2,1)S(1)}, u32[]{:S(2)}, u32[]{:S(2)}) collective-permute-start(bf16[16,3200]{1,0:T(8,128)(2,1)S(1)} %get-tuple-element.56.refs_0_), channel_id=1, source_target_pairs={{0,1},{1,0},{2,3},{3,2},{4,5},{5,4},{6,7},{7,6},{8,9},{9,8},{10,11... | collective-permute-start | bytes 307208 | tf_op jit(solution)/shard_map/ppermute | solution.py:42
  12.0 4.7 %collective-permute-start.3 = (bf16[16,3200]{1,0:T(8,128)(2,1)S(1)}, bf16[16,3200]{1,0:T(8,128)(2,1)S(1)}, u32[]{:S(2)}, u32[]{:S(2)}) collective-permute-start(bf16[16,3200]{1,0:T(8,128)(2,1)S(1)} %relay.1.refs_3_.refs_2_), channel_id=1, source_target_pairs={{0,1},{1,0},{2,3},{3,2},{4,5},{5,4},{6,7},{7,6},{8,9},{9,8},{10,11... | collective-permute-start | bytes 307208 | tf_op jit(solution)/shard_map/ppermute | solution.py:42
  12.7 19.7 %collective-permute-start.8 = (bf16[2,64,768]{2,1,0:T(8,128)(2,1)S(1)}, bf16[2,64,768]{2,1,0:T(8,128)(2,1)S(1)}, u32[]{:S(2)}, u32[]{:S(2)}) collective-permute-start(bf16[2,64,768]{2,1,0:T(8,128)(2,1)S(1)} %get-tuple-element.66), channel_id=1, source_target_pairs={{0,2},{1,3},{2,0},{3,1},{4,6},{5,7},{6,4},{7,5},{8,10},{9,11},{10,... | collective-permute-start | bytes 589832 | tf_op jit(solution)/shard_map/ppermute | solution.py:42
  16.8 16.7 %collective-permute-start.9 = (bf16[2,64,768]{2,1,0:T(8,128)(2,1)S(1)}, bf16[2,64,768]{2,1,0:T(8,128)(2,1)S(1)}, u32[]{:S(2)}, u32[]{:S(2)}) collective-permute-start(bf16[2,64,768]{2,1,0:T(8,128)(2,1)S(1)} %get-tuple-element.71), channel_id=1, source_target_pairs={{0,1},{1,0},{2,3},{3,2},{4,5},{5,4},{6,7},{7,6},{8,9},{9,8},{10,11... | collective-permute-start | bytes 589832 | tf_op jit(solution)/shard_map/ppermute | solution.py:42
  17.6 15.8 %collective-permute-start.10 = (bf16[2,64,768]{2,1,0:T(8,128)(2,1)S(1)}, bf16[2,64,768]{2,1,0:T(8,128)(2,1)S(1)}, u32[]{:S(2)}, u32[]{:S(2)}) collective-permute-start(bf16[2,64,768]{2,1,0:T(8,128)(2,1)S(1)} %get-tuple-element.72), channel_id=1, source_target_pairs={{0,3},{1,2},{2,1},{3,0},{4,7},{5,6},{6,5},{7,4},{8,11},{9,10},{10,... | collective-permute-start | bytes 589832 | tf_op jit(solution)/shard_map/ppermute | solution.py:42
  24.4 4.2 %collective-permute-start.6 = (bf16[2,40,384]{2,1,0:T(8,128)(2,1)S(1)}, bf16[2,40,384]{2,1,0:T(8,128)(2,1)S(1)}, u32[]{:S(2)}, u32[]{:S(2)}) collective-permute-start(bf16[2,40,384]{2,1,0:T(8,128)(2,1)S(1)} %join.2.refs_0_), channel_id=1, source_target_pairs={{0,16},{4,20},{8,24},{12,28},{16,0},{20,4},{24,8},{28,12},{1,17},{... | collective-permute-start | bytes 184328 | tf_op jit(solution)/shard_map/ppermute | solution.py:42
  25.9 6.5 %collective-permute-start.5 = (bf16[2,40,384]{2,1,0:T(8,128)(2,1)S(1)}, bf16[2,40,384]{2,1,0:T(8,128)(2,1)S(1)}, u32[]{:S(2)}, u32[]{:S(2)}) collective-permute-start(bf16[2,40,384]{2,1,0:T(8,128)(2,1)S(1)} %join.2.refs_0_), channel_id=1, source_target_pairs={{0,8},{4,12},{8,0},{12,4},{16,24},{20,28},{24,16},{28,20},{1,9},{5... | collective-permute-start | bytes 184328 | tf_op jit(solution)/shard_map/ppermute | solution.py:42
  28.6 4.2 %collective-permute-start.7 = (bf16[2,40,384]{2,1,0:T(8,128)(2,1)S(1)}, bf16[2,40,384]{2,1,0:T(8,128)(2,1)S(1)}, u32[]{:S(2)}, u32[]{:S(2)}) collective-permute-start(bf16[2,40,384]{2,1,0:T(8,128)(2,1)S(1)} %collective-permute-done.6.refs_2_), channel_id=1, source_target_pairs={{0,8},{4,12},{8,0},{12,4},{16,24},{20,28},{24,16},{28,20},{1,9},{5... | collective-permute-start | bytes 184328 | tf_op jit(solution)/shard_map/ppermute | solution.py:42
  34.2 7.4 %collective-permute-start.11 = (f32[88,384]{1,0:T(8,128)S(1)}, f32[88,384]{1,0:T(8,128)S(1)}, u32[]{:S(2)}, u32[]{:S(2)}) collective-permute-start(f32[88,384]{1,0:T(8,128)S(1)} %get-tuple-element.76), channel_id=1, source_target_pairs={{0,24},{4,28},{8,16},{12,20},{16,8},{20,12},{24,0},{28,4},{1,25},{... | collective-permute-start | bytes 405512 | tf_op jit(solution)/shard_map/ppermute | solution.py:42
  36.7 5.7 %collective-permute-start.12 = (f32[88,384]{1,0:T(8,128)S(1)}, f32[88,384]{1,0:T(8,128)S(1)}, u32[]{:S(2)}, u32[]{:S(2)}) collective-permute-start(f32[88,384]{1,0:T(8,128)S(1)} %get-tuple-element.77), channel_id=1, source_target_pairs={{0,16},{4,20},{8,24},{12,28},{16,0},{20,4},{24,8},{28,12},{1,17},{... | collective-permute-start | bytes 405512 | tf_op jit(solution)/shard_map/ppermute | solution.py:42
  37.2 5.2 %collective-permute-start.13 = (f32[88,384]{1,0:T(8,128)S(1)}, f32[88,384]{1,0:T(8,128)S(1)}, u32[]{:S(2)}, u32[]{:S(2)}) collective-permute-start(f32[88,384]{1,0:T(8,128)S(1)} %get-tuple-element.78), channel_id=1, source_target_pairs={{0,8},{4,12},{8,0},{12,4},{16,24},{20,28},{24,16},{28,20},{1,9},{5... | collective-permute-start | bytes 405512 | tf_op jit(solution)/shard_map/ppermute | solution.py:42
  44.7 8.2 %collective-permute-start.15 = (bf16[16,3072]{1,0:T(8,128)(2,1)S(1)}, bf16[16,3072]{1,0:T(8,128)(2,1)S(1)}, u32[]{:S(2)}, u32[]{:S(2)}) collective-permute-start(bf16[16,3072]{1,0:T(8,128)(2,1)S(1)} %get-tuple-element.88), channel_id=1, source_target_pairs={{0,3},{1,2},{2,1},{3,0},{4,7},{5,6},{6,5},{7,4},{8,11},{9,10},{10,... | collective-permute-start | bytes 294920 | tf_op jit(solution)/shard_map/ppermute | solution.py:42
  46.6 9.9 %collective-permute-start.16 = (bf16[16,3072]{1,0:T(8,128)(2,1)S(1)}, bf16[16,3072]{1,0:T(8,128)(2,1)S(1)}, u32[]{:S(2)}, u32[]{:S(2)}) collective-permute-start(bf16[16,3072]{1,0:T(8,128)(2,1)S(1)} %get-tuple-element.89), channel_id=1, source_target_pairs={{0,2},{1,3},{2,0},{3,1},{4,6},{5,7},{6,4},{7,5},{8,10},{9,11},{10,... | collective-permute-start | bytes 294920 | tf_op jit(solution)/shard_map/ppermute | solution.py:42
  47.4 9.2 %collective-permute-start.17 = (bf16[16,3072]{1,0:T(8,128)(2,1)S(1)}, bf16[16,3072]{1,0:T(8,128)(2,1)S(1)}, u32[]{:S(2)}, u32[]{:S(2)}) collective-permute-start(bf16[16,3072]{1,0:T(8,128)(2,1)S(1)} %get-tuple-element.90), channel_id=1, source_target_pairs={{0,1},{1,0},{2,3},{3,2},{4,5},{5,4},{6,7},{7,6},{8,9},{9,8},{10,11... | collective-permute-start | bytes 294920 | tf_op jit(solution)/shard_map/ppermute | solution.py:42
  56.8 6.6 %collective-permute-start.20 = (bf16[16,3072]{1,0:T(8,128)(2,1)S(1)}, bf16[16,3072]{1,0:T(8,128)(2,1)S(1)}, u32[]{:S(2)}, u32[]{:S(2)}) collective-permute-start(bf16[16,3072]{1,0:T(8,128)(2,1)S(1)} %get-tuple-element.92.refs_0_), channel_id=1, source_target_pairs={{0,24},{4,28},{8,16},{12,20},{16,8},{20,12},{24,0},{28,4},{1,25},{... | collective-permute-start | bytes 294920 | tf_op jit(solution)/shard_map/ppermute | solution.py:42
  58.6 5.4 %collective-permute-start.19 = (bf16[16,3072]{1,0:T(8,128)(2,1)S(1)}, bf16[16,3072]{1,0:T(8,128)(2,1)S(1)}, u32[]{:S(2)}, u32[]{:S(2)}) collective-permute-start(bf16[16,3072]{1,0:T(8,128)(2,1)S(1)} %get-tuple-element.92.refs_0_), channel_id=1, source_target_pairs={{0,16},{4,20},{8,24},{12,28},{16,0},{20,4},{24,8},{28,12},{1,17},{... | collective-permute-start | bytes 294920 | tf_op jit(solution)/shard_map/ppermute | solution.py:42
  59.9 4.6 %collective-permute-start.18 = (bf16[16,3072]{1,0:T(8,128)(2,1)S(1)}, bf16[16,3072]{1,0:T(8,128)(2,1)S(1)}, u32[]{:S(2)}, u32[]{:S(2)}) collective-permute-start(bf16[16,3072]{1,0:T(8,128)(2,1)S(1)} %get-tuple-element.92.refs_0_), channel_id=1, source_target_pairs={{0,8},{4,12},{8,0},{12,4},{16,24},{20,28},{24,16},{28,20},{1,9},{5... | collective-permute-start | bytes 294920 | tf_op jit(solution)/shard_map/ppermute | solution.py:42
  64.5 1.8 %collective-permute-start.21 = (bf16[4,16,3072]{2,1,0:T(8,128)(2,1)S(1)}, bf16[4,16,3072]{2,1,0:T(8,128)(2,1)S(1)}, u32[]{:S(2)}, u32[]{:S(2)}) collective-permute-start(bf16[4,16,3072]{2,1,0:T(8,128)(2,1)S(1)} %join.3.refs_0_), channel_id=1, source_target_pairs={{0,4},{4,0},{8,12},{12,8},{16,20},{20,16},{24,28},{28,24},{1,5},{5... | collective-permute-start | bytes 1179656 | tf_op jit(solution)/shard_map/ppermute | solution.py:42
  69.0 1.8 %collective-permute-start.22 = (bf16[64,3072]{1,0:T(8,128)(2,1)S(1)}, bf16[64,3072]{1,0:T(8,128)(2,1)S(1)}, u32[]{:S(2)}, u32[]{:S(2)}) collective-permute-start(bf16[64,3072]{1,0:T(8,128)(2,1)S(1)} %get-tuple-element.96), channel_id=1, source_target_pairs={{0,4},{4,0},{8,12},{12,8},{16,20},{20,16},{24,28},{28,24},{1,5},{5... | collective-permute-start | bytes 1179656 | tf_op jit(solution)/shard_map/ppermute | solution.py:42
  70.9 6.5 %collective-permute-start.23 = (bf16[16,3072]{1,0:T(8,128)(2,1)S(1)}, bf16[16,3072]{1,0:T(8,128)(2,1)S(1)}, u32[]{:S(2)}, u32[]{:S(2)}) collective-permute-start(bf16[16,3072]{1,0:T(8,128)(2,1)S(1)} %get-tuple-element.98), channel_id=1, source_target_pairs={{0,24},{4,28},{8,16},{12,20},{16,8},{20,12},{24,0},{28,4},{1,25},{... | collective-permute-start | bytes 294920 | tf_op jit(solution)/shard_map/ppermute | solution.py:42
  72.3 6.5 %collective-permute-start.24 = (bf16[16,3072]{1,0:T(8,128)(2,1)S(1)}, bf16[16,3072]{1,0:T(8,128)(2,1)S(1)}, u32[]{:S(2)}, u32[]{:S(2)}) collective-permute-start(bf16[16,3072]{1,0:T(8,128)(2,1)S(1)} %get-tuple-element.99), channel_id=1, source_target_pairs={{0,16},{4,20},{8,24},{12,28},{16,0},{20,4},{24,8},{28,12},{1,17},{... | collective-permute-start | bytes 294920 | tf_op jit(solution)/shard_map/ppermute | solution.py:42
  73.4 5.4 %collective-permute-start.25 = (bf16[16,3072]{1,0:T(8,128)(2,1)S(1)}, bf16[16,3072]{1,0:T(8,128)(2,1)S(1)}, u32[]{:S(2)}, u32[]{:S(2)}) collective-permute-start(bf16[16,3072]{1,0:T(8,128)(2,1)S(1)} %get-tuple-element.100), channel_id=1, source_target_pairs={{0,8},{4,12},{8,0},{12,4},{16,24},{20,28},{24,16},{28,20},{1,9},{5... | collective-permute-start | bytes 294920 | tf_op jit(solution)/shard_map/ppermute | solution.py:42
  (2 other events, 2.5 us)
